TPU v7x, 32 devices: a whole 2x2x4 slice. The times are simulated.
32 devices in a mesh: sect: 2 (over x), exp: 8 (over z, y), dp: 2 (over core).
Axes of the slice: x: 2, y: 2, z: 4, core: 2. Of those that a mesh axis runs over, the one named last changes fastest.
Arguments:
- decode_states: bfloat16 [256, 2048], P('exp'), may hold values from -15 to 15
- norm_gain: float32 [2048], replicated, may hold values from 0.25 to 1.75
- decode_routes: int32 [4, 256, 2], P(None, 'exp'), may hold values from 0 to 7, all different within a row; in each aligned block of 32 rows (0 to 31, 32 to 63, ..., all dimensions but the last counted through in order) at most 12 rows name the same one
- decode_gates: float32 [4, 256, 2], P(None, 'exp'), may hold values from 0.2 to 1
- up_weight: bfloat16 [2, 8, 1536, 2048], P('sect', 'exp', 'dp'), may hold values from -5 to 5
- down_weight: bfloat16 [2, 8, 1536, 2048], P('sect', 'exp', 'dp'), may hold values from -5 to 5
- traj_inputs: bfloat16 [2, 256, 2048], P('sect', 'exp'), may hold values from -6 to 6
- traj_cotangents: bfloat16 [2, 256, 2048], P('sect', 'exp'), may hold values from -6 to 6
- traj_lengths: int32 [8, 2, 4], P('exp'), may hold values from 1 to 16, 32 in all within a row
- packing: int32 [8, 8], P('exp'), may hold values from 0 to 7, each once within a row
- learner_routes: int32 [1024, 2], P('exp'), may hold values from 0 to 7, all different within a row; in each aligned block of 128 rows (0 to 127, 128 to 255, ...) at most 48 rows name the same one
- learner_gates: float32 [1024, 2], P('exp'), may hold values from 0.2 to 1
Outputs:
- final_states: bfloat16 [256, 2048], P('exp', 'sect')
- fresh_up: bfloat16 [2, 8, 1536, 2048], P('sect', 'exp', 'dp')
- fresh_down: bfloat16 [2, 8, 1536, 2048], P('sect', 'exp', 'dp')
Inputs may be any that keep to these rules, and one draw needn't show every extreme that they name: `decode_routes`: within each aligned block of 32 rows of one step (the rows of one index of exp), no expert is named more than 12 times, and that bound is met. `learner_routes`: within each aligned block of 128 rows (the slots of one learner shard), no expert is named more than 48 times, and that bound is met. `traj_lengths`: each row of 4 lengths sums to 32 and its largest is 16. `packing`: each row is a permutation of the 8 learner shards, so every holder sends exactly one trajectory to every shard.
All inputs are finite; a program needn't handle non-finite values.
Results may differ from a plain program's by a relative error of at most 0.02.
Values may be sent and summed in bfloat16 or wider, within the bound.
No kernel may reach another device: no remote copies, remote signals or barrier semaphores. Data moves between devices by JAX's collectives and lax.ppermute only.
A program may use at most 128 MiB of HBM per device.

v0:
```python
import jax
import jax.numpy as jnp
from jax import lax
from jax.sharding import PartitionSpec as P

step_size = 3.0
norm_eps = 1e-06


def partner(array, axis, apart):
    return lax.ppermute(array, axis, [(i, i ^ 1 << apart) for i in range(lax.axis_size(axis))])


def slot_table(routes, experts, capacity):
    flat_routes = routes.reshape(-1)
    member = (flat_routes[:, None] == jnp.arange(experts, dtype=jnp.int32)[None, :]).astype(
        jnp.int32
    )
    earlier = jnp.cumsum(member, axis=0) - member
    within = jnp.sum(earlier * member, axis=1)
    target = flat_routes * capacity + within
    one_hot = (target[:, None] == jnp.arange(experts * capacity, dtype=jnp.int32)[None, :]).astype(
        jnp.float32
    )
    return one_hot.reshape(routes.shape[0], routes.shape[1], experts * capacity)


def pack_trajectories(held_rows, lengths, row_pack, capacity):
    traj_count = lengths.shape[1]
    per_half = held_rows.shape[0] // 2
    column_ids = jnp.arange(row_pack.shape[0], dtype=jnp.int32)
    starts = jnp.cumsum(lengths, axis=1) - lengths
    matches = (row_pack[None, :] == column_ids[:, None]).astype(jnp.int32)
    chosen = jnp.sum(matches * column_ids[None, :], axis=1)
    half_index = chosen // traj_count
    length_of = jnp.take(lengths.reshape(-1), chosen)
    first_row = half_index * per_half + jnp.take(starts.reshape(-1), chosen)
    offsets = jnp.arange(capacity, dtype=jnp.int32)
    in_length = offsets[None, :] < length_of[:, None]
    row_index = jnp.where(in_length, first_row[:, None] + offsets[None, :], 0).reshape(-1)
    picked = jnp.take(held_rows, row_index, axis=0)
    return jnp.where(in_length.reshape(-1)[:, None, None], picked, jnp.zeros_like(picked))


def across(block):
    return partner(block, "sect", 0)


def to_experts(payload):
    arrived = lax.all_to_all(payload, "exp", split_axis=0, concat_axis=0, tiled=True)
    return arrived


def sum_and_return(partial_out):
    summed = lax.psum(partial_out.astype(jnp.bfloat16), "dp")
    returned = lax.all_to_all(summed, "exp", split_axis=0, concat_axis=0, tiled=True)
    return returned


def expert_forward(arrived, up_slice, down_slice, hidden_total):
    inputs = arrived[:, 0, :]
    before_act = jnp.einsum(
        "sd,hd->sh", inputs, up_slice, preferred_element_type=jnp.float32
    ) * inputs.shape[1] ** (-0.5)
    activated = jax.nn.silu(before_act).astype(jnp.bfloat16)
    return jnp.einsum(
        "sh,hd->sd", activated, down_slice, preferred_element_type=jnp.float32
    ) * hidden_total ** (-0.5)


def learner_update(arrived, up_slice, down_slice, hidden_total):
    inputs = arrived[:, 0, :]
    scaled_grad = arrived[:, 1, :]
    model_scale = inputs.shape[1] ** (-0.5)
    hidden_scale = hidden_total ** (-0.5)
    before_act = (
        jnp.einsum("sd,hd->sh", inputs, up_slice, preferred_element_type=jnp.float32) * model_scale
    )
    sigmoid_val = jax.nn.sigmoid(before_act)
    activated = (before_act * sigmoid_val).astype(jnp.bfloat16)
    hidden_grad = (
        jnp.einsum("sd,hd->sh", scaled_grad, down_slice, preferred_element_type=jnp.float32)
        * hidden_scale
    )
    pre_grad = (hidden_grad * sigmoid_val * (1.0 + before_act * (1.0 - sigmoid_val))).astype(
        jnp.bfloat16
    )
    down_grad = (
        jnp.einsum("sh,sd->hd", activated, scaled_grad, preferred_element_type=jnp.float32)
        * hidden_scale
    )
    up_grad = (
        jnp.einsum("sh,sd->hd", pre_grad, inputs, preferred_element_type=jnp.float32) * model_scale
    )
    new_up = (up_slice.astype(jnp.float32) - step_size * up_grad).astype(jnp.bfloat16)
    new_down = (down_slice.astype(jnp.float32) - step_size * down_grad).astype(jnp.bfloat16)
    return jnp.stack([new_up, new_down])


def decode_step(
    states, norm_gain, routes, gate_values, up_slice, down_slice, is_rollout, hidden_total
):
    experts = lax.axis_size("exp")
    capacity = 3 * routes.shape[0] * routes.shape[1] // (2 * experts)
    normed = (
        states * lax.rsqrt(jnp.mean(states * states, axis=1, keepdims=True) + norm_eps) * norm_gain
    )
    normed = normed.astype(jnp.bfloat16)
    one_hot = slot_table(routes, experts, capacity)
    outgoing = jnp.einsum(
        "rks,rd->sd", one_hot.astype(jnp.bfloat16), normed, preferred_element_type=jnp.float32
    )
    arrived = to_experts(outgoing.astype(jnp.bfloat16)[:, None, :])
    partial_out = lax.cond(
        is_rollout,
        lambda: expert_forward(arrived, up_slice, down_slice, hidden_total),
        lambda: jnp.zeros((arrived.shape[0], arrived.shape[2]), jnp.float32),
    )
    returned = sum_and_return(partial_out)
    weighted = one_hot * gate_values[:, :, None]
    mixed = jnp.einsum(
        "rks,sd->rd", weighted, returned.astype(jnp.float32), precision=lax.Precision.HIGHEST
    )
    return states + mixed


def on_device(
    decode_states,
    norm_gain,
    decode_routes,
    decode_gates,
    up_weight,
    down_weight,
    traj_inputs,
    traj_cotangents,
    traj_lengths,
    packing,
    learner_routes,
    learner_gates,
):
    experts = lax.axis_size("exp")
    is_learner = lax.axis_index("sect") == 1
    is_rollout = jnp.logical_not(is_learner)
    up_here = up_weight[0, 0]
    down_here = down_weight[0, 0]
    hidden_total = up_here.shape[0] * lax.axis_size("dp")
    held_pair = jnp.stack([traj_inputs[0], traj_cotangents[0]], axis=1)
    crossed = across(held_pair)
    held_rows = jnp.concatenate([crossed, held_pair], axis=0)

    def run_steps(states, first_step, last_step, up_mat, down_mat):
        for step_index in range(first_step, last_step):
            states = decode_step(
                states,
                norm_gain,
                decode_routes[step_index],
                decode_gates[step_index],
                up_mat,
                down_mat,
                is_rollout,
                hidden_total,
            )
        return states

    total_steps = decode_routes.shape[0]
    half_steps = total_steps // 2
    states = decode_states.astype(jnp.float32)
    capacity_t = learner_routes.shape[0] // experts
    outgoing = pack_trajectories(held_rows, traj_lengths[0], packing[0], capacity_t)
    packed = lax.all_to_all(outgoing, "exp", split_axis=0, concat_axis=0, tiled=True)
    capacity_l = 3 * learner_routes.shape[0] * learner_routes.shape[1] // (2 * experts)
    one_hot = slot_table(learner_routes, experts, capacity_l).astype(jnp.bfloat16)
    token_part = jnp.einsum(
        "rks,rd->sd", one_hot, packed[:, 0, :], preferred_element_type=jnp.float32
    )
    scaled_rows = (learner_gates[:, :, None] * packed[:, 1, None, :].astype(jnp.float32)).astype(
        jnp.bfloat16
    )
    grad_part = jnp.einsum("rks,rkd->sd", one_hot, scaled_rows, preferred_element_type=jnp.float32)
    payload = jnp.stack([token_part, grad_part], axis=1).astype(jnp.bfloat16)
    arrived = to_experts(payload)
    fresh_pair = lax.cond(
        is_learner,
        lambda: learner_update(arrived, up_here, down_here, hidden_total),
        lambda: jnp.zeros((2,) + up_here.shape, jnp.bfloat16),
    )
    returned = across(fresh_pair)
    fresh_here = jnp.where(is_learner, fresh_pair, returned)
    states = run_steps(states, 0, half_steps, up_here, down_here)
    states = run_steps(states, half_steps, total_steps, fresh_here[0], fresh_here[1])
    half_width = states.shape[1] // 2
    own_half = states[:, :half_width].astype(jnp.bfloat16)
    other_half = states[:, half_width:].astype(jnp.bfloat16)
    delivered = across(other_half)
    final_states = jnp.where(is_learner, delivered, own_half)
    return (final_states, fresh_here[0][None, None], fresh_here[1][None, None])


def solution(mesh):
    in_specs = (
        P("exp", None),
        P(),
        P(None, "exp", None),
        P(None, "exp", None),
        P("sect", "exp", "dp", None),
        P("sect", "exp", "dp", None),
        P("sect", "exp", None),
        P("sect", "exp", None),
        P("exp", None, None),
        P("exp", None),
        P("exp", None),
        P("exp", None),
    )
    out_specs = (P("exp", "sect"), P("sect", "exp", "dp", None), P("sect", "exp", "dp", None))
    return jax.shard_map(
        on_device, mesh=mesh, in_specs=in_specs, out_specs=out_specs, check_vma=False
    )
```

profile of v0, /device:TPU:0, one launch (start us, length us, event | category | flops | bytes accessed | tf_op | source)
XLA Modules:
  0.0 453.6 jit_solution(13160580384131945978)
XLA Ops:
  7.2 1.1 copy.152
  8.3 1.1 copy.153
  10.0 3.0 collective-permute-start
  17.2 2.1 collective-permute-done
  20.1 2.7 gather_fusion
  22.8 2.5 broadcast_select_fusion.2
  25.3 6.3 %all-to-all-start.5 = ((bf16[128,2,2048]{2,1,0:T(2,128)(2,1)}), bf16[128,2,2048]{2,1,0:T(2,128)(2,1)S(1)}, u32[]{:S(2)}, u32[]{:S(2)}) async-start(bf16[128,2,2048]{2,1,0:T(2,128)(2,1)} %broadcast_select_fusion.2), calls=%async_computation.5 | async-start | bytes 2097152 | tf_op jit(solution)/shard_map/all_to_all | solution.py:170
  33.3 23.4 %all-to-all-done.5 = bf16[128,2,2048]{2,1,0:T(2,128)(2,1)S(1)} async-done(((bf16[128,2,2048]{2,1,0:T(2,128)(2,1)}), bf16[128,2,2048]{2,1,0:T(2,128)(2,1)S(1)}, u32[]{:S(2)}, u32[]{:S(2)}) %all-to-all-start.5) | async-done | bytes 1048608 | tf_op jit(solution)/shard_map/all_to_all | solution.py:170
  56.7 1.5 fusion.83
  60.1 4.9 %copy.154 = bf16[384,2,2048]{2,1,0:T(2,128)(2,1)} copy(bf16[384,2,2048]{2,0,1:T(8,128)(2,1)S(1)} %pad_maximum_fusion.1) | data formatting | bytes 6291456 | tf_op jit(solution)/shard_map/stack | solution.py:180
  65.0 4.7 %all-to-all-start.6 = ((bf16[384,2,2048]{2,1,0:T(2,128)(2,1)}), bf16[384,2,2048]{2,1,0:T(2,128)(2,1)}, u32[]{:S(2)}, u32[]{:S(2)}) async-start(bf16[384,2,2048]{2,1,0:T(2,128)(2,1)} %copy.154), calls=%async_computation.6 | async-start | bytes 6291456 | tf_op jit(solution)/shard_map/all_to_all | solution.py:50
  73.0 66.7 %all-to-all-done.6 = bf16[384,2,2048]{2,1,0:T(2,128)(2,1)} async-done(((bf16[384,2,2048]{2,1,0:T(2,128)(2,1)}), bf16[384,2,2048]{2,1,0:T(2,128)(2,1)}, u32[]{:S(2)}, u32[]{:S(2)}) %all-to-all-start.6) | async-done | bytes 3145760 | tf_op jit(solution)/shard_map/all_to_all | solution.py:50
  139.7 3.6 conditional.7
  139.7 3.4 broadcast.248
  143.3 20.6 %collective-permute-start.1 = (bf16[2,768,2048]{2,1,0:T(8,128)(2,1)}, bf16[2,768,2048]{2,1,0:T(8,128)(2,1)}, u32[]{:S(2)}, u32[]{:S(2)}) collective-permute-start(bf16[2,768,2048]{2,1,0:T(8,128)(2,1)} %get-tuple-element.162), channel_id=1, source_target_pairs={{0,16},{16,0},{1,17},{17,1},{2,18},{18,2},{3,19},{19,3},{4,20},{20... | collective-permute-start | bytes 18874376 | tf_op jit(solution)/shard_map/ppermute | solution.py:11
  165.7 1.2 fusion.53
  167.5 1.6 reduce.2
  169.1 2.1 reshape.297
  171.2 3.6 all-to-all-start
  174.9 11.6 %all-to-all-done = bf16[8,2,12288]{2,1,0:T(2,128)(2,1)S(1)} async-done(((bf16[8,2,12288]{2,1,0:T(2,128)(2,1)}), bf16[8,2,12288]{2,1,0:T(2,128)(2,1)S(1)}, u32[]{:S(2)}, u32[]{:S(2)}) %all-to-all-start) | async-done | bytes 393248 | tf_op jit(solution)/shard_map/all_to_all | solution.py:50
  186.4 1.1 reshape.298
  187.6 4.5 conditional.5
  187.6 4.2 convolution_multiply_fusion
  192.9 17.0 %all-reduce.5.cloned.1.call-done = bf16[8,12,2048]{2,1,0:T(8,128)(2,1)} async-done(((bf16[8,12,2048]{2,1,0:T(8,128)(2,1)}), bf16[8,12,2048]{2,1,0:T(8,128)(2,1)}) %all-reduce.5.cloned.1.call-update) | async-done | bytes 393232 | tf_op jit(solution)/shard_map/psum | solution.py:55
  210.0 5.8 %all-to-all-start.1 = ((bf16[8,12,2048]{2,1,0:T(8,128)(2,1)}), bf16[8,12,2048]{2,1,0:T(8,128)(2,1)}, u32[]{:S(2)}, u32[]{:S(2)}) async-start(bf16[8,12,2048]{2,1,0:T(8,128)(2,1)} %all-reduce.5.cloned.1.call-done), calls=%async_computation.1 | async-start | bytes 1048576 | tf_op jit(solution)/shard_map/all_to_all | solution.py:56
  215.7 1.4 convert_reduce_fusion.3
  217.1 13.7 %all-to-all-done.1 = bf16[8,12,2048]{2,1,0:T(8,128)(2,1)} async-done(((bf16[8,12,2048]{2,1,0:T(8,128)(2,1)}), bf16[8,12,2048]{2,1,0:T(8,128)(2,1)}, u32[]{:S(2)}, u32[]{:S(2)}) %all-to-all-start.1) | async-done | bytes 393248 | tf_op jit(solution)/shard_map/all_to_all | solution.py:56
  230.8 1.1 all_to_all.53
  231.9 1.3 multiply_reduce_fusion.2
  234.3 1.6 reduce.3
  235.9 2.1 reshape.299
  238.0 3.6 all-to-all-start.2
  241.7 11.8 %all-to-all-done.2 = bf16[8,2,12288]{2,1,0:T(2,128)(2,1)S(1)} async-done(((bf16[8,2,12288]{2,1,0:T(2,128)(2,1)}), bf16[8,2,12288]{2,1,0:T(2,128)(2,1)S(1)}, u32[]{:S(2)}, u32[]{:S(2)}) %all-to-all-start.2) | async-done | bytes 393248 | tf_op jit(solution)/shard_map/all_to_all | solution.py:50
  253.5 1.1 reshape.300
  254.6 4.2 conditional.6
  254.6 4.2 convolution_multiply_fusion.2
  259.8 17.0 %all-reduce.7.cloned.1.call-done = bf16[8,12,2048]{2,1,0:T(8,128)(2,1)} async-done(((bf16[8,12,2048]{2,1,0:T(8,128)(2,1)}), bf16[8,12,2048]{2,1,0:T(8,128)(2,1)}) %all-reduce.7.cloned.1.call-update) | async-done | bytes 393232 | tf_op jit(solution)/shard_map/psum | solution.py:55
  276.8 5.8 %all-to-all-start.3 = ((bf16[8,12,2048]{2,1,0:T(8,128)(2,1)}), bf16[8,12,2048]{2,1,0:T(8,128)(2,1)S(1)}, u32[]{:S(2)}, u32[]{:S(2)}) async-start(bf16[8,12,2048]{2,1,0:T(8,128)(2,1)} %all-reduce.7.cloned.1.call-done), calls=%async_computation.3 | async-start | bytes 1048576 | tf_op jit(solution)/shard_map/all_to_all | solution.py:56
  282.7 14.8 %all-to-all-done.3 = bf16[8,12,2048]{2,1,0:T(8,128)(2,1)S(1)} async-done(((bf16[8,12,2048]{2,1,0:T(8,128)(2,1)}), bf16[8,12,2048]{2,1,0:T(8,128)(2,1)S(1)}, u32[]{:S(2)}, u32[]{:S(2)}) %all-to-all-start.3) | async-done | bytes 393248 | tf_op jit(solution)/shard_map/all_to_all | solution.py:56
  299.2 1.1 reshape.301
  300.4 3.6 all-to-all-start.4
  304.1 11.8 %all-to-all-done.4 = bf16[8,2,12288]{2,1,0:T(2,128)(2,1)S(1)} async-done(((bf16[8,2,12288]{2,1,0:T(2,128)(2,1)}), bf16[8,2,12288]{2,1,0:T(2,128)(2,1)S(1)}, u32[]{:S(2)}, u32[]{:S(2)}) %all-to-all-start.4) | async-done | bytes 393248 | tf_op jit(solution)/shard_map/all_to_all | solution.py:50
  315.9 1.1 reshape.302
  317.0 6.1 %broadcast_select_fusion = bf16[2,768,2048]{2,1,0:T(8,128)(2,1)} fusion(bf16[2,768,2048]{2,1,0:T(8,128)(2,1)} %get-tuple-element.162, bf16[2,768,2048]{2,1,0:T(8,128)(2,1)} %collective-permute-done.1, pred[]{:T(512)S(6)} %eq.173), kind=kLoop, calls=%fused_computation.59 | loop fusion | flops 3145728 | bytes 18874368 | tf_op jit(solution)/shard_map/jit(_where)/select_n | solution.py:188
  323.1 5.9 %slice_bitcast_fusion.10 = (bf16[1,1,768,2048]{3,2,1,0:T(8,128)(2,1)}, bf16[1,1,768,2048]{3,2,1,0:T(8,128)(2,1)}, bf16[768,2048]{1,0:T(8,128)(2,1)S(1)}, bf16[768,2048]{1,0:T(8,128)(2,1)}) fusion(bf16[2,768,2048]{2,1,0:T(8,128)(2,1)} %broadcast_select_fusion), kind=kLoop, calls=%fused_computation.63 | loop fusion | bytes 18874368 | tf_op jit(solution)/shard_map/broadcast_in_dim;squeeze | solution.py:196
  329.0 5.0 %conditional.8 = (bf16[96,2048]{1,0:T(8,128)(2,1)}) conditional(s32[]{:T(128)} %convert_element_type.161, () %tuple.43, (bf16[96,1,2048]{2,1,0:T(2,128)(2,1)}, bf16[768,2048]{1,0:T(8,128)(2,1)}, bf16[768,2048]{1,0:T(8,128)(2,1)S(1)}) %tuple.46), branch_computations={%region_29.31_spmd, %region_30.32_spmd} | conditional | flops 604815360 | bytes 7077896 | solution.py:114
  329.1 5.0 %convolution_multiply_fusion.6 = bf16[96,2048]{1,0:T(8,128)(2,1)} fusion(bf16[768,2048]{1,0:T(8,128)(2,1)S(1)} %get-tuple-element.57, bf16[768,2048]{1,0:T(8,128)(2,1)} %get-tuple-element.56, bf16[96,1,2048]{2,1,0:T(2,128)(2,1)} %get-tuple-element.118), kind=kOutput, calls=%fused_computation.41 | convolution fusion | flops 604815360 | bytes 7077888 | tf_op jit(solution)/shard_map/cond/branch_1_fun/sh,hd->sd/dot_general | solution.py:66
  334.0 1.9 all_to_all.61
  335.9 17.0 %all-reduce.9.cloned.1.call-done = bf16[8,12,2048]{2,1,0:T(8,128)(2,1)} async-done(((bf16[8,12,2048]{2,1,0:T(8,128)(2,1)}), bf16[8,12,2048]{2,1,0:T(8,128)(2,1)}) %all-reduce.9.cloned.1.call-update) | async-done | bytes 393232 | tf_op jit(solution)/shard_map/psum | solution.py:55
  352.9 5.8 %all-to-all-start.7 = ((bf16[8,12,2048]{2,1,0:T(8,128)(2,1)}), bf16[8,12,2048]{2,1,0:T(8,128)(2,1)}, u32[]{:S(2)}, u32[]{:S(2)}) async-start(bf16[8,12,2048]{2,1,0:T(8,128)(2,1)} %all-reduce.9.cloned.1.call-done), calls=%async_computation.7 | async-start | bytes 1048576 | tf_op jit(solution)/shard_map/all_to_all | solution.py:56
  359.4 14.3 %all-to-all-done.7 = bf16[8,12,2048]{2,1,0:T(8,128)(2,1)} async-done(((bf16[8,12,2048]{2,1,0:T(8,128)(2,1)}), bf16[8,12,2048]{2,1,0:T(8,128)(2,1)}, u32[]{:S(2)}, u32[]{:S(2)}) %all-to-all-start.7) | async-done | bytes 393248 | tf_op jit(solution)/shard_map/all_to_all | solution.py:56
  373.8 1.9 all_to_all.63
  375.6 1.4 multiply_reduce_fusion
  378.1 1.6 reduce.5
  379.6 2.1 reshape.303
  381.8 3.6 all-to-all-start.8
  385.5 11.8 %all-to-all-done.8 = bf16[8,2,12288]{2,1,0:T(2,128)(2,1)S(1)} async-done(((bf16[8,2,12288]{2,1,0:T(2,128)(2,1)}), bf16[8,2,12288]{2,1,0:T(2,128)(2,1)S(1)}, u32[]{:S(2)}, u32[]{:S(2)}) %all-to-all-start.8) | async-done | bytes 393248 | tf_op jit(solution)/shard_map/all_to_all | solution.py:50
  397.3 1.1 reshape.304
  398.4 4.2 conditional.9
  398.4 4.2 convolution_multiply_fusion.8
  403.6 17.0 %all-reduce.11.cloned.1.call-done = bf16[8,12,2048]{2,1,0:T(8,128)(2,1)} async-done(((bf16[8,12,2048]{2,1,0:T(8,128)(2,1)}), bf16[8,12,2048]{2,1,0:T(8,128)(2,1)}) %all-reduce.11.cloned.1.call-update) | async-done | bytes 393232 | tf_op jit(solution)/shard_map/psum | solution.py:55
  420.6 20.7 %all_to_all.78 = bf16[8,12,2048]{2,1,0:T(8,128)(2,1)S(1)} all-to-all(bf16[8,12,2048]{2,1,0:T(8,128)(2,1)} %all-reduce.11.cloned.1.call-done), channel_id=1, replica_groups=mesh['sect'=2,'exp'=8,'dp'=2] {'exp'}, dimensions={0} | all-to-all | bytes 786432 | tf_op jit(solution)/shard_map/all_to_all | solution.py:56
  441.7 1.5 collective-permute-start.2
  443.2 2.8 collective-permute-done.2
  (133 shorter events, 23.2 us)
Async XLA Ops:
  10.0 9.3 %collective-permute-start = (bf16[32,2,2048]{2,1,0:T(2,128)(2,1)S(1)}, bf16[32,2,2048]{2,1,0:T(2,128)(2,1)S(1)}, u32[]{:S(2)}, u32[]{:S(2)}) collective-permute-start(bf16[32,2,2048]{2,1,0:T(2,128)(2,1)S(1)} %pad_maximum_fusion.2), channel_id=1, source_target_pairs={{0,16},{16,0},{1,17},{17,1},{2,18},{18,2},{3,19},{19,3},{4,20},{20... | collective-permute-start | bytes 786440 | tf_op jit(solution)/shard_map/ppermute | solution.py:11
  20.1 11.5 %copy-start.12 = (s32[128,2]{0,1:T(2,128)S(1)}, s32[128,2]{0,1:T(2,128)}, u32[]{:S(2)}) copy-start(s32[128,2]{0,1:T(2,128)} %param.34) | copy-start | bytes 3076
  25.3 31.4 %all-to-all-start.5 = ((bf16[128,2,2048]{2,1,0:T(2,128)(2,1)}), bf16[128,2,2048]{2,1,0:T(2,128)(2,1)S(1)}, u32[]{:S(2)}, u32[]{:S(2)}) async-start(bf16[128,2,2048]{2,1,0:T(2,128)(2,1)} %broadcast_select_fusion.2), calls=%async_computation.5 | async-start | bytes 2097152 | tf_op jit(solution)/shard_map/all_to_all | solution.py:170
  33.3 25.2 %copy-start.18 = (f32[128,2]{0,1:T(2,128)S(1)}, f32[128,2]{0,1:T(2,128)}, u32[]{:S(2)}) copy-start(f32[128,2]{0,1:T(2,128)} %param.35) | copy-start | bytes 3076
  65.0 4.7 %copy-start.11 = (s32[4,32,2]{1,2,0:T(2,128)S(1)}, s32[4,32,2]{1,2,0:T(2,128)}, u32[]{:S(2)}) copy-start(s32[4,32,2]{1,2,0:T(2,128)} %param.26) | copy-start | bytes 3076
  65.0 7.4 %copy-start.13 = (f32[4,32,2]{1,2,0:T(2,128)S(1)}, f32[4,32,2]{1,2,0:T(2,128)}, u32[]{:S(2)}) copy-start(f32[4,32,2]{1,2,0:T(2,128)} %param.27) | copy-start | bytes 3076
  65.0 74.7 %copy-start = (bf16[1,1,768,2048]{3,2,1,0:T(8,128)(2,1)S(1)}, bf16[1,1,768,2048]{3,2,1,0:T(8,128)(2,1)}, u32[]{:S(2)}) copy-start(bf16[1,1,768,2048]{3,2,1,0:T(8,128)(2,1)} %param.28) | copy-start | bytes 9437188
  65.0 74.6 %all-to-all-start.6 = ((bf16[384,2,2048]{2,1,0:T(2,128)(2,1)}), bf16[384,2,2048]{2,1,0:T(2,128)(2,1)}, u32[]{:S(2)}, u32[]{:S(2)}) async-start(bf16[384,2,2048]{2,1,0:T(2,128)(2,1)} %copy.154), calls=%async_computation.6 | async-start | bytes 6291456 | tf_op jit(solution)/shard_map/all_to_all | solution.py:50
  139.7 25.8 %copy-start.7 = (bf16[32,2048]{1,0:T(8,128)(2,1)S(1)}, bf16[32,2048]{1,0:T(8,128)(2,1)}, u32[]{:S(2)}) copy-start(bf16[32,2048]{1,0:T(8,128)(2,1)} %param.24) | copy-start | bytes 393220
  139.7 26.0 %copy-start.8 = (f32[2048]{0:T(1024)S(1)}, f32[2048]{0:T(1024)}, u32[]{:S(2)}) copy-start(f32[2048]{0:T(1024)} %param.25) | copy-start | bytes 24580
  143.3 173.7 %collective-permute-start.1 = (bf16[2,768,2048]{2,1,0:T(8,128)(2,1)}, bf16[2,768,2048]{2,1,0:T(8,128)(2,1)}, u32[]{:S(2)}, u32[]{:S(2)}) collective-permute-start(bf16[2,768,2048]{2,1,0:T(8,128)(2,1)} %get-tuple-element.162), channel_id=1, source_target_pairs={{0,16},{16,0},{1,17},{17,1},{2,18},{18,2},{3,19},{19,3},{4,20},{20... | collective-permute-start | bytes 18874376 | tf_op jit(solution)/shard_map/ppermute | solution.py:11
  171.2 15.2 %all-to-all-start = ((bf16[8,2,12288]{2,1,0:T(2,128)(2,1)}), bf16[8,2,12288]{2,1,0:T(2,128)(2,1)S(1)}, u32[]{:S(2)}, u32[]{:S(2)}) async-start(bf16[8,2,12288]{2,1,0:T(2,128)(2,1)} %reshape.297), calls=%async_computation | async-start | bytes 786432 | tf_op jit(solution)/shard_map/all_to_all | solution.py:50
  174.8 35.1 %all-reduce.5.cloned.1.call-start = ((), (), s32[]{:S(2)}) async-start(), calls=%async_computation.10 | async-start | bytes 1048576 | tf_op jit(solution)/shard_map/psum | solution.py:55
  210.0 20.8 %all-to-all-start.1 = ((bf16[8,12,2048]{2,1,0:T(8,128)(2,1)}), bf16[8,12,2048]{2,1,0:T(8,128)(2,1)}, u32[]{:S(2)}, u32[]{:S(2)}) async-start(bf16[8,12,2048]{2,1,0:T(8,128)(2,1)} %all-reduce.5.cloned.1.call-done), calls=%async_computation.1 | async-start | bytes 1048576 | tf_op jit(solution)/shard_map/all_to_all | solution.py:56
  233.3 0.7 copy-start.5
  238.0 15.5 %all-to-all-start.2 = ((bf16[8,2,12288]{2,1,0:T(2,128)(2,1)}), bf16[8,2,12288]{2,1,0:T(2,128)(2,1)S(1)}, u32[]{:S(2)}, u32[]{:S(2)}) async-start(bf16[8,2,12288]{2,1,0:T(2,128)(2,1)} %reshape.299), calls=%async_computation.2 | async-start | bytes 786432 | tf_op jit(solution)/shard_map/all_to_all | solution.py:50
  241.7 35.2 %all-reduce.7.cloned.1.call-start = ((), (), s32[]{:S(2)}) async-start(), calls=%async_computation.11 | async-start | bytes 1048576 | tf_op jit(solution)/shard_map/psum | solution.py:55
  254.6 28.0 %copy-start.15 = (s32[32,2]{0,1:T(2,128)S(1)}, s32[32,2]{0,1:T(2,128)}, u32[]{:S(2)}) copy-start(s32[32,2]{0,1:T(2,128)} %get-tuple-element.145) | copy-start | bytes 772
  254.6 28.0 %copy-start.17 = (f32[32,2]{0,1:T(2,128)S(1)}, f32[32,2]{0,1:T(2,128)}, u32[]{:S(2)}) copy-start(f32[32,2]{0,1:T(2,128)} %get-tuple-element.141) | copy-start | bytes 772
  258.9 38.8 %copy-start.6 = (f32[32,2048]{1,0:T(8,128)S(1)}, f32[32,2048]{1,0:T(8,128)}, u32[]{:S(2)}) copy-start(f32[32,2048]{1,0:T(8,128)} %copy-done.5) | copy-start | bytes 786436
  258.9 38.8 %copy-start.9 = (f32[32,96]{1,0:T(8,128)S(1)}, f32[32,96]{1,0:T(8,128)}, u32[]{:S(2)}) copy-start(f32[32,96]{1,0:T(8,128)} %get-tuple-element.129) | copy-start | bytes 36868
  276.8 20.7 %all-to-all-start.3 = ((bf16[8,12,2048]{2,1,0:T(8,128)(2,1)}), bf16[8,12,2048]{2,1,0:T(8,128)(2,1)S(1)}, u32[]{:S(2)}, u32[]{:S(2)}) async-start(bf16[8,12,2048]{2,1,0:T(8,128)(2,1)} %all-reduce.7.cloned.1.call-done), calls=%async_computation.3 | async-start | bytes 1048576 | tf_op jit(solution)/shard_map/all_to_all | solution.py:56
  300.4 15.5 %all-to-all-start.4 = ((bf16[8,2,12288]{2,1,0:T(2,128)(2,1)}), bf16[8,2,12288]{2,1,0:T(2,128)(2,1)S(1)}, u32[]{:S(2)}, u32[]{:S(2)}) async-start(bf16[8,2,12288]{2,1,0:T(2,128)(2,1)} %reshape.301), calls=%async_computation.4 | async-start | bytes 786432 | tf_op jit(solution)/shard_map/all_to_all | solution.py:50
  304.0 48.9 %all-reduce.9.cloned.1.call-start = ((), (), s32[]{:S(2)}) async-start(), calls=%async_computation.12 | async-start | bytes 1048576 | tf_op jit(solution)/shard_map/psum | solution.py:55
  329.0 29.7 %copy-start.14 = (s32[32,2]{0,1:T(2,128)S(1)}, s32[32,2]{0,1:T(2,128)}, u32[]{:S(2)}) copy-start(s32[32,2]{0,1:T(2,128)} %get-tuple-element.142) | copy-start | bytes 772
  329.0 29.7 %copy-start.16 = (f32[32,2]{0,1:T(2,128)S(1)}, f32[32,2]{0,1:T(2,128)}, u32[]{:S(2)}) copy-start(f32[32,2]{0,1:T(2,128)} %get-tuple-element.138) | copy-start | bytes 772
  352.9 20.8 %all-to-all-start.7 = ((bf16[8,12,2048]{2,1,0:T(8,128)(2,1)}), bf16[8,12,2048]{2,1,0:T(8,128)(2,1)}, u32[]{:S(2)}, u32[]{:S(2)}) async-start(bf16[8,12,2048]{2,1,0:T(8,128)(2,1)} %all-reduce.9.cloned.1.call-done), calls=%async_computation.7 | async-start | bytes 1048576 | tf_op jit(solution)/shard_map/all_to_all | solution.py:56
  377.0 0.7 copy-start.3
  381.8 15.5 %all-to-all-start.8 = ((bf16[8,2,12288]{2,1,0:T(2,128)(2,1)}), bf16[8,2,12288]{2,1,0:T(2,128)(2,1)S(1)}, u32[]{:S(2)}, u32[]{:S(2)}) async-start(bf16[8,2,12288]{2,1,0:T(2,128)(2,1)} %reshape.303), calls=%async_computation.8 | async-start | bytes 786432 | tf_op jit(solution)/shard_map/all_to_all | solution.py:50
  385.4 35.2 %all-reduce.11.cloned.1.call-start = ((), (), s32[]{:S(2)}) async-start(), calls=%async_computation.13 | async-start | bytes 1048576 | tf_op jit(solution)/shard_map/psum | solution.py:55
  402.6 38.8 %copy-start.4 = (f32[32,2048]{1,0:T(8,128)S(1)}, f32[32,2048]{1,0:T(8,128)}, u32[]{:S(2)}) copy-start(f32[32,2048]{1,0:T(8,128)} %copy-done.3) | copy-start | bytes 786436
  402.6 38.8 %copy-start.10 = (f32[32,96]{1,0:T(8,128)S(1)}, f32[32,96]{1,0:T(8,128)}, u32[]{:S(2)}) copy-start(f32[32,96]{1,0:T(8,128)} %get-tuple-element.125) | copy-start | bytes 36868
  441.7 4.3 collective-permute-start.2
Sparse Core Ops, SparseCore 0:
  193.1 16.8 all-reduce.4
  259.9 16.8 all-reduce.6
  336.0 16.8 all-reduce.8
  403.7 16.8 all-reduce.10
where the time goes:
time: 460 us; the launch traced here: 454 us
  waiting for transfers between devices  253 us (55%)
  starting transfers between devices  68.1 us (15%)
  local copies, waits for them, and re-layouts  46.5 us (10%)
  other arithmetic  25.7 us (6%)
  matrix products  24.5 us (5%)
  blocking collectives  20.7 us (4%)
  between operations  14.7 us (3%)
    all_to_all x5, waiting for transfers between devices, to_experts(): lax.all_to_all(payload, 'exp', split_axis=0, concat_axis=0, tiled=True)  114 us
    psum x4, waiting for transfers between devices, sum_and_return(): summed = lax.psum(partial_out.astype(jnp.bfloat16), 'dp')  68 us
    all_to_all x3, waiting for transfers between devices, sum_and_return(): lax.all_to_all(summed, 'exp', split_axis=0, concat_axis=0, tiled=True)  42.8 us
    ppermute x3, starting transfers between devices, partner(): lax.ppermute(array, axis, [(i, i ^ 1 << apart) for i in range(lax.axis_si...  25.1 us
    all_to_all x1, waiting for transfers between devices, on_device(): lax.all_to_all(outgoing, 'exp', split_axis=0, concat_axis=0, tiled=True)  23.4 us
    all_to_all x1, blocking collectives, sum_and_return(): lax.all_to_all(summed, 'exp', split_axis=0, concat_axis=0, tiled=True)  20.7 us
    all_to_all x5, starting transfers between devices, to_experts(): lax.all_to_all(payload, 'exp', split_axis=0, concat_axis=0, tiled=True)  19.2 us
    dot_general x4, matrix products, expert_forward(): jnp.einsum('sh,hd->sd', activated, down_slice, preferred_element_type=jnp...  17.6 us
  transfers between devices with their start and end apart: 16, of which 15 were waited for; matrix products, arithmetic and copies ran while one was open for 8% of the time, Pallas kernels for 0%

commit v1 on v0

v1 whole, which is shorter than its diff:
```python
import functools

import jax
import jax.numpy as jnp
import numpy as np
from jax import lax
from jax.experimental import pallas as pl
from jax.experimental.pallas import tpu as pltpu
from jax.sharding import PartitionSpec as P

step_size = 3.0
norm_eps = 1e-06
lanes = 256
f32, bf16, i32 = jnp.float32, jnp.bfloat16, jnp.int32
nt_dims = (((1,), (1,)), ((), ()))
tn_dims = (((0,), (0,)), ((), ()))
smem = pl.BlockSpec(memory_space=pltpu.SMEM)


def shifted(array, axis, by):
    size = lax.axis_size(axis)
    return lax.ppermute(array, axis, [(i, (i + by) % size) for i in range(size)])


def flipped(array, axis, bit):
    return lax.ppermute(array, axis, [(i, i ^ bit) for i in range(lax.axis_size(axis))])


def fits(megabytes):
    return pltpu.CompilerParams(vmem_limit_bytes=megabytes * 1024 * 1024)


def dot(a, b, dims=(((1,), (0,)), ((), ()))):
    return lax.dot_general(a, b, dims, preferred_element_type=f32)


def picked(shape, targets):
    rows = lax.broadcasted_iota(i32, shape, 0)
    return [rows == target for target in targets]


def prepare_kernel(experts, capacity, part_ref, routes_ref, rows_ref, targets_ref, states_ref, payload_ref):
    row_count = rows_ref.shape[0]
    stacked, width = states_ref.shape
    blocks = stacked // row_count
    before = lax.broadcasted_iota(i32, (stacked, stacked), 0)
    after = lax.broadcasted_iota(i32, (stacked, stacked), 1)
    row_of = lax.rem(after, row_count)
    first = before < row_count
    earlier = jnp.where(first & (before < row_of), 1.0, 0.0).astype(bf16)
    every = jnp.where(first, 1.0, 0.0).astype(bf16)
    block_of = lax.div(lax.broadcasted_iota(i32, (1, stacked), 1), row_count)
    expert_ids = lax.broadcasted_iota(i32, (experts, stacked), 0)
    for step in range(routes_ref.shape[0]):
        seen = jnp.zeros((experts, stacked), f32)
        for k in range(routes_ref.shape[1]):
            route = routes_ref[step, k : k + 1, :]
            member = jnp.where(expert_ids == route, 1.0, 0.0)
            ahead = dot(member.astype(bf16), earlier) + seen
            rank = jnp.sum(member * ahead, axis=0, keepdims=True).astype(i32)
            seen = seen + dot(member.astype(bf16), every)
            place = (route * blocks + block_of) * capacity + rank
            targets_ref[step, k : k + 1, :] = place
    start = part_ref[0] * (blocks * width)
    for block in range(blocks):
        column = pl.multiple_of(start + block * width, width)
        states_ref[block * row_count : (block + 1) * row_count, :] = rows_ref[:, pl.ds(column, width)].astype(f32)
    targets = [targets_ref[0, k : k + 1, :] for k in range(routes_ref.shape[1])]
    chosen = sum(jnp.where(hit, 1.0, 0.0) for hit in picked((payload_ref.shape[0], stacked), targets))
    payload_ref[...] = dot(chosen.astype(bf16), states_ref[...].astype(bf16)).astype(bf16)


def combine_kernel(last, targets_ref, gates_ref, next_ref, states_ref, returned_ref, new_ref, *payload_ref):
    routes = gates_ref.shape[0]
    shape = (returned_ref.shape[0], states_ref.shape[0])
    targets = [targets_ref[k : k + 1, :] for k in range(routes)]
    weights = sum(jnp.where(hit, gates_ref[k : k + 1, :], 0.0) for k, hit in enumerate(picked(shape, targets)))
    mixed = lax.dot_general(
        weights,
        returned_ref[...].astype(f32),
        tn_dims,
        precision=lax.Precision.HIGHEST,
        preferred_element_type=f32,
    )
    states = states_ref[...] + mixed
    new_ref[...] = states
    if not last:
        targets = [next_ref[k : k + 1, :] for k in range(routes)]
        chosen = sum(jnp.where(hit, 1.0, 0.0) for hit in picked(shape, targets))
        payload_ref[0][...] = dot(chosen.astype(bf16), states.astype(bf16)).astype(bf16)


def expert_kernel(parts, slots, features, hidden, part_ref, gain_ref, order_ref, *refs):
    arrived, (up_ref, down_ref) = refs[:parts], refs[parts : parts + 2]
    outs, (normed_ref, sums_ref, stack_ref) = refs[parts + 2 : 2 * parts + 2], refs[2 * parts + 2 :]
    width = arrived[0].shape[1]
    blocks = features // (parts * width)
    me = part_ref[0]

    @pl.when(pl.program_id(0) == 0)
    def _():
        square = jnp.zeros((slots, 1), f32)
        stacks = []
        for ref in arrived:
            stack = dot(order_ref[...], ref[...], tn_dims)
            stacks.append(stack)
            for block in range(blocks):
                rows = stack[block * slots : (block + 1) * slots]
                square = square + jnp.sum(rows * rows, axis=1, keepdims=True)
        scale = lax.rsqrt(square * (1.0 / features) + norm_eps)
        for j, stack in enumerate(stacks):
            start = lax.rem(me + parts - j, parts) * (blocks * width)
            for block in range(blocks):
                rows = stack[block * slots : (block + 1) * slots]
                columns = pl.ds(pl.multiple_of(start + block * width, width), width)
                normed_ref[:, columns] = (rows * scale * gain_ref[:, columns]).astype(bf16)
        sums_ref[...] = jnp.zeros_like(sums_ref)

    before_act = dot(normed_ref[...], up_ref[...], nt_dims) * features ** (-0.5)
    activated = (before_act / (1.0 + jnp.exp(-before_act))).astype(bf16)
    sums_ref[...] += dot(activated, down_ref[...])

    @pl.when(pl.program_id(0) == pl.num_programs(0) - 1)
    def _():
        for j, out_ref in enumerate(outs):
            start = lax.rem(me + j, parts) * (blocks * width)
            for block in range(blocks):
                columns = pl.ds(pl.multiple_of(start + block * width, width), width)
                stack_ref[block * slots : (block + 1) * slots, :] = (sums_ref[:, columns] * hidden ** (-0.5)).astype(bf16)
            out_ref[...] = dot(order_ref[...], stack_ref[...]).astype(bf16)


def update_kernel(parts, features, hidden, part_ref, weight_ref, *refs):
    held, (up_ref, down_ref, new_up_ref, new_down_ref) = refs[:parts], refs[parts:]
    count = held[0].shape[0] // 2
    width = held[0].shape[1]
    me = part_ref[0]
    columns = [pl.ds(pl.multiple_of(lax.rem(me + parts - j, parts) * width, width), width) for j in range(parts)]
    weight = weight_ref[...]
    before_act = sum(dot(up_ref[:, c], ref[:count], nt_dims) for c, ref in zip(columns, held)) * features ** (-0.5)
    sigmoid = 1.0 / (1.0 + jnp.exp(-before_act))
    hidden_grad = sum(dot(down_ref[:, c], ref[count:], nt_dims) for c, ref in zip(columns, held)) * hidden ** (-0.5)
    pre_grad = hidden_grad * weight * sigmoid * (1.0 + before_act * (1.0 - sigmoid))
    pre_grad = pre_grad.astype(bf16)
    activated = (before_act * sigmoid * weight).astype(bf16)
    for c, ref in zip(columns, held):
        up_grad = dot(pre_grad, ref[:count])
        new_up_ref[:, c] = (up_ref[:, c].astype(f32) - (step_size * features ** (-0.5)) * up_grad).astype(bf16)
        down_grad = dot(activated, ref[count:])
        new_down_ref[:, c] = (down_ref[:, c].astype(f32) - (step_size * hidden ** (-0.5)) * down_grad).astype(bf16)


def unset_kernel(*refs):
    pass


def unset(*like):
    return pl.pallas_call(
        unset_kernel,
        out_shape=[jax.ShapeDtypeStruct(a.shape, a.dtype) for a in like],
        out_specs=[pl.BlockSpec(memory_space=pl.ANY)] * len(like),
    )()


def on_device(
    decode_states,
    norm_gain,
    decode_routes,
    decode_gates,
    up_weight,
    down_weight,
    traj_inputs,
    traj_cotangents,
    traj_lengths,
    packing,
    learner_routes,
    learner_gates,
):
    experts, parts = lax.axis_size("exp"), lax.axis_size("dp")
    is_rollout = lax.axis_index("sect") == 0
    me = lax.axis_index("exp")
    part = lax.axis_index("dp")
    part_ref = part.reshape(1).astype(i32)
    up_here, down_here = up_weight[0, 0], down_weight[0, 0]
    hidden_here, features = up_here.shape
    hidden = hidden_here * parts
    steps, row_count, routes_each = decode_routes.shape
    share = features // parts
    blocks = share // lanes
    capacity = 3 * row_count * routes_each // (2 * experts)
    slots = experts * capacity
    stacked = blocks * row_count
    moved = blocks * slots
    tile = hidden_here // 3

    own_rows = lax.dynamic_slice_in_dim(jnp.concatenate([traj_inputs[0], traj_cotangents[0]]), part * share, share, 1)
    crossed_rows = flipped(own_rows, "sect", 1)
    up_there = lax.ppermute(up_here, "sect", [(1, 0)])

    routes = jnp.tile(jnp.swapaxes(decode_routes, 1, 2), (1, 1, blocks))
    gates = jnp.tile(jnp.swapaxes(decode_gates, 1, 2), (1, 1, blocks))
    targets, states, payload = pl.pallas_call(
        functools.partial(prepare_kernel, experts, capacity),
        out_shape=[
            jax.ShapeDtypeStruct(routes.shape, i32),
            jax.ShapeDtypeStruct((stacked, lanes), f32),
            jax.ShapeDtypeStruct((moved, lanes), bf16),
        ],
        in_specs=[smem, pl.BlockSpec(memory_space=pltpu.VMEM), pl.BlockSpec(memory_space=pltpu.VMEM)],
        compiler_params=fits(16),
    )(part_ref, routes, decode_states)
    gain = norm_gain.reshape(1, features)
    place = np.arange(moved)
    source = (place // capacity % blocks) * slots + place // (capacity * blocks) * capacity + place % capacity
    order = jnp.asarray((source[:, None] == place[None, :]).astype(np.float32), bf16)

    def whole(array):
        return pl.BlockSpec(array.shape, lambda i: (0,) * array.ndim)

    def expert_forward(arrived, up_mat, down_mat):
        tiles = pl.BlockSpec((tile, features), lambda i: (i, 0))
        out = jax.ShapeDtypeStruct((moved, lanes), bf16)
        return pl.pallas_call(
            functools.partial(expert_kernel, parts, slots, features, hidden),
            grid=(hidden_here // tile,),
            out_shape=[out] * parts,
            in_specs=[smem, whole(gain), whole(order)] + [whole(a) for a in arrived] + [tiles, tiles],
            out_specs=[whole(out)] * parts,
            scratch_shapes=[
                pltpu.VMEM((slots, features), bf16),
                pltpu.VMEM((slots, features), f32),
                pltpu.VMEM((moved, lanes), bf16),
            ],
            compiler_params=fits(24),
        )(part_ref, gain, order, *arrived, up_mat, down_mat)

    def decode_step(step, states, payload, up_mat, down_mat):
        last = step == steps - 1
        arrived = lax.all_to_all(payload, "exp", split_axis=0, concat_axis=0, tiled=True)
        arrived = [arrived] + [shifted(arrived, "dp", j) for j in range(1, parts)]
        partials = expert_forward(arrived, up_mat, down_mat)
        received = [shifted(partials[j], "dp", j) for j in range(1, parts)]
        summed = sum((r.astype(f32) for r in received), partials[0].astype(f32)).astype(bf16)
        returned = lax.all_to_all(summed, "exp", split_axis=0, concat_axis=0, tiled=True)
        outs = [jax.ShapeDtypeStruct((stacked, lanes), f32)]
        if not last:
            outs = outs + [jax.ShapeDtypeStruct((moved, lanes), bf16)]
        results = pl.pallas_call(
            functools.partial(combine_kernel, last),
            out_shape=outs,
            compiler_params=fits(16),
        )(targets[step], gates[step], targets[min(step + 1, steps - 1)], states, returned)
        return results[0], (payload if last else results[1])

    def learner_rows():
        first = jnp.where(is_rollout, own_rows, crossed_rows)
        second = jnp.where(is_rollout, crossed_rows, own_rows)
        half = first.shape[0] // 2
        rows = jnp.stack([first[:half], second[:half], first[half:], second[half:]]).reshape(2, 2 * half, share)
        flat = [learner_routes.T.reshape(-1), learner_gates.T.reshape(-1), traj_lengths.reshape(-1), packing.reshape(-1)]
        notes = jnp.concatenate([a.astype(f32) for a in flat])
        notes = jnp.pad(notes, (0, -notes.shape[0] % 1024)).reshape(1, -1, 128)
        bit = experts // 2
        while bit:
            rows = jnp.concatenate([rows, flipped(rows, "exp", bit)], axis=1)
            notes = jnp.concatenate([notes, flipped(notes, "exp", bit)], axis=0)
            bit //= 2
        rows = rows.reshape(-1, share)
        rows = [rows] + [shifted(rows, "dp", j) for j in range(1, parts)]
        return rows, weights_of(notes.reshape(experts, -1))

    def weights_of(notes):
        slot_count, each = learner_routes.shape
        halves, trajs = traj_lengths.shape[1:]
        per_half = traj_inputs.shape[1]
        longest = slot_count // experts
        ids = jnp.arange(experts, dtype=i32)
        holder_of = ids
        holder_of = jnp.zeros((experts,), i32)
        bit, low = experts // 2, 1
        while bit:
            holder_of = holder_of + jnp.where(ids // low % 2 == 1, bit, 0)
            bit, low = bit // 2, low * 2
        holder_of = holder_of ^ me
        sizes = [slot_count * each, slot_count * each, halves * trajs, experts]
        cuts = np.cumsum(sizes)
        route_table = notes[:, : cuts[0]].reshape(experts, each, slot_count)
        gate_table = notes[:, cuts[0] : cuts[1]].reshape(experts, each, slot_count)
        lengths = notes[:, cuts[1] : cuts[2]].reshape(experts, halves, trajs).astype(i32)
        shards = notes[:, cuts[2] : cuts[3]].astype(i32)
        here = jnp.sum(jnp.where(route_table == me.astype(f32), gate_table, 0.0), axis=1)
        here = here.reshape(experts, experts, longest)
        held = holder_of[:, None] == ids[None, :]
        by_holder = jnp.sum(jnp.where(held[None, :, :, None], here[:, None], 0.0), axis=2)
        sent = shards[:, :, None] == holder_of[None, None, :]
        by_traj = jnp.sum(jnp.where(sent[:, :, :, None], jnp.swapaxes(by_holder, 0, 1)[:, None], 0.0), axis=2)
        by_traj = by_traj.reshape(experts, halves, trajs, longest)
        starts = jnp.cumsum(lengths, axis=2) - lengths
        offset = jnp.arange(per_half, dtype=i32) - starts[..., None]
        inside = (offset >= 0) & (offset < lengths[..., None])
        chosen = inside[..., None] & (offset[..., None] == jnp.arange(longest, dtype=i32))
        weights = jnp.sum(jnp.where(chosen, by_traj[:, :, :, None, :], 0.0), axis=(2, 4))
        return weights.reshape(1, -1)

    def update(rows, weights, up_mat, down_mat):
        small = hidden_here // 6
        tiles = pl.BlockSpec((small, features), lambda i: (i, 0))
        return pl.pallas_call(
            functools.partial(update_kernel, parts, features, hidden),
            grid=(hidden_here // small,),
            out_shape=[jax.ShapeDtypeStruct(up_mat.shape, bf16)] * 2,
            in_specs=[smem, whole(weights)] + [whole(a) for a in rows] + [tiles, tiles],
            out_specs=[tiles, tiles],
            compiler_params=fits(48),
        )(part_ref, weights, *rows, up_mat, down_mat)

    half_steps = steps // 2

    def first_rollout():
        now, sent = states, payload
        for step in range(half_steps):
            now, sent = decode_step(step, now, sent, up_here, down_here)
        return (now, sent) + tuple(unset(up_here, down_here))

    def first_learner():
        rows, weights = learner_rows()
        return (states, payload) + tuple(update(rows, weights, up_here, down_here))

    states, payload, new_up, new_down = lax.cond(is_rollout, first_rollout, first_learner)
    states_there = lax.ppermute(states, "sect", [(0, 1)])
    payload_there = lax.ppermute(payload, "sect", [(0, 1)])
    down_late, _ = lax.optimization_barrier((down_here, states))
    down_there = lax.ppermute(down_late, "sect", [(1, 0)])

    def second_rollout():
        rows, weights = learner_rows()
        return states, rows, weights

    def second_learner():
        now, sent = states_there, payload_there
        for step in range(half_steps, steps):
            now, sent = decode_step(step, now, sent, new_up, new_down)
        gathered = jax.ShapeDtypeStruct((2 * experts * 2 * traj_inputs.shape[1], share), bf16)
        weights = jax.ShapeDtypeStruct((1, gathered.shape[0] // 2), f32)
        *rows, weights = unset(*[gathered] * parts, weights)
        return now, rows, weights

    states, rows, weights = lax.cond(is_rollout, second_rollout, second_learner)

    mine = states.astype(bf16).reshape(blocks, row_count, lanes).swapaxes(0, 1).reshape(row_count, share)
    spread = jnp.zeros((parts, row_count, share), bf16)
    for j in range(parts):
        piece = shifted(mine, "dp", j) if j else mine
        spread = lax.dynamic_update_slice(spread, piece[None], (lax.rem(part + parts - j, parts), 0, 0))
    joined = spread.swapaxes(0, 1).reshape(row_count, features)
    delivered = lax.ppermute(joined[:, : features // 2], "sect", [(1, 0)])
    final_states = jnp.where(is_rollout, delivered, joined[:, features // 2 :])

    new_up, new_down = lax.cond(
        is_rollout,
        lambda: tuple(update(rows, weights, up_there, down_there)),
        lambda: (new_up, new_down),
    )
    return final_states, new_up[None, None], new_down[None, None]


def solution(mesh):
    in_specs = (
        P("exp", None),
        P(),
        P(None, "exp", None),
        P(None, "exp", None),
        P("sect", "exp", "dp", None),
        P("sect", "exp", "dp", None),
        P("sect", "exp", None),
        P("sect", "exp", None),
        P("exp", None, None),
        P("exp", None),
        P("exp", None),
        P("exp", None),
    )
    out_specs = (P("exp", "sect"), P("sect", "exp", "dp", None), P("sect", "exp", "dp", None))
    return jax.shard_map(on_device, mesh=mesh, in_specs=in_specs, out_specs=out_specs, check_vma=False)
```

time: 460 us -> 203 us (0.44); the launches traced: 454 us -> 202 us
  waiting for transfers between devices: 253 us -> 85.5 us
  local copies, waits for them, and re-layouts: 46.5 us -> 5.31 us
  Pallas kernels: 0 us -> 32.2 us
  matrix products: 24.5 us -> 0 us
  starting transfers between devices: 68.1 us -> 46.6 us
  other arithmetic: 25.7 us -> 7.47 us
  between operations: 14.7 us -> 0.79 us
    all_to_all x9 -> x2, waiting for transfers between devices: 180 us -> 16.9 us  [decode_step(): lax.all_to_all(summed, 'exp', split_axis=0, concat_axis=0, tiled=True)]
    psum x4 -> x0, waiting for transfers between devices: 68 us -> none  [sum_and_return(): summed = lax.psum(partial_out.astype(jnp.bfloat16), 'dp')]
    ppermute x3 -> x18, waiting for transfers between devices: 4.87 us -> 68.6 us  [the longest x7 48.4 us: flipped(): lax.ppermute(array, axis, [(i, i ^ bit) for i in range(lax.axis_size(axis...]
    all_to_all x9 -> x2, starting transfers between devices: 42.9 us -> 6.78 us  [decode_step(): lax.all_to_all(summed, 'exp', split_axis=0, concat_axis=0, tiled=True)]
    pallas_call x0 -> x7, Pallas kernels: none -> 32.2 us  [the longest x1 17 us: update(): pl.pallas_call(functools.partial(update_kernel, parts, features, hidden),...]
    dot_general x14 -> x0, matrix products: 24.5 us -> none  [the longest x4 17.6 us: expert_forward(): jnp.einsum('sh,hd->sd', activated, down_slice, preferred_element_type=jnp...]
    another operation x8 -> x6, local copies, waits for them, and re-layouts: 17.3 us -> 1.62 us  [the longest x2 0.78 us: on_device(): routes = jnp.tile(jnp.swapaxes(decode_routes, 1, 2), (1, 1, blocks))]
    ppermute x3 -> x18, starting transfers between devices: 25.1 us -> 39.8 us  [the longest x1 21.7 us: on_device(): payload_there = lax.ppermute(payload, 'sect', [(0, 1)])]
  transfers between devices with their start and end apart: 16 -> 20, of which waited for: 15 -> 15; matrix products, arithmetic and copies ran while one was open for 8% -> 5% of each run, Pallas kernels for 0% -> 8%
where the time goes in v1:
time: 203 us; the launch traced here: 202 us
  waiting for transfers between devices  85.5 us (42%)
  starting transfers between devices  46.6 us (23%)
  Pallas kernels  32.2 us (16%)
  blocking collectives  24.1 us (12%)
  other arithmetic  7.47 us (4%)
  local copies, waits for them, and re-layouts  5.31 us (3%)
    ppermute x7, waiting for transfers between devices, flipped(): lax.ppermute(array, axis, [(i, i ^ bit) for i in range(lax.axis_size(axis...  48.4 us
    all_to_all x2, blocking collectives, decode_step(): lax.all_to_all(payload, 'exp', split_axis=0, concat_axis=0, tiled=True)  24.1 us
    ppermute x1, starting transfers between devices, on_device(): payload_there = lax.ppermute(payload, 'sect', [(0, 1)])  21.7 us
    pallas_call x1, Pallas kernels, update(): pl.pallas_call(functools.partial(update_kernel, parts, features, hidden),...  17 us
    all_to_all x2, waiting for transfers between devices, decode_step(): lax.all_to_all(summed, 'exp', split_axis=0, concat_axis=0, tiled=True)  16.9 us
    ppermute x7, starting transfers between devices, flipped(): lax.ppermute(array, axis, [(i, i ^ bit) for i in range(lax.axis_size(axis...  12.4 us
    pallas_call x2, Pallas kernels, expert_forward(): pl.pallas_call(functools.partial(expert_kernel, parts, slots, features, h...  11.6 us
    ppermute x1, waiting for transfers between devices, on_device(): delivered = lax.ppermute(joined[:, :features // 2], 'sect', [(1, 0)])  11.1 us
  transfers between devices with their start and end apart: 20, of which 15 were waited for; matrix products, arithmetic and copies ran while one was open for 5% of the time, Pallas kernels for 8%

profile of v1, /device:TPU:0, one launch (start us, length us, event | category | flops | bytes accessed | tf_op | source)
XLA Modules:
  0.0 202.2 jit_solution(11621341640438904525)
XLA Ops:
  0.6 1.5 fusion.20
  2.2 2.9 %collective-permute-start.22 = (bf16[64,1024]{1,0:T(8,128)(2,1)}, bf16[64,1024]{1,0:T(8,128)(2,1)}, u32[]{:S(2)}, u32[]{:S(2)}) collective-permute-start(bf16[64,1024]{1,0:T(8,128)(2,1)} %fusion.20), channel_id=1, source_target_pairs={{0,16},{16,0},{1,17},{17,1},{2,18},{18,2},{3,19},{19,3},{4,20},{20... | collective-permute-start | bytes 393224 | tf_op jit(solution)/shard_map/ppermute | solution.py:26
  5.1 1.3 collective-permute-start.27
  6.4 0.7 tile.8
  7.1 0.1 tile.9.routes_ref
  7.2 0.7 tile.20
  7.9 0.1 tile.21
  8.0 0.9 copy-done
  8.9 0.9 shard_map.148
  9.7 69.6 %conditional.3 = (f32[128,256]{1,0:T(8,128)}, bf16[384,256]{1,0:T(8,128)(2,1)S(1)}, bf16[768,2048]{1,0:T(8,128)(2,1)}, bf16[768,2048]{1,0:T(8,128)(2,1)}) conditional(s32[]{:T(128)} %convert_element_type.135, (s32[128,2]{0,1:T(2,128)}, f32[128,2]{0,1:T(2,128)}, s32[1,2,4]{2,1,0:T(2,128)}, s32[1,8]{1,0:T(1,128)}, s32[]{:T(128)}, /*index=5*/pred[]{:T(512)}, ...), branch_computations={%region_0.6_spmd, %region_6.7_spmd} | conditional | flops 13316569 | bytes 25023388 | solution.py:329
  9.7 13.4 %all_to_all.64 = bf16[8,48,256]{2,1,0:T(8,128)(2,1)S(1)} all-to-all(bf16[8,48,256]{2,1,0:T(8,128)(2,1)S(1)} %bitcast.171), channel_id=1, replica_groups=mesh['sect'=2,'exp'=8,'dp'=2] {'exp'}, dimensions={0} | all-to-all | bytes 393216 | tf_op jit(solution)/shard_map/cond/branch_1_fun/all_to_all | solution.py:239
  23.2 1.4 collective-permute-done.7.refs_1_
  24.6 6.2 %branch_1_fun.6 = (bf16[384,256]{1,0:T(8,128)(2,1)S(1)}, bf16[384,256]{1,0:T(8,128)(2,1)S(1)}) custom-call(s32[1]{0:T(128)} %get-tuple-element.130.part_ref, f32[1,2048]{1,0:T(1,128)} %get-tuple-element.131.gain_ref, bf16[384,384]{1,0:T(8,128)(2,1)} %get-tuple-element.132.order_ref, bf16[384,256]{1,0:T(8,128)(2,1)S(1)} %bitcast.138, ...), custom_call_target="tpu_custom_call" | custom-call | tf_op jit(solution)/shard_map/cond/branch_1_fun/pallas_call | solution.py:223
  30.8 0.2 collective-permute-start.8
  31.0 1.3 collective-permute-done.8
  32.3 0.7 add_convert_fusion.1
  33.1 3.4 %all-to-all-start.1 = ((bf16[8,48,256]{2,1,0:T(8,128)(2,1)}), bf16[8,48,256]{2,1,0:T(8,128)(2,1)S(1)}, u32[]{:S(2)}, u32[]{:S(2)}) async-start(bf16[8,48,256]{2,1,0:T(8,128)(2,1)} %bitcast.161), calls=%async_computation.1 | async-start | bytes 393216 | tf_op jit(solution)/shard_map/cond/branch_1_fun/all_to_all | solution.py:244
  36.5 8.4 %all-to-all-done.1 = bf16[8,48,256]{2,1,0:T(8,128)(2,1)S(1)} async-done(((bf16[8,48,256]{2,1,0:T(8,128)(2,1)}), bf16[8,48,256]{2,1,0:T(8,128)(2,1)S(1)}, u32[]{:S(2)}, u32[]{:S(2)}) %all-to-all-start.1) | async-done | bytes 196640 | tf_op jit(solution)/shard_map/cond/branch_1_fun/all_to_all | solution.py:244
  44.9 1.6 branch_1_fun.7
  46.5 10.7 %all_to_all.65 = bf16[8,48,256]{2,1,0:T(8,128)(2,1)S(1)} all-to-all(bf16[8,48,256]{2,1,0:T(8,128)(2,1)S(1)} %bitcast.145), channel_id=1, replica_groups=mesh['sect'=2,'exp'=8,'dp'=2] {'exp'}, dimensions={0} | all-to-all | bytes 393216 | tf_op jit(solution)/shard_map/cond/branch_1_fun/all_to_all | solution.py:239
  57.2 1.4 collective-permute-done.9.refs_1_
  58.7 5.4 %branch_1_fun.8 = (bf16[384,256]{1,0:T(8,128)(2,1)S(1)}, bf16[384,256]{1,0:T(8,128)(2,1)S(1)}) custom-call(s32[1]{0:T(128)} %get-tuple-element.130.part_ref, f32[1,2048]{1,0:T(1,128)S(1)} %copy-done.4, bf16[384,384]{1,0:T(8,128)(2,1)} %get-tuple-element.132.order_ref, bf16[384,256]{1,0:T(8,128)(2,1)S(1)} %bitcast.134, ...), custom_call_target="tpu_custom_call" | custom-call | tf_op jit(solution)/shard_map/cond/branch_1_fun/pallas_call | solution.py:223
  64.1 0.2 collective-permute-start.10
  64.3 1.3 collective-permute-done.10
  65.6 0.7 add_convert_fusion
  66.3 3.4 %all-to-all-start.3 = ((bf16[8,48,256]{2,1,0:T(8,128)(2,1)}), bf16[8,48,256]{2,1,0:T(8,128)(2,1)S(1)}, u32[]{:S(2)}, u32[]{:S(2)}) async-start(bf16[8,48,256]{2,1,0:T(8,128)(2,1)} %bitcast.32), calls=%async_computation.3 | async-start | bytes 393216 | tf_op jit(solution)/shard_map/cond/branch_1_fun/all_to_all | solution.py:244
  69.7 8.5 %all-to-all-done.3 = bf16[8,48,256]{2,1,0:T(8,128)(2,1)S(1)} async-done(((bf16[8,48,256]{2,1,0:T(8,128)(2,1)}), bf16[8,48,256]{2,1,0:T(8,128)(2,1)S(1)}, u32[]{:S(2)}, u32[]{:S(2)}) %all-to-all-start.3) | async-done | bytes 196640 | tf_op jit(solution)/shard_map/cond/branch_1_fun/all_to_all | solution.py:244
  78.2 1.1 branch_1_fun.9
  79.3 1.3 collective-permute-start.28
  80.6 21.7 %collective-permute-start.23 = (bf16[384,256]{1,0:T(8,128)(2,1)S(1)}, bf16[384,256]{1,0:T(8,128)(2,1)S(1)}, u32[]{:S(2)}, u32[]{:S(2)}) collective-permute-start(bf16[384,256]{1,0:T(8,128)(2,1)S(1)} %get-tuple-element.199), channel_id=1, source_target_pairs={{0,16},{1,17},{2,18},{3,19},{4,20},{5,21},{6,22},{7,23},{8,24},{9,... | collective-permute-start | bytes 589832 | tf_op jit(solution)/shard_map/ppermute | solution.py:331
  102.3 1.3 collective-permute-start.24
  103.6 3.4 %collective-permute-done.24 = f32[128,256]{1,0:T(8,128)S(1)} collective-permute-done((f32[128,256]{1,0:T(8,128)}, f32[128,256]{1,0:T(8,128)S(1)}, u32[]{:S(2)}, u32[]{:S(2)}) %collective-permute-start.24) | collective-permute-done | bytes 131104 | tf_op jit(solution)/shard_map/ppermute | solution.py:330
  107.0 62.6 %conditional.4 = (f32[128,256]{1,0:T(8,128)S(1)}, bf16[1024,1024]{1,0:T(8,128)(2,1)}, bf16[1024,1024]{1,0:T(8,128)(2,1)}, f32[1,512]{1,0:T(1,128)S(1)}) conditional(s32[]{:T(128)} %convert_element_type.135, (s32[4,2,128]{2,1,0:T(2,128)S(1)}, f32[4,2,128]{2,1,0:T(2,128)S(1)}, bf16[384,256]{1,0:T(8,128)(2,1)S(1)}, s32[1]{0:T(128)}, ...), branch_computations={%region_7.8_spmd, %region_8.14_spmd} | conditional | flops 13316569 | bytes 25809848 | solution.py:348
  107.0 1.0 broadcast_select_fusion.3
  108.1 3.0 %collective-permute-start.15 = (bf16[2,64,1024]{2,1,0:T(8,128)(2,1)S(1)}, bf16[2,64,1024]{2,1,0:T(8,128)(2,1)S(1)}, u32[]{:S(2)}, u32[]{:S(2)}) collective-permute-start(bf16[2,64,1024]{2,1,0:T(8,128)(2,1)S(1)} %bitcast.157), channel_id=1, source_target_pairs={{0,8},{2,10},{4,12},{6,14},{8,0},{10,2},{12,4},{14,6},{1,9},{3,11}... | collective-permute-start | bytes 786440 | tf_op jit(solution)/shard_map/cond/branch_1_fun/ppermute | solution.py:26
  111.0 8.3 %collective-permute-done.15 = bf16[2,64,1024]{2,1,0:T(8,128)(2,1)S(1)} collective-permute-done((bf16[2,64,1024]{2,1,0:T(8,128)(2,1)S(1)}, bf16[2,64,1024]{2,1,0:T(8,128)(2,1)S(1)}, u32[]{:S(2)}, u32[]{:S(2)}) %collective-permute-start.15) | collective-permute-done | bytes 262176 | tf_op jit(solution)/shard_map/cond/branch_1_fun/ppermute | solution.py:26
  119.4 0.7 collective-permute-start.16
  120.1 11.5 %collective-permute-done.16 = bf16[2,128,1024]{2,1,0:T(8,128)(2,1)S(1)} collective-permute-done((bf16[2,128,1024]{2,1,0:T(8,128)(2,1)S(1)}, bf16[2,128,1024]{2,1,0:T(8,128)(2,1)S(1)}, u32[]{:S(2)}, u32[]{:S(2)}) %collective-permute-start.16) | collective-permute-done | bytes 524320 | tf_op jit(solution)/shard_map/cond/branch_1_fun/ppermute | solution.py:26
  131.7 1.6 collective-permute-start.17
  133.3 21.1 %collective-permute-done.17 = bf16[2,256,1024]{2,1,0:T(8,128)(2,1)S(1)} collective-permute-done((bf16[2,256,1024]{2,1,0:T(8,128)(2,1)S(1)}, bf16[2,256,1024]{2,1,0:T(8,128)(2,1)S(1)}, u32[]{:S(2)}, u32[]{:S(2)}) %collective-permute-start.17) | collective-permute-done | bytes 1048608 | tf_op jit(solution)/shard_map/cond/branch_1_fun/ppermute | solution.py:26
  154.4 1.6 pad_maximum_fusion.10
  156.1 2.0 %collective-permute-start.19 = (f32[1,8,128]{2,1,0:T(8,128)S(1)}, f32[1,8,128]{2,1,0:T(8,128)S(1)}, u32[]{:S(2)}, u32[]{:S(2)}) collective-permute-start(f32[1,8,128]{2,1,0:T(8,128)S(1)} %get-tuple-element.248), channel_id=1, source_target_pairs={{0,8},{2,10},{4,12},{6,14},{8,0},{10,2},{12,4},{14,6},{1,9},{3,11}... | collective-permute-start | bytes 12296 | tf_op jit(solution)/shard_map/cond/branch_1_fun/ppermute | solution.py:26
  158.2 2.5 %collective-permute-done.19 = f32[1,8,128]{2,1,0:T(8,128)S(1)} collective-permute-done((f32[1,8,128]{2,1,0:T(8,128)S(1)}, f32[1,8,128]{2,1,0:T(8,128)S(1)}, u32[]{:S(2)}, u32[]{:S(2)}) %collective-permute-start.19) | collective-permute-done | bytes 4128 | tf_op jit(solution)/shard_map/cond/branch_1_fun/ppermute | solution.py:26
  160.6 0.6 collective-permute-start.20
  161.3 3.0 %collective-permute-done.20 = f32[2,8,128]{2,1,0:T(8,128)S(1)} collective-permute-done((f32[2,8,128]{2,1,0:T(8,128)S(1)}, f32[2,8,128]{2,1,0:T(8,128)S(1)}, u32[]{:S(2)}, u32[]{:S(2)}) %collective-permute-start.20) | collective-permute-done | bytes 8224 | tf_op jit(solution)/shard_map/cond/branch_1_fun/ppermute | solution.py:26
  164.3 1.5 collective-permute-start.21
  165.9 2.1 %collective-permute-done.21 = f32[4,8,128]{2,1,0:T(8,128)S(1)} collective-permute-done((f32[4,8,128]{2,1,0:T(8,128)S(1)}, f32[4,8,128]{2,1,0:T(8,128)S(1)}, u32[]{:S(2)}, u32[]{:S(2)}) %collective-permute-start.21) | collective-permute-done | bytes 16416 | tf_op jit(solution)/shard_map/cond/branch_1_fun/ppermute | solution.py:26
  168.1 0.1 copy.71
  168.2 0.2 select_reduce_fusion.5
  168.6 0.1 copy.62
  168.7 0.1 copy.61
  168.9 0.2 select_reduce_fusion.4
  169.1 0.1 compare_and_fusion.1
  169.3 0.2 select_reduce_fusion.3
  169.5 0.1 reshape.455
  169.9 0.9 dynamic_update_slice.6
  170.8 0.2 collective-permute-done.25
  171.0 0.1 copy.68
  171.1 0.9 dynamic_update_slice.7
  172.1 1.3 collective-permute-start.26
  173.4 11.1 %collective-permute-done.26 = bf16[32,1024]{1,0:T(8,128)(2,1)S(1)} collective-permute-done((bf16[32,1024]{1,0:T(8,128)(2,1)S(1)}, bf16[32,1024]{1,0:T(8,128)(2,1)S(1)}, u32[]{:S(2)}, u32[]{:S(2)}) %collective-permute-start.26) | collective-permute-done | bytes 65568 | tf_op jit(solution)/shard_map/ppermute | solution.py:356
  184.5 0.6 slice_select_fusion
  185.2 17.0 %conditional.5 = ((bf16[768,2048]{1,0:T(8,128)(2,1)}, bf16[768,2048]{1,0:T(8,128)(2,1)})) conditional(s32[]{:T(128)} %convert_element_type.135, (bf16[768,2048]{1,0:T(8,128)(2,1)}, bf16[768,2048]{1,0:T(8,128)(2,1)}) %tuple.49, (s32[1]{0:T(128)}, f32[1,512]{1,0:T(1,128)S(1)}, bf16[1024,1024]{1,0:T(8,128)(2,1)}, bf16[1024,1024]{1,0:T(8,128)(2,1)}, ...), branch_computations={%region_14.15_spmd, %region_15.16_spmd} | conditional | bytes 8 | solution.py:359
  185.2 17.0 %branch_1_fun.11 = (bf16[768,2048]{1,0:T(8,128)(2,1)}, bf16[768,2048]{1,0:T(8,128)(2,1)}) custom-call(s32[1]{0:T(128)} %get-tuple-element.173.part_ref, f32[1,512]{1,0:T(1,128)S(1)} %get-tuple-element.174.weight_ref, bf16[1024,1024]{1,0:T(8,128)(2,1)} %get-tuple-element.175.refs_0_, bf16[1024,1024]{1,0:T(8,128)(2,1)} %get-tuple-element.176.refs_1_, ...), custom_call_target="tpu_custom_call" | custom-call | tf_op jit(solution)/shard_map/cond/branch_1_fun/pallas_call | solution.py:308
  (60 shorter events, 1.2 us)
Async XLA Ops:
  2.2 7.6 %collective-permute-start.22 = (bf16[64,1024]{1,0:T(8,128)(2,1)}, bf16[64,1024]{1,0:T(8,128)(2,1)}, u32[]{:S(2)}, u32[]{:S(2)}) collective-permute-start(bf16[64,1024]{1,0:T(8,128)(2,1)} %fusion.20), channel_id=1, source_target_pairs={{0,16},{16,0},{1,17},{17,1},{2,18},{18,2},{3,19},{19,3},{4,20},{20... | collective-permute-start | bytes 393224 | tf_op jit(solution)/shard_map/ppermute | solution.py:26
  5.1 180.1 %collective-permute-start.27 = (bf16[768,2048]{1,0:T(8,128)(2,1)}, bf16[768,2048]{1,0:T(8,128)(2,1)}, u32[]{:S(2)}, u32[]{:S(2)}) collective-permute-start(bf16[768,2048]{1,0:T(8,128)(2,1)} %bitcast.147), channel_id=1, source_target_pairs={{16,0},{17,1},{18,2},{19,3},{20,4},{21,5},{22,6},{23,7},{24,8},{25... | collective-permute-start | bytes 9437192 | tf_op jit(solution)/shard_map/ppermute | solution.py:198
  8.0 0.9 copy-start
  23.2 1.4 collective-permute-start.7
  24.6 34.1 %copy-start.1 = (bf16[768,2048]{1,0:T(8,128)(2,1)S(1)}, bf16[768,2048]{1,0:T(8,128)(2,1)}, u32[]{:S(2)}) copy-start(bf16[768,2048]{1,0:T(8,128)(2,1)} %get-tuple-element.134.refs_2_) | copy-start | bytes 9437188 | tf_op jit(solution)/shard_map/cond
  24.6 34.1 %copy-start.4 = (f32[1,2048]{1,0:T(1,128)S(1)}, f32[1,2048]{1,0:T(1,128)}, u32[]{:S(2)}) copy-start(f32[1,2048]{1,0:T(1,128)} %get-tuple-element.131.gain_ref) | copy-start | bytes 24580 | tf_op jit(solution)/shard_map/cond
  30.8 1.5 collective-permute-start.8
  33.1 11.9 %all-to-all-start.1 = ((bf16[8,48,256]{2,1,0:T(8,128)(2,1)}), bf16[8,48,256]{2,1,0:T(8,128)(2,1)S(1)}, u32[]{:S(2)}, u32[]{:S(2)}) async-start(bf16[8,48,256]{2,1,0:T(8,128)(2,1)} %bitcast.161), calls=%async_computation.1 | async-start | bytes 393216 | tf_op jit(solution)/shard_map/cond/branch_1_fun/all_to_all | solution.py:244
  57.2 1.4 collective-permute-start.9
  64.1 1.5 collective-permute-start.10
  66.3 11.9 %all-to-all-start.3 = ((bf16[8,48,256]{2,1,0:T(8,128)(2,1)}), bf16[8,48,256]{2,1,0:T(8,128)(2,1)S(1)}, u32[]{:S(2)}, u32[]{:S(2)}) async-start(bf16[8,48,256]{2,1,0:T(8,128)(2,1)} %bitcast.32), calls=%async_computation.3 | async-start | bytes 393216 | tf_op jit(solution)/shard_map/cond/branch_1_fun/all_to_all | solution.py:244
  79.3 105.9 %collective-permute-start.28 = (bf16[768,2048]{1,0:T(8,128)(2,1)}, bf16[768,2048]{1,0:T(8,128)(2,1)}, u32[]{:S(2)}, u32[]{:S(2)}) collective-permute-start(bf16[768,2048]{1,0:T(8,128)(2,1)} %bitcast.152), channel_id=1, source_target_pairs={{16,0},{17,1},{18,2},{19,3},{20,4},{21,5},{22,6},{23,7},{24,8},{25... | collective-permute-start | bytes 9437192 | tf_op jit(solution)/shard_map/ppermute | solution.py:333
  80.6 26.4 %collective-permute-start.23 = (bf16[384,256]{1,0:T(8,128)(2,1)S(1)}, bf16[384,256]{1,0:T(8,128)(2,1)S(1)}, u32[]{:S(2)}, u32[]{:S(2)}) collective-permute-start(bf16[384,256]{1,0:T(8,128)(2,1)S(1)} %get-tuple-element.199), channel_id=1, source_target_pairs={{0,16},{1,17},{2,18},{3,19},{4,20},{5,21},{6,22},{7,23},{8,24},{9,... | collective-permute-start | bytes 589832 | tf_op jit(solution)/shard_map/ppermute | solution.py:331
  102.3 4.7 %collective-permute-start.24 = (f32[128,256]{1,0:T(8,128)}, f32[128,256]{1,0:T(8,128)S(1)}, u32[]{:S(2)}, u32[]{:S(2)}) collective-permute-start(f32[128,256]{1,0:T(8,128)} %get-tuple-element.202), channel_id=1, source_target_pairs={{0,16},{1,17},{2,18},{3,19},{4,20},{5,21},{6,22},{7,23},{8,24},{9,... | collective-permute-start | bytes 393224 | tf_op jit(solution)/shard_map/ppermute | solution.py:330
  108.1 11.2 %collective-permute-start.15 = (bf16[2,64,1024]{2,1,0:T(8,128)(2,1)S(1)}, bf16[2,64,1024]{2,1,0:T(8,128)(2,1)S(1)}, u32[]{:S(2)}, u32[]{:S(2)}) collective-permute-start(bf16[2,64,1024]{2,1,0:T(8,128)(2,1)S(1)} %bitcast.157), channel_id=1, source_target_pairs={{0,8},{2,10},{4,12},{6,14},{8,0},{10,2},{12,4},{14,6},{1,9},{3,11}... | collective-permute-start | bytes 786440 | tf_op jit(solution)/shard_map/cond/branch_1_fun/ppermute | solution.py:26
  119.3 36.6 %copy-start.13 = (s32[1,8]{1,0:T(1,128)S(1)}, s32[1,8]{1,0:T(1,128)}, u32[]{:S(2)}) copy-start(s32[1,8]{1,0:T(1,128)} %get-tuple-element.171) | copy-start | bytes 100 | tf_op jit(solution)/shard_map/cond
  119.4 36.6 %copy-start.9 = (s32[1,2,4]{2,1,0:T(2,128)S(1)}, s32[1,2,4]{2,1,0:T(2,128)}, u32[]{:S(2)}) copy-start(s32[1,2,4]{2,1,0:T(2,128)} %get-tuple-element.170) | copy-start | bytes 100 | tf_op jit(solution)/shard_map/cond
  119.4 36.7 %copy-start.7 = (s32[128,2]{0,1:T(2,128)S(1)}, s32[128,2]{0,1:T(2,128)}, u32[]{:S(2)}) copy-start(s32[128,2]{0,1:T(2,128)} %get-tuple-element.168) | copy-start | bytes 3076 | tf_op jit(solution)/shard_map/cond
  119.4 36.7 %copy-start.11 = (f32[128,2]{0,1:T(2,128)S(1)}, f32[128,2]{0,1:T(2,128)}, u32[]{:S(2)}) copy-start(f32[128,2]{0,1:T(2,128)} %get-tuple-element.169) | copy-start | bytes 3076 | tf_op jit(solution)/shard_map/cond
  119.4 46.5 %copy-start.3 = (f32[128,256]{1,0:T(8,128)S(1)}, f32[128,256]{1,0:T(8,128)}, u32[]{:S(2)}) copy-start(f32[128,256]{1,0:T(8,128)} %get-tuple-element.265) | copy-start | bytes 393220 | tf_op jit(solution)/shard_map/cond
  119.4 12.2 %collective-permute-start.16 = (bf16[2,128,1024]{2,1,0:T(8,128)(2,1)S(1)}, bf16[2,128,1024]{2,1,0:T(8,128)(2,1)S(1)}, u32[]{:S(2)}, u32[]{:S(2)}) collective-permute-start(bf16[2,128,1024]{2,1,0:T(8,128)(2,1)S(1)} %pad_maximum_fusion.12), channel_id=1, source_target_pairs={{0,4},{2,6},{4,0},{6,2},{8,12},{10,14},{12,8},{14,10},{1,5},{3,7},... | collective-permute-start | bytes 1572872 | tf_op jit(solution)/shard_map/cond/branch_1_fun/ppermute | solution.py:26
  131.7 22.7 %collective-permute-start.17 = (bf16[2,256,1024]{2,1,0:T(8,128)(2,1)S(1)}, bf16[2,256,1024]{2,1,0:T(8,128)(2,1)S(1)}, u32[]{:S(2)}, u32[]{:S(2)}) collective-permute-start(bf16[2,256,1024]{2,1,0:T(8,128)(2,1)S(1)} %pad_maximum_fusion.11), channel_id=1, source_target_pairs={{0,2},{2,0},{4,6},{6,4},{8,10},{10,8},{12,14},{14,12},{1,3},{3,1},... | collective-permute-start | bytes 3145736 | tf_op jit(solution)/shard_map/cond/branch_1_fun/ppermute | solution.py:26
  155.9 13.7 %collective-permute-start.18 = (bf16[1024,1024]{1,0:T(8,128)(2,1)}, bf16[1024,1024]{1,0:T(8,128)(2,1)}, u32[]{:S(2)}, u32[]{:S(2)}) collective-permute-start(bf16[1024,1024]{1,0:T(8,128)(2,1)} %bitcast.51), channel_id=1, source_target_pairs={{0,1},{1,0},{2,3},{3,2},{4,5},{5,4},{6,7},{7,6},{8,9},{9,8},{10,11... | collective-permute-start | bytes 6291464 | tf_op jit(solution)/shard_map/cond/branch_1_fun/ppermute | solution.py:22
  156.1 4.5 %collective-permute-start.19 = (f32[1,8,128]{2,1,0:T(8,128)S(1)}, f32[1,8,128]{2,1,0:T(8,128)S(1)}, u32[]{:S(2)}, u32[]{:S(2)}) collective-permute-start(f32[1,8,128]{2,1,0:T(8,128)S(1)} %get-tuple-element.248), channel_id=1, source_target_pairs={{0,8},{2,10},{4,12},{6,14},{8,0},{10,2},{12,4},{14,6},{1,9},{3,11}... | collective-permute-start | bytes 12296 | tf_op jit(solution)/shard_map/cond/branch_1_fun/ppermute | solution.py:26
  160.6 3.7 %collective-permute-start.20 = (f32[2,8,128]{2,1,0:T(8,128)S(1)}, f32[2,8,128]{2,1,0:T(8,128)S(1)}, u32[]{:S(2)}, u32[]{:S(2)}) collective-permute-start(f32[2,8,128]{2,1,0:T(8,128)S(1)} %pad_maximum_fusion.18), channel_id=1, source_target_pairs={{0,4},{2,6},{4,0},{6,2},{8,12},{10,14},{12,8},{14,10},{1,5},{3,7},... | collective-permute-start | bytes 24584 | tf_op jit(solution)/shard_map/cond/branch_1_fun/ppermute | solution.py:26
  164.3 3.7 %collective-permute-start.21 = (f32[4,8,128]{2,1,0:T(8,128)S(1)}, f32[4,8,128]{2,1,0:T(8,128)S(1)}, u32[]{:S(2)}, u32[]{:S(2)}) collective-permute-start(f32[4,8,128]{2,1,0:T(8,128)S(1)} %pad_maximum_fusion.14), channel_id=1, source_target_pairs={{0,2},{2,0},{4,6},{6,4},{8,10},{10,8},{12,14},{14,12},{1,3},{3,1},... | collective-permute-start | bytes 49160 | tf_op jit(solution)/shard_map/cond/branch_1_fun/ppermute | solution.py:26
  169.7 1.3 collective-permute-start.25
  172.1 12.4 %collective-permute-start.26 = (bf16[32,1024]{1,0:T(8,128)(2,1)S(1)}, bf16[32,1024]{1,0:T(8,128)(2,1)S(1)}, u32[]{:S(2)}, u32[]{:S(2)}) collective-permute-start(bf16[32,1024]{1,0:T(8,128)(2,1)S(1)} %slice.94), channel_id=1, source_target_pairs={{16,0},{17,1},{18,2},{19,3},{20,4},{21,5},{22,6},{23,7},{24,8},{25... | collective-permute-start | bytes 196616 | tf_op jit(solution)/shard_map/ppermute | solution.py:356

commit v2 on v1

v2 whole, which is shorter than its diff:
```python
import functools

import jax
import jax.numpy as jnp
from jax import lax
from jax.experimental import pallas as pl
from jax.experimental.pallas import tpu as pltpu
from jax.sharding import PartitionSpec as P

step_size = 3.0
norm_eps = 1e-06
lanes = 256
note_rows = 16
f32, bf16, i32 = jnp.float32, jnp.bfloat16, jnp.int32
nt_dims = (((1,), (1,)), ((), ()))
tn_dims = (((0,), (0,)), ((), ()))
smem = pl.BlockSpec(memory_space=pltpu.SMEM)
vmem = pl.BlockSpec(memory_space=pltpu.VMEM)
anywhere = pl.BlockSpec(memory_space=pl.ANY)
stays = pl.BlockSpec(memory_space=pltpu.HBM)


def shifted(array, axis, by):
    size = lax.axis_size(axis)
    return lax.ppermute(array, axis, [(i, (i + by) % size) for i in range(size)])


def flipped(array, axis, bit):
    return lax.ppermute(array, axis, [(i, i ^ bit) for i in range(lax.axis_size(axis))])


def fits(megabytes):
    return pltpu.CompilerParams(vmem_limit_bytes=megabytes * 1024 * 1024)


def costs(flops, moved):
    return pl.CostEstimate(flops=flops, bytes_accessed=moved, transcendentals=0)


def dot(a, b, dims=(((1,), (0,)), ((), ())), precision=None):
    return lax.dot_general(a, b, dims, precision=precision, preferred_element_type=f32)


def one_hot(rows, targets_ref):
    ids = lax.broadcasted_iota(i32, (rows, targets_ref.shape[1]), 0)
    hits = [jnp.where(ids == targets_ref[k : k + 1, :], 1.0, 0.0) for k in range(targets_ref.shape[0])]
    return sum(hits[1:], hits[0]).astype(bf16)


def prepare_kernel(
    experts, capacity, part_ref, routes_ref, gates_ref, all_rows_ref, inputs_ref, grads_ref,
    targets_ref, tiled_ref, states_ref, payload_ref, own_ref, rows_ref, sems,
):
    row_count, share = rows_ref.shape
    steps, routes_each = targets_ref.shape[:2]
    stacked, width = states_ref.shape
    blocks = stacked // row_count
    own = pl.ds(pl.multiple_of(part_ref[0] * share, share), share)
    held = inputs_ref.shape[0]
    row_copy = pltpu.make_async_copy(all_rows_ref.at[:, own], rows_ref, sems.at[0])
    copies = [
        pltpu.make_async_copy(inputs_ref.at[:, own], own_ref.at[pl.ds(0, held)], sems.at[1]),
        pltpu.make_async_copy(grads_ref.at[:, own], own_ref.at[pl.ds(held, held)], sems.at[2]),
    ]
    row_copy.start()
    for copy in copies:
        copy.start()
    before = lax.broadcasted_iota(i32, (row_count, stacked), 0)
    after = lax.rem(lax.broadcasted_iota(i32, (row_count, stacked), 1), row_count)
    repeat = jnp.where(before == after, 1.0, 0.0)
    earlier = jnp.where(before < after, 1.0, 0.0).astype(bf16)
    every = jnp.ones((row_count, stacked), bf16)
    block_of = lax.div(lax.broadcasted_iota(i32, (1, stacked), 1), row_count)
    expert_ids = lax.broadcasted_iota(i32, (experts, row_count), 0)
    tall_ids = lax.broadcasted_iota(i32, (experts, stacked), 0)
    routes = dot(routes_ref[...].astype(f32), repeat, precision=lax.Precision.HIGHEST)
    routes = (routes + 0.5).astype(i32)
    tiled_ref[...] = dot(gates_ref[...], repeat, precision=lax.Precision.HIGHEST)
    for step in range(steps):
        seen = jnp.zeros((experts, stacked), f32)
        for k in range(routes_each):
            at = step * routes_each + k
            member = jnp.where(expert_ids == routes_ref[at : at + 1, :], 1.0, 0.0).astype(bf16)
            route = routes[at : at + 1, :]
            ahead = dot(member, earlier) + seen
            rank = jnp.sum(jnp.where(tall_ids == route, ahead, 0.0), axis=0, keepdims=True)
            seen = seen + dot(member, every)
            place = (route * blocks + block_of) * capacity + (rank + 0.5).astype(i32)
            targets_ref[step, k : k + 1, :] = place
    row_copy.wait()
    for block in range(blocks):
        columns = slice(block * width, (block + 1) * width)
        states_ref[block * row_count : (block + 1) * row_count, :] = rows_ref[:, columns].astype(f32)
    payload_ref[...] = dot(one_hot(payload_ref.shape[0], targets_ref.at[0]), states_ref[...].astype(bf16)).astype(bf16)
    for copy in copies:
        copy.wait()


def dispatch_kernel(step, targets_ref, states_ref, payload_ref):
    payload_ref[...] = dot(one_hot(payload_ref.shape[0], targets_ref.at[step]), states_ref[...].astype(bf16)).astype(bf16)


def combine_kernel(step, last, targets_ref, gates_ref, states_ref, returned_ref, new_ref, payload_ref):
    ids = lax.broadcasted_iota(i32, (returned_ref.shape[0], states_ref.shape[0]), 0)
    weights = jnp.zeros(ids.shape, f32)
    routes_each = targets_ref.shape[1]
    for k in range(routes_each):
        at = step * routes_each + k
        weights = weights + jnp.where(ids == targets_ref[step, k : k + 1, :], gates_ref[at : at + 1, :], 0.0)
    high = weights.astype(bf16)
    low = (weights - high.astype(f32)).astype(bf16)
    returned = returned_ref[...]
    states = states_ref[...] + (dot(high, returned, tn_dims) + dot(low, returned, tn_dims))
    new_ref[...] = states
    if last:
        payload_ref[...] = states.astype(bf16)
    else:
        payload_ref[...] = dot(one_hot(returned.shape[0], targets_ref.at[step + 1]), states.astype(bf16)).astype(bf16)


def expert_kernel(parts, slots, capacity, features, hidden, part_ref, gain_ref, *refs):
    arrived, (up_ref, down_ref) = refs[:parts], refs[parts : parts + 2]
    outs = refs[parts + 2 : 2 * parts + 2]
    up_held, down_held, normed_ref, stack_ref, order_ref, sems = refs[2 * parts + 2 :]
    width = arrived[0].shape[1]
    blocks = features // (parts * width)
    me = part_ref[0]
    up_copy = pltpu.make_async_copy(up_ref, up_held, sems.at[0])
    down_copy = pltpu.make_async_copy(down_ref, down_held, sems.at[1])
    up_copy.start()
    down_copy.start()
    moved = blocks * slots
    column = lax.broadcasted_iota(i32, (1, moved), 1)
    slot = lax.rem(column, slots)
    target = (lax.div(slot, capacity) * blocks + lax.div(column, slots)) * capacity + lax.rem(slot, capacity)
    hits = lax.broadcasted_iota(i32, (moved, moved), 0) == target
    order_ref[...] = jnp.where(hits, 1.0, 0.0).astype(bf16)
    square = jnp.zeros((slots, 1), f32)
    stacks = []
    for ref in arrived:
        stack = dot(order_ref[...], ref[...], tn_dims)
        stacks.append(stack)
        for block in range(blocks):
            rows = stack[block * slots : (block + 1) * slots]
            square = square + jnp.sum(rows * rows, axis=1, keepdims=True)
    scale = lax.rsqrt(square * (1.0 / features) + norm_eps)
    for j, stack in enumerate(stacks):
        start = lax.rem(me + parts - j, parts) * (blocks * width)
        for block in range(blocks):
            rows = stack[block * slots : (block + 1) * slots]
            columns = pl.ds(pl.multiple_of(start + block * width, width), width)
            normed_ref[:, columns] = (rows * scale * gain_ref[:, columns]).astype(bf16)
    up_copy.wait()
    before_act = dot(normed_ref[...], up_held[...], nt_dims) * features ** (-0.5)
    activated = (before_act / (1.0 + jnp.exp(-before_act))).astype(bf16)
    down_copy.wait()
    normed_ref[...] = (dot(activated, down_held[...]) * hidden ** (-0.5)).astype(bf16)
    for j, out_ref in enumerate(outs):
        start = lax.rem(me + j, parts) * (blocks * width)
        for block in range(blocks):
            columns = pl.ds(pl.multiple_of(start + block * width, width), width)
            stack_ref[block * slots : (block + 1) * slots, :] = normed_ref[:, columns]
        out_ref[...] = dot(order_ref[...], stack_ref[...]).astype(bf16)


def gathered_copies(part, parts, height, units, inputs_ref, grads_ref, sems):
    per_part = len(units) // parts
    width = units[0].shape[1]
    rows = (height - note_rows) // 2
    in_copies, grad_copies = [], []
    for j in range(parts):
        columns = pl.ds(pl.multiple_of(lax.rem(part + parts - j, parts) * width, width), width)
        blocks = [(u, at) for u in units[j * per_part : (j + 1) * per_part] for at in range(0, u.shape[0], height)]
        for i, (unit, at) in enumerate(blocks):
            place, sem = pl.ds(i * rows, rows), 2 * (j * len(blocks) + i)
            source = unit.at[pl.ds(at, rows)]
            in_copies.append(pltpu.make_async_copy(source, inputs_ref.at[place, columns], sems.at[sem]))
            source = unit.at[pl.ds(at + rows, rows)]
            grad_copies.append(pltpu.make_async_copy(source, grads_ref.at[place, columns], sems.at[sem + 1]))
    return in_copies, grad_copies


def unit_kernel(first_ref, second_ref, routes_ref, gates_ref, lengths_ref, shards_ref, unit_ref, sems):
    held = first_ref.shape[0] // 2
    copies = []
    for i, ref in enumerate((first_ref, second_ref)):
        for j in range(2):
            place = pl.ds((2 * j + i) * held, held)
            source = ref.at[pl.ds(j * held, held)]
            copies.append(pltpu.make_async_copy(source, unit_ref.at[place], sems.at[2 * i + j]))
    for copy in copies:
        copy.start()
    wide = routes_ref.shape[1]

    def widened(ref):
        count = ref.shape[1]
        places = lax.broadcasted_iota(i32, (count, wide), 0) == lax.broadcasted_iota(i32, (count, wide), 1)
        return dot(ref[...].astype(f32), jnp.where(places, 1.0, 0.0))

    gates = gates_ref[...]
    terms = []
    for _ in range(3):
        terms.append(gates.astype(bf16).astype(f32))
        gates = gates - terms[-1]
    tables = [routes_ref[...].astype(f32)] + terms + [widened(lengths_ref), widened(shards_ref)]
    ids = lax.broadcasted_iota(i32, (note_rows, wide), 0)
    notes, at = jnp.zeros((note_rows, wide), f32), 0
    for table in tables:
        for row in range(table.shape[0]):
            notes = notes + jnp.where(ids == at, table[row : row + 1, :], 0.0)
            at += 1
    base = 4 * held
    unit_ref[base:, :] = jnp.zeros((note_rows, unit_ref.shape[1]), bf16)
    unit_ref[base:, :wide] = notes.astype(bf16)
    for copy in copies:
        copy.wait()


def weights_kernel(height, halves, each, trajs, wide, sources, me_ref, *refs):
    units, (weights_ref, notes_ref, table_ref, sems) = refs[:-4], refs[-4:]
    blocks = [(u, at) for u in units for at in range(0, u.shape[0], height)]
    count = len(blocks)
    per_half = (height - note_rows) // (2 * halves)
    longest = wide // count
    total = weights_ref.shape[1]
    copies = []
    for i, (unit, at) in enumerate(blocks):
        source = unit.at[pl.ds(at + height - note_rows, note_rows), pl.ds(0, wide)]
        copies.append(pltpu.make_async_copy(source, notes_ref.at[i], sems.at[i]))
    for copy in copies:
        copy.start()
    for copy in copies:
        copy.wait()
    me = me_ref[0]
    holders = []
    for group, flip, far, near in sources:
        place = lax.rem((lax.rem(me, group) ^ flip) + group - far, group)
        holders.append((lax.div(me, group) * group + place) ^ near)
    ids = lax.broadcasted_iota(i32, (count, 1), 0)
    holder_of = jnp.zeros((count, 1), i32)
    for i, holder in enumerate(holders):
        holder_of = holder_of + jnp.where(ids == i, holder, 0)
        notes = notes_ref[i].astype(f32)
        row = jnp.zeros((1, wide), f32)
        for k in range(each):
            gate = sum(notes[(1 + t) * each + k : (1 + t) * each + k + 1, :] for t in range(3))
            row = row + jnp.where(notes[k : k + 1, :] == me.astype(f32), gate, 0.0)
        table_ref[i : i + 1, :] = row
    exact = lax.Precision.HIGHEST
    slot = lax.broadcasted_iota(i32, (wide, longest), 0) - lax.broadcasted_iota(i32, (wide, longest), 1)
    down = lax.broadcasted_iota(i32, (trajs, wide), 0)
    across = lax.broadcasted_iota(i32, (trajs, wide), 1)
    row_ids = lax.broadcasted_iota(i32, (1, total), 1)
    offset_ids = lax.broadcasted_iota(i32, (longest, total), 0)
    weights = jnp.zeros((1, total), f32)
    for i, holder in enumerate(holders):
        own_slots = dot(table_ref[...], jnp.where(slot == holder * longest, 1.0, 0.0), precision=exact)
        notes = notes_ref[i].astype(f32)
        at = 4 * each + halves
        sent = jnp.where(holder_of.astype(f32) == notes[at : at + 1, :count], 1.0, 0.0)
        by_traj = dot(own_slots, sent, tn_dims, precision=exact)
        for half in range(halves):
            lengths = notes[4 * each + half : 4 * each + half + 1, :]
            length = jnp.sum(jnp.where(across == down, lengths, 0.0), axis=1, keepdims=True).astype(i32)
            start = jnp.sum(jnp.where(across < down, lengths, 0.0), axis=1, keepdims=True).astype(i32)
            place = row_ids - (i * halves + half) * per_half
            inside = (place >= start) & (place < start + length)
            offset = place - jnp.sum(jnp.where(inside, start, 0), axis=0, keepdims=True)
            spread = dot(by_traj[:, half * trajs : (half + 1) * trajs], jnp.where(inside, 1.0, 0.0), precision=exact)
            weights = weights + jnp.sum(jnp.where(offset_ids == offset, spread, 0.0), axis=0, keepdims=True)
    weights_ref[...] = weights


def tile_copies(ref, held, tile, sems):
    places = [pl.ds(start, tile) for start in range(0, held.shape[0], tile)]
    return [pltpu.make_async_copy(ref.at[p], held.at[p], sems.at[i]) for i, p in enumerate(places)]


def start_all(*groups):
    for copies in groups:
        for copy in copies:
            copy.start()


def wait_all(copies):
    for copy in copies:
        copy.wait()


def activation(features, up_tile, inputs, weight):
    before_act = dot(up_tile, inputs, nt_dims) * features ** (-0.5)
    sigmoid = 1.0 / (1.0 + jnp.exp(-before_act))
    return (before_act * sigmoid * weight).astype(bf16), sigmoid * (1.0 + before_act * (1.0 - sigmoid)) * weight


def new_tile(old, step, change, rows):
    return (old.astype(f32) - (step_size * step) * dot(change, rows)).astype(bf16)


def learner_kernel(parts, height, features, hidden, tile, part_ref, weight_ref, *refs):
    units, (up_ref, down_ref, new_up_ref, new_down_ref, inputs, grads, up, down, new_up, new_down) = refs[:-13], refs[-13:-3]
    row_sems, sems, out_sems = refs[-3:]
    in_copies, grad_copies = gathered_copies(part_ref[0], parts, height, units, inputs, grads, row_sems)
    up_copies = tile_copies(up_ref, up, tile, sems.at[0])
    down_copies = tile_copies(down_ref, down, tile, sems.at[1])
    up_outs = tile_copies(new_up, new_up_ref, tile, out_sems.at[0])
    down_outs = tile_copies(new_down, new_down_ref, tile, out_sems.at[1])
    start_all(up_copies[:1], in_copies, down_copies[:1], grad_copies, up_copies[1:], down_copies[1:])
    weight = weight_ref[...]
    for i in range(len(up_copies)):
        here = pl.ds(i * tile, tile)
        up_copies[i].wait()
        if i == 0:
            wait_all(in_copies)
        activated, slope = activation(features, up[here, :], inputs[...], weight)
        down_copies[i].wait()
        if i == 0:
            wait_all(grad_copies)
        pre_grad = (dot(down[here, :], grads[...], nt_dims) * hidden ** (-0.5) * slope).astype(bf16)
        new_down[here, :] = new_tile(down[here, :], hidden ** (-0.5), activated, grads[...])
        down_outs[i].start()
        new_up[here, :] = new_tile(up[here, :], features ** (-0.5), pre_grad, inputs[...])
        up_outs[i].start()
    wait_all(up_outs + down_outs)


def forward_kernel(parts, height, features, tile, part_ref, weight_ref, *refs):
    units, (up_ref, inputs, grads, activated, slopes, up, row_sems, sems) = refs[:-8], refs[-8:]
    in_copies, grad_copies = gathered_copies(part_ref[0], parts, height, units, inputs, grads, row_sems)
    up_copies = tile_copies(up_ref, up, tile, sems)
    start_all(up_copies[:1], in_copies, up_copies[1:], grad_copies)
    wait_all(in_copies)
    for i, copy in enumerate(up_copies):
        here = pl.ds(i * tile, tile)
        copy.wait()
        activated[here, :], slopes[here, :] = activation(features, up[here, :], inputs[...], weight_ref[...])
    wait_all(grad_copies)


def late_kernel(features, hidden, tile, go_ref, *refs):
    refs, (up, down, inputs, grads, activated, slopes, new_up, new_down, row_sems, sems, out_sems) = refs[:-11], refs[-11:]
    up_ref, down_ref, inputs_ref, grads_ref, activated_ref, slopes_ref, _, _, new_up_ref, new_down_ref = refs

    @pl.when(go_ref[0] == 1)
    def _():
        up_copies = tile_copies(up_ref, up, tile, sems.at[0])
        down_copies = tile_copies(down_ref, down, tile, sems.at[1])
        active_copies = tile_copies(activated_ref, activated, tile, sems.at[2])
        slope_copies = tile_copies(slopes_ref, slopes, tile, sems.at[3])
        grad_copy = pltpu.make_async_copy(grads_ref, grads, row_sems.at[0])
        in_copy = pltpu.make_async_copy(inputs_ref, inputs, row_sems.at[1])
        up_outs = tile_copies(new_up, new_up_ref, tile, out_sems.at[0])
        down_outs = tile_copies(new_down, new_down_ref, tile, out_sems.at[1])
        start_all([grad_copy], down_copies[:1], slope_copies[:1], active_copies[:1], [in_copy])
        start_all(up_copies[:1], down_copies[1:], slope_copies[1:], active_copies[1:], up_copies[1:])
        grad_copy.wait()
        for i in range(len(up_copies)):
            here = pl.ds(i * tile, tile)
            down_copies[i].wait()
            slope_copies[i].wait()
            hidden_grad = dot(down[here, :], grads[...], nt_dims) * hidden ** (-0.5)
            pre_grad = (hidden_grad * slopes[here, :]).astype(bf16)
            active_copies[i].wait()
            new_down[here, :] = new_tile(down[here, :], hidden ** (-0.5), activated[here, :], grads[...])
            down_outs[i].start()
            if i == 0:
                in_copy.wait()
            up_copies[i].wait()
            new_up[here, :] = new_tile(up[here, :], features ** (-0.5), pre_grad, inputs[...])
            up_outs[i].start()
        wait_all(up_outs + down_outs)


def join_kernel(parts, row_count, part_ref, *refs):
    pieces, (left_ref, right_ref, joined_ref) = refs[:parts], refs[parts:]
    width = pieces[0].shape[1]
    blocks = pieces[0].shape[0] // row_count
    for j, piece in enumerate(pieces):
        start = lax.rem(part_ref[0] + parts - j, parts) * (blocks * width)
        for block in range(blocks):
            columns = pl.ds(pl.multiple_of(start + block * width, width), width)
            joined_ref[:, columns] = piece[block * row_count : (block + 1) * row_count, :]
    half = left_ref.shape[1]
    left_ref[...] = joined_ref[:, :half]
    right_ref[...] = joined_ref[:, half:]


def unset_kernel(*refs):
    pass


def unset(*like):
    arrays = pl.pallas_call(
        unset_kernel,
        out_shape=[jax.ShapeDtypeStruct(a.shape, a.dtype) for a in like],
        out_specs=[anywhere] * len(like),
        cost_estimate=costs(1, 1),
    )()
    return tuple(arrays)


def on_device(
    decode_states,
    norm_gain,
    decode_routes,
    decode_gates,
    up_weight,
    down_weight,
    traj_inputs,
    traj_cotangents,
    traj_lengths,
    packing,
    learner_routes,
    learner_gates,
):
    experts, parts = lax.axis_size("exp"), lax.axis_size("dp")
    is_rollout = lax.axis_index("sect") == 0
    go = is_rollout.astype(i32).reshape(1)
    me = lax.axis_index("exp")
    part_ref = lax.axis_index("dp").reshape(1).astype(i32)
    up_here, down_here = up_weight[0, 0], down_weight[0, 0]
    hidden_here, features = up_here.shape
    hidden = hidden_here * parts
    steps, row_count, routes_each = decode_routes.shape
    half_steps = steps // 2
    share = features // parts
    blocks = share // lanes
    capacity = 3 * row_count * routes_each // (2 * experts)
    slots = experts * capacity
    stacked = blocks * row_count
    moved = blocks * slots
    tile = hidden_here // 3
    line = 8
    per_half = traj_inputs.shape[1]
    gathered = experts * 2 * per_half
    height = 4 * per_half + note_rows

    routes = jnp.swapaxes(decode_routes, 1, 2).reshape(steps * routes_each, row_count)
    gates = jnp.swapaxes(decode_gates, 1, 2).reshape(steps * routes_each, row_count)
    targets, gates, states, payload, own_rows = pl.pallas_call(
        functools.partial(prepare_kernel, experts, capacity),
        out_shape=[
            jax.ShapeDtypeStruct((steps, routes_each, stacked), i32),
            jax.ShapeDtypeStruct((steps * routes_each, stacked), f32),
            jax.ShapeDtypeStruct((stacked, lanes), f32),
            jax.ShapeDtypeStruct((moved, lanes), bf16),
            jax.ShapeDtypeStruct((2 * per_half, share), bf16),
        ],
        in_specs=[smem, vmem, vmem] + [stays] * 3,
        scratch_shapes=[pltpu.VMEM((row_count, share), bf16), pltpu.SemaphoreType.DMA((3,))],
        compiler_params=fits(60),
        cost_estimate=costs(1, 1),
    )(part_ref, routes, gates, decode_states, traj_inputs[0], traj_cotangents[0])

    crossed_rows = flipped(own_rows, "sect", 1)
    up_sent, down_sent, crossed_rows = lax.optimization_barrier((up_here, down_here, crossed_rows))
    up_there = lax.ppermute(up_sent, "sect", [(1, 0)])
    down_there = lax.ppermute(down_sent, "sect", [(1, 0)])

    gain = norm_gain.reshape(1, features)
    def expert_forward(arrived, up_mat, down_mat):
        return pl.pallas_call(
            functools.partial(expert_kernel, parts, slots, capacity, features, hidden),
            out_shape=[jax.ShapeDtypeStruct((moved, lanes), bf16)] * parts,
            in_specs=[smem, vmem] + [vmem] * parts + [stays, stays],
            scratch_shapes=[
                pltpu.VMEM((hidden_here, features), bf16),
                pltpu.VMEM((hidden_here, features), bf16),
                pltpu.VMEM((slots, features), bf16),
                pltpu.VMEM((moved, lanes), bf16),
                pltpu.VMEM((moved, moved), bf16),
                pltpu.SemaphoreType.DMA((2,)),
            ],
            compiler_params=fits(48),
            cost_estimate=costs(1, 1),
        )(part_ref, gain, *arrived, up_mat, down_mat)

    def decode_step(step, states, payload, up_mat, down_mat):
        last = step in (half_steps - 1, steps - 1)
        arrived = lax.all_to_all(payload, "exp", split_axis=0, concat_axis=0, tiled=True)
        arrived = [arrived] + [shifted(arrived, "dp", j) for j in range(1, parts)]
        partials = expert_forward(arrived, up_mat, down_mat)
        received = [shifted(partials[j], "dp", j) for j in range(1, parts)]
        summed = sum((r.astype(f32) for r in received), partials[0].astype(f32)).astype(bf16)
        returned = lax.all_to_all(summed, "exp", split_axis=0, concat_axis=0, tiled=True)
        outs = [
            jax.ShapeDtypeStruct((stacked, lanes), f32),
            jax.ShapeDtypeStruct((stacked if last else moved, lanes), bf16),
        ]
        results = pl.pallas_call(
            functools.partial(combine_kernel, step, last),
            out_shape=outs,
            compiler_params=fits(16),
            cost_estimate=costs(1, 1),
        )(targets, gates, states, returned)
        return tuple(results)
    def learner_rows(halves):
        wide = learner_routes.shape[0]
        notes = [learner_routes.T, learner_gates.T, traj_lengths[0], packing]
        unit = pl.pallas_call(
            unit_kernel,
            out_shape=jax.ShapeDtypeStruct((height, share), bf16),
            in_specs=[anywhere] * 2 + [vmem] * 4,
            scratch_shapes=[pltpu.SemaphoreType.DMA((4,))],
            compiler_params=fits(16),
            cost_estimate=costs(1, 1),
        )(*halves, *notes)
        others, group = [0], experts
        while group > line:
            group = group // 2
            unit = jnp.concatenate([unit, flipped(unit, "exp", group)])
            others = others + [o ^ group for o in others]
        far = group // 2
        shifts = sorted(range(1, far), key=lambda s: (min(s, far - s), s))

        def along(s):
            pairs = [(i, i // group * group + (i + 2 * s) % group) for i in range(experts)]
            return lax.ppermute(unit, "exp", pairs)

        near = jnp.concatenate([along(s) for s in shifts[:-1]])
        sides = [flipped(unit, "exp", 1), flipped(near, "exp", 1)]
        last = along(shifts[-1])
        units = [jnp.concatenate([unit, sides[0], near]), sides[1], last, flipped(last, "exp", 1)]
        places = [(0, 0), (1, 0)] + [(flip, s) for flip in range(2) for s in shifts[:-1]]
        places = places + [(0, shifts[-1]), (1, shifts[-1])]
        sources = [(group, flip, 2 * s, o) for flip, s in places for o in others]
        return units, sources

    def with_parts(units, sources):
        units = list(units)
        others = [shifted(u, "dp", j) for j in range(1, parts) for u in units]
        wide = learner_routes.shape[0]
        weights = pl.pallas_call(
            functools.partial(
                weights_kernel, height, 2, learner_routes.shape[1], traj_lengths.shape[2], wide, sources
            ),
            out_shape=jax.ShapeDtypeStruct((1, gathered), f32),
            in_specs=[smem] + [anywhere] * len(units),
            scratch_shapes=[
                pltpu.VMEM((experts, note_rows, wide), bf16),
                pltpu.VMEM((experts, wide), f32),
                pltpu.SemaphoreType.DMA((experts,)),
            ],
            compiler_params=fits(16),
            cost_estimate=costs(1, 1),
        )(me.reshape(1).astype(i32), *units)
        return units + others, weights

    rows_like = jax.ShapeDtypeStruct((gathered, features), bf16)
    weight_like = jax.ShapeDtypeStruct((hidden_here, features), bf16)
    active_like = jax.ShapeDtypeStruct((hidden_here, gathered), bf16)
    slopes_like = jax.ShapeDtypeStruct((hidden_here, gathered), f32)
    row_space = [pltpu.VMEM(rows_like.shape, bf16)] * 2
    weight_space = pltpu.VMEM(weight_like.shape, bf16)

    def sems_of(*shape):
        return pltpu.SemaphoreType.DMA(shape)

    def update(units, weights, up_mat, down_mat):
        return pl.pallas_call(
            functools.partial(learner_kernel, parts, height, features, hidden, tile),
            out_shape=[weight_like] * 2,
            in_specs=[smem, vmem] + [anywhere] * (len(units) + 2),
            out_specs=[anywhere] * 2,
            scratch_shapes=row_space + [weight_space] * 4 + [sems_of(2 * parts * experts), sems_of(2, 3), sems_of(2, 3)],
            compiler_params=fits(56),
            cost_estimate=costs(1, 1),
        )(part_ref, weights, *units, up_mat, down_mat)

    def update_forward(units, weights):
        return pl.pallas_call(
            functools.partial(forward_kernel, parts, height, features, tile),
            out_shape=[rows_like, rows_like, active_like, slopes_like],
            in_specs=[smem, vmem] + [anywhere] * (len(units) + 1),
            scratch_shapes=[weight_space, sems_of(2 * parts * experts), sems_of(3)],
            compiler_params=fits(56),
            cost_estimate=costs(1, 1),
        )(part_ref, weights, *units, up_there)

    def update_late(known, new_up, new_down):
        space = [weight_space] * 2 + row_space + [pltpu.VMEM(a.shape, a.dtype) for a in (active_like, slopes_like)]
        return pl.pallas_call(
            functools.partial(late_kernel, features, hidden, tile),
            out_shape=[weight_like] * 2,
            in_specs=[smem] + [stays] * 8,
            out_specs=[anywhere] * 2,
            scratch_shapes=space + [weight_space] * 2 + [sems_of(2), sems_of(4, 3), sems_of(2, 3)],
            input_output_aliases={7: 0, 8: 1},
            compiler_params=fits(60),
            cost_estimate=costs(1, 1),
        )(go, up_there, down_there, *known, new_up, new_down)

    final_like = jax.ShapeDtypeStruct((stacked, lanes), bf16)
    block_rows = height * max(1, experts // line)
    gather_like = [jax.ShapeDtypeStruct((block_rows * n, share), bf16) for n in (line // 2, line // 2 - 2, 1, 1)]

    sources = []

    def first_rollout():
        return decode_step(0, states, payload, up_here, down_here) + unset(*gather_like)

    def first_learner():
        units, places = learner_rows([crossed_rows, own_rows])
        sources.append(places)
        return (states, payload) + tuple(units)

    states, payload, *rows = lax.cond(is_rollout, first_rollout, first_learner)

    def second_rollout():
        now, sent = states, payload
        for step in range(1, half_steps):
            now, sent = decode_step(step, now, sent, up_here, down_here)
        return (now,) + tuple(unset(up_here, down_here))

    def second_learner():
        units, weights = with_parts(rows, sources[0])
        return (states,) + tuple(update(units, weights, up_here, down_here))

    states, new_up, new_down = lax.cond(is_rollout, second_rollout, second_learner)
    states_there = lax.ppermute(states, "sect", [(0, 1)])

    def third_rollout():
        return (states, payload) + tuple(learner_rows([own_rows, crossed_rows])[0])

    def third_learner():
        sent = pl.pallas_call(
            functools.partial(dispatch_kernel, half_steps),
            out_shape=jax.ShapeDtypeStruct((moved, lanes), bf16),
            compiler_params=fits(16),
            cost_estimate=costs(1, 1),
        )(targets, states_there)
        return decode_step(half_steps, states_there, sent, new_up, new_down) + unset(*gather_like)

    states, payload, *rows = lax.cond(is_rollout, third_rollout, third_learner)

    def fourth_rollout():
        return unset(final_like) + tuple(update_forward(*with_parts(rows, sources[0])))

    def fourth_learner():
        now, sent = states, payload
        for step in range(half_steps + 1, steps):
            now, sent = decode_step(step, now, sent, new_up, new_down)
        return (sent,) + unset(rows_like, rows_like, active_like, slopes_like)

    mine, *known = lax.cond(is_rollout, fourth_rollout, fourth_learner)

    pieces = [mine] + [shifted(mine, "dp", j) for j in range(1, parts)]
    left, right = pl.pallas_call(
        functools.partial(join_kernel, parts, row_count),
        out_shape=[jax.ShapeDtypeStruct((row_count, features // 2), bf16)] * 2,
        in_specs=[smem] + [vmem] * parts,
        scratch_shapes=[pltpu.VMEM((row_count, features), bf16)],
        cost_estimate=costs(1, 1),
    )(part_ref, *pieces)
    delivered = lax.ppermute(left, "sect", [(1, 0)])
    new_up, new_down = update_late(known, new_up, new_down)
    final_states = jnp.where(is_rollout, delivered, right)
    return final_states, new_up[None, None], new_down[None, None]


def solution(mesh):
    in_specs = (
        P("exp", None),
        P(),
        P(None, "exp", None),
        P(None, "exp", None),
        P("sect", "exp", "dp", None),
        P("sect", "exp", "dp", None),
        P("sect", "exp", None),
        P("sect", "exp", None),
        P("exp", None, None),
        P("exp", None),
        P("exp", None),
        P("exp", None),
    )
    out_specs = (P("exp", "sect"), P("sect", "exp", "dp", None), P("sect", "exp", "dp", None))
    return jax.shard_map(on_device, mesh=mesh, in_specs=in_specs, out_specs=out_specs, check_vma=False)
```

time: 203 us -> 168 us (0.83)
  waiting for transfers between devices: 85.5 us -> 60.3 us
  starting transfers between devices: 46.6 us -> 27.8 us
  Pallas kernels: 32.2 us -> 41.6 us
  other arithmetic: 7.47 us -> 3.37 us
    ppermute x7 -> x4, waiting for transfers between devices: 48.4 us -> 13.3 us  [flipped(): lax.ppermute(array, axis, [(i, i ^ bit) for i in range(lax.axis_size(axis...]
    ppermute x4 -> x6, starting transfers between devices: 25.6 us -> 6.58 us  [the longest x3 2.74 us: along(): return lax.ppermute(unit, 'exp', pairs)]
    ppermute x4 -> x6, waiting for transfers between devices: 11.1 us -> 22.4 us  [the longest x3 22.4 us: along(): return lax.ppermute(unit, 'exp', pairs)]
    pallas_call x5 -> x9, Pallas kernels: 31.3 us -> 39.1 us  [the longest x1 11 us: update_late(): pl.pallas_call(functools.partial(late_kernel, features, hidden, tile), ou...]
    ppermute x7 -> x4, starting transfers between devices: 12.4 us -> 6.61 us  [flipped(): lax.ppermute(array, axis, [(i, i ^ bit) for i in range(lax.axis_size(axis...]
    ppermute x1, starting transfers between devices: 1.3 us -> 6.21 us  [on_device(): states_there = lax.ppermute(states, 'sect', [(0, 1)])]
    cond x19, local copies, waits for them, and re-layouts: 0.23 us -> 4.82 us
    concatenate x7 -> x2, other arithmetic: 3.28 us -> 1.2 us  [the longest x1 1.16 us: learner_rows(): jnp.concatenate([unit, sides[0], near])]
  transfers between devices with their start and end apart: 20 -> 22, of which waited for: 15 -> 14; matrix products, arithmetic and copies ran while one was open for 5% -> 3% of each run, Pallas kernels for 8% -> 24%
where the time goes in v2:
time: 168 us; the launch traced here: 165 us
  waiting for transfers between devices  60.3 us (36%)
  Pallas kernels  41.6 us (25%)
  starting transfers between devices  27.8 us (17%)
  blocking collectives  24.3 us (14%)
  local copies, waits for them, and re-layouts  7.07 us (4%)
  other arithmetic  3.37 us (2%)
    all_to_all x2, blocking collectives, decode_step(): lax.all_to_all(payload, 'exp', split_axis=0, concat_axis=0, tiled=True)  24.3 us
    ppermute x3, waiting for transfers between devices, along(): return lax.ppermute(unit, 'exp', pairs)  22.4 us
    all_to_all x2, waiting for transfers between devices, decode_step(): lax.all_to_all(summed, 'exp', split_axis=0, concat_axis=0, tiled=True)  15.1 us
    ppermute x4, waiting for transfers between devices, flipped(): lax.ppermute(array, axis, [(i, i ^ bit) for i in range(lax.axis_size(axis...  13.3 us
    pallas_call x1, Pallas kernels, update_late(): pl.pallas_call(functools.partial(late_kernel, features, hidden, tile), ou...  11 us
    pallas_call x2, Pallas kernels, expert_forward(): pl.pallas_call(functools.partial(expert_kernel, parts, slots, capacity, f...  10.2 us
    pallas_call x1, Pallas kernels, update_forward(): pl.pallas_call(functools.partial(forward_kernel, parts, height, features,...  8.52 us
    all_to_all x2, starting transfers between devices, decode_step(): lax.all_to_all(summed, 'exp', split_axis=0, concat_axis=0, tiled=True)  6.78 us
  transfers between devices with their start and end apart: 22, of which 14 were waited for; matrix products, arithmetic and copies ran while one was open for 3% of the time, Pallas kernels for 24%

profile of v2, /device:TPU:0, one launch (start us, length us, event | category | flops | bytes accessed | tf_op | source)
XLA Modules:
  0.0 165.5 jit_solution(4093129251645978439)
XLA Ops:
  0.6 2.5 %shard_map.139 = (s32[4,2,128]{2,1,0:T(2,128)S(1)}, f32[8,128]{1,0:T(8,128)S(1)}, f32[128,256]{1,0:T(8,128)}, bf16[384,256]{1,0:T(8,128)(2,1)S(1)}, bf16[64,1024]{1,0:T(8,128)(2,1)}) custom-call(s32[1]{0:T(128)} %bitcast.24.part_ref, s32[8,32]{1,0:T(8,128)} %bitcast.70, f32[8,32]{1,0:T(8,128)} %bitcast.71, bf16[32,2048]{1,0:T(8,128)(2,1)} %all_rows_ref.1, ...), custom_call_target="tpu_custom_call" | custom-call | flops 1 | bytes 1 | tf_op jit(solution)/shard_map/pallas_call | solution.py:440
  3.1 3.0 %collective-permute-start.28 = (bf16[64,1024]{1,0:T(8,128)(2,1)}, bf16[64,1024]{1,0:T(8,128)(2,1)}, u32[]{:S(2)}, u32[]{:S(2)}) collective-permute-start(bf16[64,1024]{1,0:T(8,128)(2,1)} %get-tuple-element.259), channel_id=1, source_target_pairs={{0,16},{16,0},{1,17},{17,1},{2,18},{18,2},{3,19},{19,3},{4,20},{20... | collective-permute-start | bytes 393224 | tf_op jit(solution)/shard_map/ppermute | solution.py:29
  6.1 3.8 %collective-permute-done.28 = bf16[64,1024]{1,0:T(8,128)(2,1)} collective-permute-done((bf16[64,1024]{1,0:T(8,128)(2,1)}, bf16[64,1024]{1,0:T(8,128)(2,1)}, u32[]{:S(2)}, u32[]{:S(2)}) %collective-permute-start.28) | collective-permute-done | bytes 131104 | tf_op jit(solution)/shard_map/ppermute | solution.py:29
  9.9 1.3 collective-permute-start.30
  11.2 35.3 %conditional.4 = (f32[128,256]{1,0:T(8,128)}, bf16[384,256]{1,0:T(8,128)(2,1)S(1)}, bf16[576,1024]{1,0:T(8,128)(2,1)S(1)}, bf16[288,1024]{1,0:T(8,128)(2,1)S(1)}...) conditional(s32[]{:T(128)} %convert_element_type.43, (s32[128,2]{0,1:T(2,128)}, f32[128,2]{0,1:T(2,128)}, ...), branch_computations={%region_0.0_spmd, %region_1.0_spmd} | conditional | flops 5898241 | bytes 11796769 | solution.py:607
  11.3 13.7 %all_to_all.64 = bf16[8,48,256]{2,1,0:T(8,128)(2,1)S(1)} all-to-all(bf16[8,48,256]{2,1,0:T(8,128)(2,1)S(1)} %bitcast.61), channel_id=1, replica_groups=mesh['sect'=2,'exp'=8,'dp'=2] {'exp'}, dimensions={0} | all-to-all | bytes 393216 | tf_op jit(solution)/shard_map/cond/branch_1_fun/all_to_all | solution.py:480
  24.9 1.4 collective-permute-done.14.refs_1_
  26.4 5.1 %branch_1_fun.10 = (bf16[384,256]{1,0:T(8,128)(2,1)S(1)}, bf16[384,256]{1,0:T(8,128)(2,1)S(1)}) custom-call(s32[1]{0:T(128)} %get-tuple-element.137.part_ref, f32[1,2048]{1,0:T(1,128)} %get-tuple-element.138.gain_ref, bf16[384,256]{1,0:T(8,128)(2,1)S(1)} %bitcast.47, bf16[384,256]{1,0:T(8,128)(2,1)S(1)} %collective-permute-done.14.refs_1_, ...), custom_call_target="tpu_custom_call" | custom-call | flops 1 | bytes 1 | tf_op jit(solution)/shard_map/cond/branch_1_fun/pallas_call | solution.py:462
  31.4 0.2 collective-permute-start.15
  31.7 1.3 collective-permute-done.15
  33.0 0.7 add_convert_fusion
  33.7 3.4 %all-to-all-start.1 = ((bf16[8,48,256]{2,1,0:T(8,128)(2,1)}), bf16[8,48,256]{2,1,0:T(8,128)(2,1)S(1)}, u32[]{:S(2)}, u32[]{:S(2)}) async-start(bf16[8,48,256]{2,1,0:T(8,128)(2,1)} %bitcast.5), calls=%async_computation.1 | async-start | bytes 393216 | tf_op jit(solution)/shard_map/cond/branch_1_fun/all_to_all | solution.py:485
  37.1 0.9 copy.61.states_ref
  38.0 7.6 %all-to-all-done.1 = bf16[8,48,256]{2,1,0:T(8,128)(2,1)S(1)} async-done(((bf16[8,48,256]{2,1,0:T(8,128)(2,1)}), bf16[8,48,256]{2,1,0:T(8,128)(2,1)S(1)}, u32[]{:S(2)}, u32[]{:S(2)}) %all-to-all-start.1) | async-done | bytes 196640 | tf_op jit(solution)/shard_map/cond/branch_1_fun/all_to_all | solution.py:485
  45.6 1.0 branch_1_fun.11
  46.5 0.0 copy-start.26
  46.6 0.6 copy-done.8
  47.2 32.3 %conditional.5 = (f32[128,256]{1,0:T(8,128)}, bf16[768,2048]{1,0:T(8,128)(2,1)S(1)}, bf16[768,2048]{1,0:T(8,128)(2,1)}) conditional(s32[]{:T(128)} %convert_element_type.43, (s32[]{:T(128)}, bf16[576,1024]{1,0:T(8,128)(2,1)S(1)}, bf16[288,1024]{1,0:T(8,128)(2,1)S(1)}, bf16[144,1024]{1,0:T(8,128)(2,1)S(1)}, bf16[144,1024]{1,0:T(8,128)(2,1)S(1)}, ...), branch_computations={%region_2.0_spmd, %region_3.0_spmd} | conditional | flops 393219 | bytes 28320180 | solution.py:619
  47.2 10.7 %all_to_all.65 = bf16[8,48,256]{2,1,0:T(8,128)(2,1)S(1)} all-to-all(bf16[8,48,256]{2,1,0:T(8,128)(2,1)S(1)} %bitcast.62), channel_id=1, replica_groups=mesh['sect'=2,'exp'=8,'dp'=2] {'exp'}, dimensions={0} | all-to-all | bytes 393216 | tf_op jit(solution)/shard_map/cond/branch_1_fun/all_to_all | solution.py:480
  57.9 1.4 collective-permute-done.16.refs_1_
  59.3 5.1 %branch_1_fun.13 = (bf16[384,256]{1,0:T(8,128)(2,1)S(1)}, bf16[384,256]{1,0:T(8,128)(2,1)S(1)}) custom-call(s32[1]{0:T(128)} %get-tuple-element.164.part_ref, f32[1,2048]{1,0:T(1,128)} %get-tuple-element.165.gain_ref, bf16[384,256]{1,0:T(8,128)(2,1)S(1)} %bitcast.49, bf16[384,256]{1,0:T(8,128)(2,1)S(1)} %collective-permute-done.16.refs_1_, ...), custom_call_target="tpu_custom_call" | custom-call | flops 1 | bytes 1 | tf_op jit(solution)/shard_map/cond/branch_1_fun/pallas_call | solution.py:462
  64.4 0.2 collective-permute-start.17
  64.6 1.3 collective-permute-done.17
  65.9 0.7 add_convert_fusion.1
  66.6 3.4 %all-to-all-start.3 = ((bf16[8,48,256]{2,1,0:T(8,128)(2,1)}), bf16[8,48,256]{2,1,0:T(8,128)(2,1)S(1)}, u32[]{:S(2)}, u32[]{:S(2)}) async-start(bf16[8,48,256]{2,1,0:T(8,128)(2,1)} %bitcast.10), calls=%async_computation.3 | async-start | bytes 393216 | tf_op jit(solution)/shard_map/cond/branch_1_fun/all_to_all | solution.py:485
  70.1 0.9 copy.62.states_ref
  71.0 7.6 %all-to-all-done.3 = bf16[8,48,256]{2,1,0:T(8,128)(2,1)S(1)} async-done(((bf16[8,48,256]{2,1,0:T(8,128)(2,1)}), bf16[8,48,256]{2,1,0:T(8,128)(2,1)S(1)}, u32[]{:S(2)}, u32[]{:S(2)}) %all-to-all-start.3) | async-done | bytes 196640 | tf_op jit(solution)/shard_map/cond/branch_1_fun/all_to_all | solution.py:485
  78.5 1.0 branch_1_fun.14
  79.5 1.3 collective-permute-start.33
  80.8 6.2 %collective-permute-start.29 = (f32[128,256]{1,0:T(8,128)}, f32[128,256]{1,0:T(8,128)S(1)}, u32[]{:S(2)}, u32[]{:S(2)}) collective-permute-start(f32[128,256]{1,0:T(8,128)} %get-tuple-element.270), channel_id=1, source_target_pairs={{0,16},{1,17},{2,18},{3,19},{4,20},{5,21},{6,22},{7,23},{8,24},{9,... | collective-permute-start | bytes 393224 | tf_op jit(solution)/shard_map/ppermute | solution.py:620
  87.0 2.8 %collective-permute-done.29 = f32[128,256]{1,0:T(8,128)S(1)} collective-permute-done((f32[128,256]{1,0:T(8,128)}, f32[128,256]{1,0:T(8,128)S(1)}, u32[]{:S(2)}, u32[]{:S(2)}) %collective-permute-start.29) | collective-permute-done | bytes 131104 | tf_op jit(solution)/shard_map/ppermute | solution.py:620
  89.8 42.9 %conditional.6 = (f32[128,256]{1,0:T(8,128)S(1)}, bf16[384,256]{1,0:T(8,128)(2,1)}, bf16[576,1024]{1,0:T(8,128)(2,1)}, bf16[288,1024]{1,0:T(8,128)(2,1)}, bf16[1...) conditional(s32[]{:T(128)} %convert_element_type.43, (s32[4,2,128]{2,1,0:T(2,128)S(1)}, f32[128,256]{1,0:T(8,128)S(1)}, ...), branch_computations={%region_4.0_spmd, %region_5.0_spmd} | conditional | flops 5898241 | bytes 16777588 | solution.py:634
  89.9 1.0 branch_1_fun.16
  90.8 1.2 collective-permute-start.22
  92.0 0.9 collective-permute-start.21
  92.9 0.7 collective-permute-start.24
  93.6 8.0 %collective-permute-done.22 = bf16[144,1024]{1,0:T(8,128)(2,1)S(1)} collective-permute-done((bf16[144,1024]{1,0:T(8,128)(2,1)S(1)}, bf16[144,1024]{1,0:T(8,128)(2,1)S(1)}, u32[]{:S(2)}, u32[]{:S(2)}) %collective-permute-start.22) | collective-permute-done | bytes 294944 | tf_op jit(solution)/shard_map/cond/branch_1_fun/ppermute | solution.py:518
  101.5 5.8 %collective-permute-done.21 = bf16[144,1024]{1,0:T(8,128)(2,1)S(1)} collective-permute-done((bf16[144,1024]{1,0:T(8,128)(2,1)S(1)}, bf16[144,1024]{1,0:T(8,128)(2,1)S(1)}, u32[]{:S(2)}, u32[]{:S(2)}) %collective-permute-start.21) | collective-permute-done | bytes 294944 | tf_op jit(solution)/shard_map/cond/branch_1_fun/ppermute | solution.py:518
  107.4 1.2 collective-permute-start.23
  108.6 0.9 collective-permute-start.20
  109.5 8.6 %collective-permute-done.24 = bf16[144,1024]{1,0:T(8,128)(2,1)S(1)} collective-permute-done((bf16[144,1024]{1,0:T(8,128)(2,1)S(1)}, bf16[144,1024]{1,0:T(8,128)(2,1)S(1)}, u32[]{:S(2)}, u32[]{:S(2)}) %collective-permute-start.24) | collective-permute-done | bytes 294944 | tf_op jit(solution)/shard_map/cond/branch_1_fun/ppermute | solution.py:518
  118.1 1.5 collective-permute-start.25
  119.6 0.9 copy.41
  120.5 7.5 %collective-permute-done.20 = bf16[144,1024]{1,0:T(8,128)(2,1)S(1)} collective-permute-done((bf16[144,1024]{1,0:T(8,128)(2,1)S(1)}, bf16[144,1024]{1,0:T(8,128)(2,1)S(1)}, u32[]{:S(2)}, u32[]{:S(2)}) %collective-permute-start.20) | collective-permute-done | bytes 294944 | tf_op jit(solution)/shard_map/cond/branch_1_fun/ppermute | solution.py:29
  128.0 1.2 pad_maximum_fusion.2
  129.2 2.0 %collective-permute-done.25 = bf16[144,1024]{1,0:T(8,128)(2,1)S(1)} collective-permute-done((bf16[144,1024]{1,0:T(8,128)(2,1)S(1)}, bf16[144,1024]{1,0:T(8,128)(2,1)S(1)}, u32[]{:S(2)}, u32[]{:S(2)}) %collective-permute-start.25) | collective-permute-done | bytes 294944 | tf_op jit(solution)/shard_map/cond/branch_1_fun/ppermute | solution.py:29
  131.2 0.7 copy-done.14
  131.9 0.8 copy-done.6
  132.7 15.3 %conditional.7 = (bf16[128,256]{1,0:T(8,128)(2,1)S(1)}, bf16[512,2048]{1,0:T(8,128)(2,1)}, bf16[512,2048]{1,0:T(8,128)(2,1)}, bf16[768,512]{1,0:T(8,128)(2,1)}, f32[768,512]{1,0:T(8,128)}) conditional(s32[]{:T(128)} %convert_element_type.43, (bf16[384,256]{1,0:T(8,128)(2,1)}, s32[1]{0:T(128)}, f32[1,2048]{1,0:T(1,128)}, ...), branch_computations={%region_6.0_spmd, %region_7.0_spmd} | conditional | flops 393219 | bytes 18882904 | solution.py:645
  132.7 0.5 collective-permute-start.5
  133.2 0.1 collective-permute-start.6
  133.3 0.4 collective-permute-start.7
  133.8 5.1 %branch_1_fun.18.weight_ref = f32[1,512]{1,0:T(1,128)S(1)} custom-call(s32[1]{0:T(128)} %bitcast.23.me_ref, bf16[576,1024]{1,0:T(8,128)(2,1)} %get-tuple-element.214.refs_0_, bf16[288,1024]{1,0:T(8,128)(2,1)} %get-tuple-element.215.refs_1_, bf16[144,1024]{1,0:T(8,128)(2,1)} %get-tuple-element.216.refs_2_, bf16[144,1024]{1,0:T(8,128)(2,1)} %get-tuple-element.217.refs_3_), custom_call_target="tpu_custom_call" | custom-call | flops 1 | bytes 1 | tf_op jit(solution)/shard_map/cond/branch_1_fun/pallas_call | solution.py:533
  138.9 0.0 copy-start
  138.9 0.6 copy-done
  139.5 8.5 %branch_1_fun.19 = (bf16[512,2048]{1,0:T(8,128)(2,1)}, bf16[512,2048]{1,0:T(8,128)(2,1)}, bf16[768,512]{1,0:T(8,128)(2,1)}, f32[768,512]{1,0:T(8,128)}) custom-call(s32[1]{0:T(128)} %get-tuple-element.212.part_ref, f32[1,512]{1,0:T(1,128)} %copy-done, bf16[576,1024]{1,0:T(8,128)(2,1)S(1)} %copy-done.4, bf16[288,1024]{1,0:T(8,128)(2,1)S(1)} %copy-done.7, ...), custom_call_target="tpu_custom_call" | custom-call | flops 1 | bytes 1 | tf_op jit(solution)/shard_map/cond/branch_1_fun/pallas_call | solution.py:571
  148.0 0.1 collective-permute-start.31
  148.2 1.2 collective-permute-done.31.refs_1_
  149.4 0.6 copy-done.22
  150.0 1.5 shard_map.140
  151.5 1.3 collective-permute-start.32
  152.8 11.0 %shard_map.141 = (bf16[768,2048]{1,0:T(8,128)(2,1)S(1)}, bf16[768,2048]{1,0:T(8,128)(2,1)}) custom-call(s32[1]{0:T(128)} %bitcast.34.go_ref, bf16[768,2048]{1,0:T(8,128)(2,1)} %collective-permute-done.30.refs_0_, bf16[768,2048]{1,0:T(8,128)(2,1)} %collective-permute-done.33.refs_1_, ...), custom_call_target="tpu_custom_call", output_to_operand_aliasing={{0}: (7, {}), {1}: (8, {})} | custom-call | flops 1 | bytes 1 | tf_op jit(solution)/shard_map/pallas_call | solution.py:582
  163.8 0.7 broadcast_select_fusion
  164.5 0.9 copy-done.2
  (39 shorter events, 0.1 us)
Async XLA Ops:
  3.1 6.8 %collective-permute-start.28 = (bf16[64,1024]{1,0:T(8,128)(2,1)}, bf16[64,1024]{1,0:T(8,128)(2,1)}, u32[]{:S(2)}, u32[]{:S(2)}) collective-permute-start(bf16[64,1024]{1,0:T(8,128)(2,1)} %get-tuple-element.259), channel_id=1, source_target_pairs={{0,16},{16,0},{1,17},{17,1},{2,18},{18,2},{3,19},{19,3},{4,20},{20... | collective-permute-start | bytes 393224 | tf_op jit(solution)/shard_map/ppermute | solution.py:29
  9.9 122.8 %collective-permute-start.30 = (bf16[768,2048]{1,0:T(8,128)(2,1)}, bf16[768,2048]{1,0:T(8,128)(2,1)}, u32[]{:S(2)}, u32[]{:S(2)}) collective-permute-start(bf16[768,2048]{1,0:T(8,128)(2,1)} %bitcast.52), channel_id=1, source_target_pairs={{16,0},{17,1},{18,2},{19,3},{20,4},{21,5},{22,6},{23,7},{24,8},{25... | collective-permute-start | bytes 9437192 | tf_op jit(solution)/shard_map/ppermute | solution.py:457
  24.9 1.4 collective-permute-start.14
  31.4 1.5 collective-permute-start.15
  33.7 11.9 %all-to-all-start.1 = ((bf16[8,48,256]{2,1,0:T(8,128)(2,1)}), bf16[8,48,256]{2,1,0:T(8,128)(2,1)S(1)}, u32[]{:S(2)}, u32[]{:S(2)}) async-start(bf16[8,48,256]{2,1,0:T(8,128)(2,1)} %bitcast.5), calls=%async_computation.1 | async-start | bytes 393216 | tf_op jit(solution)/shard_map/cond/branch_1_fun/all_to_all | solution.py:485
  46.5 0.7 copy-start.8
  46.5 43.3 %copy-start.23 = (s32[128,2]{0,1:T(2,128)S(1)}, s32[128,2]{0,1:T(2,128)}, u32[]{:S(2)}) copy-start(s32[128,2]{0,1:T(2,128)} %param.30) | copy-start | bytes 3076
  46.5 43.3 %copy-start.24 = (f32[128,2]{0,1:T(2,128)S(1)}, f32[128,2]{0,1:T(2,128)}, u32[]{:S(2)}) copy-start(f32[128,2]{0,1:T(2,128)} %param.31) | copy-start | bytes 3076
  46.5 43.3 %copy-start.25 = (s32[1,2,4]{2,1,0:T(2,128)S(1)}, s32[1,2,4]{2,1,0:T(2,128)}, u32[]{:S(2)}) copy-start(s32[1,2,4]{2,1,0:T(2,128)} %param.28) | copy-start | bytes 100
  46.5 43.3 %copy-start.26 = (s32[1,8]{1,0:T(1,128)S(1)}, s32[1,8]{1,0:T(1,128)}, u32[]{:S(2)}) copy-start(s32[1,8]{1,0:T(1,128)} %param.29) | copy-start | bytes 100
  57.9 1.4 collective-permute-start.16
  64.4 1.5 collective-permute-start.17
  66.6 11.9 %all-to-all-start.3 = ((bf16[8,48,256]{2,1,0:T(8,128)(2,1)}), bf16[8,48,256]{2,1,0:T(8,128)(2,1)S(1)}, u32[]{:S(2)}, u32[]{:S(2)}) async-start(bf16[8,48,256]{2,1,0:T(8,128)(2,1)} %bitcast.10), calls=%async_computation.3 | async-start | bytes 393216 | tf_op jit(solution)/shard_map/cond/branch_1_fun/all_to_all | solution.py:485
  79.5 73.3 %collective-permute-start.33 = (bf16[768,2048]{1,0:T(8,128)(2,1)}, bf16[768,2048]{1,0:T(8,128)(2,1)}, u32[]{:S(2)}, u32[]{:S(2)}) collective-permute-start(bf16[768,2048]{1,0:T(8,128)(2,1)} %bitcast.59), channel_id=1, source_target_pairs={{16,0},{17,1},{18,2},{19,3},{20,4},{21,5},{22,6},{23,7},{24,8},{25... | collective-permute-start | bytes 9437192 | tf_op jit(solution)/shard_map/ppermute | solution.py:458
  80.8 9.0 %collective-permute-start.29 = (f32[128,256]{1,0:T(8,128)}, f32[128,256]{1,0:T(8,128)S(1)}, u32[]{:S(2)}, u32[]{:S(2)}) collective-permute-start(f32[128,256]{1,0:T(8,128)} %get-tuple-element.270), channel_id=1, source_target_pairs={{0,16},{1,17},{2,18},{3,19},{4,20},{5,21},{6,22},{7,23},{8,24},{9,... | collective-permute-start | bytes 393224 | tf_op jit(solution)/shard_map/ppermute | solution.py:620
  90.8 10.7 %collective-permute-start.22 = (bf16[144,1024]{1,0:T(8,128)(2,1)S(1)}, bf16[144,1024]{1,0:T(8,128)(2,1)S(1)}, u32[]{:S(2)}, u32[]{:S(2)}) collective-permute-start(bf16[144,1024]{1,0:T(8,128)(2,1)S(1)} %branch_1_fun.16), channel_id=1, source_target_pairs={{0,12},{2,14},{4,0},{6,2},{8,4},{10,6},{12,8},{14,10},{1,13},{3,15... | collective-permute-start | bytes 884744 | tf_op jit(solution)/shard_map/cond/branch_1_fun/ppermute | solution.py:518
  92.0 15.3 %collective-permute-start.21 = (bf16[144,1024]{1,0:T(8,128)(2,1)S(1)}, bf16[144,1024]{1,0:T(8,128)(2,1)S(1)}, u32[]{:S(2)}, u32[]{:S(2)}) collective-permute-start(bf16[144,1024]{1,0:T(8,128)(2,1)S(1)} %branch_1_fun.16), channel_id=1, source_target_pairs={{0,4},{2,6},{4,8},{6,10},{8,12},{10,14},{12,0},{14,2},{1,5},{3,7},... | collective-permute-start | bytes 884744 | tf_op jit(solution)/shard_map/cond/branch_1_fun/ppermute | solution.py:518
  92.9 25.2 %collective-permute-start.24 = (bf16[144,1024]{1,0:T(8,128)(2,1)S(1)}, bf16[144,1024]{1,0:T(8,128)(2,1)S(1)}, u32[]{:S(2)}, u32[]{:S(2)}) collective-permute-start(bf16[144,1024]{1,0:T(8,128)(2,1)S(1)} %branch_1_fun.16), channel_id=1, source_target_pairs={{0,8},{2,10},{4,12},{6,14},{8,0},{10,2},{12,4},{14,6},{1,9},{3,11}... | collective-permute-start | bytes 884744 | tf_op jit(solution)/shard_map/cond/branch_1_fun/ppermute | solution.py:518
  107.4 23.8 %collective-permute-start.23 = (bf16[288,1024]{1,0:T(8,128)(2,1)S(1)}, bf16[288,1024]{1,0:T(8,128)(2,1)S(1)}, u32[]{:S(2)}, u32[]{:S(2)}) collective-permute-start(bf16[288,1024]{1,0:T(8,128)(2,1)S(1)} %pad_maximum_fusion.3), channel_id=1, source_target_pairs={{0,2},{2,0},{4,6},{6,4},{8,10},{10,8},{12,14},{14,12},{1,3},{3,1},... | collective-permute-start | bytes 1769480 | tf_op jit(solution)/shard_map/cond/branch_1_fun/ppermute | solution.py:29
  108.6 19.4 %collective-permute-start.20 = (bf16[144,1024]{1,0:T(8,128)(2,1)S(1)}, bf16[144,1024]{1,0:T(8,128)(2,1)S(1)}, u32[]{:S(2)}, u32[]{:S(2)}) collective-permute-start(bf16[144,1024]{1,0:T(8,128)(2,1)S(1)} %branch_1_fun.16), channel_id=1, source_target_pairs={{0,2},{2,0},{4,6},{6,4},{8,10},{10,8},{12,14},{14,12},{1,3},{3,1},... | collective-permute-start | bytes 884744 | tf_op jit(solution)/shard_map/cond/branch_1_fun/ppermute | solution.py:29
  118.1 13.1 %copy-start.12 = (bf16[144,1024]{1,0:T(8,128)(2,1)}, bf16[144,1024]{1,0:T(8,128)(2,1)S(1)}, u32[]{:S(2)}) copy-start(bf16[144,1024]{1,0:T(8,128)(2,1)S(1)} %collective-permute-done.24) | copy-start | bytes 884740 | tf_op jit(solution)/shard_map/cond
  118.1 13.1 %collective-permute-start.25 = (bf16[144,1024]{1,0:T(8,128)(2,1)S(1)}, bf16[144,1024]{1,0:T(8,128)(2,1)S(1)}, u32[]{:S(2)}, u32[]{:S(2)}) collective-permute-start(bf16[144,1024]{1,0:T(8,128)(2,1)S(1)} %collective-permute-done.24), channel_id=1, source_target_pairs={{0,2},{2,0},{4,6},{6,4},{8,10},{10,8},{12,14},{14,12},{1,3},{3,1},... | collective-permute-start | bytes 884744 | tf_op jit(solution)/shard_map/cond/branch_1_fun/ppermute | solution.py:29
  131.2 0.7 copy-start.14
  131.9 0.8 copy-start.6
  132.7 6.8 %copy-start.13 = (bf16[144,1024]{1,0:T(8,128)(2,1)S(1)}, bf16[144,1024]{1,0:T(8,128)(2,1)}, u32[]{:S(2)}) copy-start(bf16[144,1024]{1,0:T(8,128)(2,1)} %get-tuple-element.216.refs_2_) | copy-start | bytes 884740 | tf_op jit(solution)/shard_map/cond
  132.7 6.7 %collective-permute-start.4 = (bf16[576,1024]{1,0:T(8,128)(2,1)}, bf16[576,1024]{1,0:T(8,128)(2,1)}, u32[]{:S(2)}, u32[]{:S(2)}) collective-permute-start(bf16[576,1024]{1,0:T(8,128)(2,1)} %get-tuple-element.214.refs_0_), channel_id=1, source_target_pairs={{0,1},{1,0},{2,3},{3,2},{4,5},{5,4},{6,7},{7,6},{8,9},{9,8},{10,11... | collective-permute-start | bytes 3538952 | tf_op jit(solution)/shard_map/cond/branch_1_fun/ppermute | solution.py:25
  132.7 6.7 %collective-permute-start.5 = (bf16[288,1024]{1,0:T(8,128)(2,1)}, bf16[288,1024]{1,0:T(8,128)(2,1)}, u32[]{:S(2)}, u32[]{:S(2)}) collective-permute-start(bf16[288,1024]{1,0:T(8,128)(2,1)} %get-tuple-element.215.refs_1_), channel_id=1, source_target_pairs={{0,1},{1,0},{2,3},{3,2},{4,5},{5,4},{6,7},{7,6},{8,9},{9,8},{10,11... | collective-permute-start | bytes 1769480 | tf_op jit(solution)/shard_map/cond/branch_1_fun/ppermute | solution.py:25
  133.2 6.2 %collective-permute-start.6 = (bf16[144,1024]{1,0:T(8,128)(2,1)}, bf16[144,1024]{1,0:T(8,128)(2,1)}, u32[]{:S(2)}, u32[]{:S(2)}) collective-permute-start(bf16[144,1024]{1,0:T(8,128)(2,1)} %get-tuple-element.216.refs_2_), channel_id=1, source_target_pairs={{0,1},{1,0},{2,3},{3,2},{4,5},{5,4},{6,7},{7,6},{8,9},{9,8},{10,11... | collective-permute-start | bytes 884744 | tf_op jit(solution)/shard_map/cond/branch_1_fun/ppermute | solution.py:25
  133.3 6.1 %collective-permute-start.7 = (bf16[144,1024]{1,0:T(8,128)(2,1)}, bf16[144,1024]{1,0:T(8,128)(2,1)}, u32[]{:S(2)}, u32[]{:S(2)}) collective-permute-start(bf16[144,1024]{1,0:T(8,128)(2,1)} %get-tuple-element.217.refs_3_), channel_id=1, source_target_pairs={{0,1},{1,0},{2,3},{3,2},{4,5},{5,4},{6,7},{7,6},{8,9},{9,8},{10,11... | collective-permute-start | bytes 884744 | tf_op jit(solution)/shard_map/cond/branch_1_fun/ppermute | solution.py:25
  133.7 5.7 %copy-start.4 = (bf16[576,1024]{1,0:T(8,128)(2,1)S(1)}, bf16[576,1024]{1,0:T(8,128)(2,1)}, u32[]{:S(2)}) copy-start(bf16[576,1024]{1,0:T(8,128)(2,1)} %get-tuple-element.214.refs_0_) | copy-start | bytes 3538948 | tf_op jit(solution)/shard_map/cond
  133.7 5.7 %copy-start.7 = (bf16[288,1024]{1,0:T(8,128)(2,1)S(1)}, bf16[288,1024]{1,0:T(8,128)(2,1)}, u32[]{:S(2)}) copy-start(bf16[288,1024]{1,0:T(8,128)(2,1)} %get-tuple-element.215.refs_1_) | copy-start | bytes 1769476 | tf_op jit(solution)/shard_map/cond
  133.8 5.8 %copy-start.15 = (bf16[144,1024]{1,0:T(8,128)(2,1)S(1)}, bf16[144,1024]{1,0:T(8,128)(2,1)}, u32[]{:S(2)}) copy-start(bf16[144,1024]{1,0:T(8,128)(2,1)} %get-tuple-element.217.refs_3_) | copy-start | bytes 884740 | tf_op jit(solution)/shard_map/cond
  138.9 0.6 copy-start
  148.0 1.3 collective-permute-start.31
  149.4 0.6 copy-start.22
  151.5 12.3 %collective-permute-start.32 = (bf16[32,1024]{1,0:T(8,128)(2,1)}, bf16[32,1024]{1,0:T(8,128)(2,1)S(1)}, u32[]{:S(2)}, u32[]{:S(2)}) collective-permute-start(bf16[32,1024]{1,0:T(8,128)(2,1)} %get-tuple-element.281), channel_id=1, source_target_pairs={{16,0},{17,1},{18,2},{19,3},{20,4},{21,5},{22,6},{23,7},{24,8},{25... | collective-permute-start | bytes 196616 | tf_op jit(solution)/shard_map/ppermute | solution.py:655
  152.8 11.0 %copy-start.21 = (bf16[32,1024]{1,0:T(8,128)(2,1)S(1)}, bf16[32,1024]{1,0:T(8,128)(2,1)}, u32[]{:S(2)}) copy-start(bf16[32,1024]{1,0:T(8,128)(2,1)} %get-tuple-element.282) | copy-start | bytes 196612
  163.8 1.7 %copy-start.2 = (bf16[768,2048]{1,0:T(8,128)(2,1)}, bf16[768,2048]{1,0:T(8,128)(2,1)S(1)}, u32[]{:S(2)}) copy-start(bf16[768,2048]{1,0:T(8,128)(2,1)S(1)} %get-tuple-element.288) | copy-start | bytes 9437188

commit v3 on v2

--- a/solution.py
+++ b/solution.py
@@ -217,7 +217,7 @@
 
 
 def weights_kernel(height, halves, each, trajs, wide, sources, me_ref, *refs):
-    units, (weights_ref, notes_ref, table_ref, sems) = refs[:-4], refs[-4:]
+    units, (weights_ref, notes_ref, table_ref, facts_ref, sems) = refs[:-5], refs[-5:]
     blocks = [(u, at) for u in units for at in range(0, u.shape[0], height)]
     count = len(blocks)
     per_half = (height - note_rows) // (2 * halves)
@@ -232,47 +232,44 @@
     for copy in copies:
         copy.wait()
     me = me_ref[0]
-    holders = []
-    for group, flip, far, near in sources:
+    ids = lax.broadcasted_iota(i32, (count, 1), 0)
+    places = lax.broadcasted_iota(i32, (note_rows, wide), 1)
+    holder_of = jnp.zeros((count, 1), f32)
+    for i, (group, flip, far, near) in enumerate(sources):
         place = lax.rem((lax.rem(me, group) ^ flip) + group - far, group)
-        holders.append((lax.div(me, group) * group + place) ^ near)
-    ids = lax.broadcasted_iota(i32, (count, 1), 0)
-    holder_of = jnp.zeros((count, 1), i32)
-    for i, holder in enumerate(holders):
-        holder_of = holder_of + jnp.where(ids == i, holder, 0)
+        holder = ((lax.div(me, group) * group + place) ^ near).astype(f32)
+        holder_of = holder_of + jnp.where(ids == i, holder, 0.0)
         notes = notes_ref[i].astype(f32)
         row = jnp.zeros((1, wide), f32)
         for k in range(each):
             gate = sum(notes[(1 + t) * each + k : (1 + t) * each + k + 1, :] for t in range(3))
             row = row + jnp.where(notes[k : k + 1, :] == me.astype(f32), gate, 0.0)
         table_ref[i : i + 1, :] = row
-    exact = lax.Precision.HIGHEST
-    slot = lax.broadcasted_iota(i32, (wide, longest), 0) - lax.broadcasted_iota(i32, (wide, longest), 1)
-    down = lax.broadcasted_iota(i32, (trajs, wide), 0)
-    across = lax.broadcasted_iota(i32, (trajs, wide), 1)
-    row_ids = lax.broadcasted_iota(i32, (1, total), 1)
-    offset_ids = lax.broadcasted_iota(i32, (longest, total), 0)
-    weights = jnp.zeros((1, total), f32)
-    for i, holder in enumerate(holders):
-        own_slots = dot(table_ref[...], jnp.where(slot == holder * longest, 1.0, 0.0), precision=exact)
-        notes = notes_ref[i].astype(f32)
-        at = 4 * each + halves
-        sent = jnp.where(holder_of.astype(f32) == notes[at : at + 1, :count], 1.0, 0.0)
-        by_traj = dot(own_slots, sent, tn_dims, precision=exact)
         for half in range(halves):
-            lengths = notes[4 * each + half : 4 * each + half + 1, :]
-            length = jnp.sum(jnp.where(across == down, lengths, 0.0), axis=1, keepdims=True).astype(i32)
-            start = jnp.sum(jnp.where(across < down, lengths, 0.0), axis=1, keepdims=True).astype(i32)
-            place = row_ids - (i * halves + half) * per_half
-            inside = (place >= start) & (place < start + length)
-            offset = place - jnp.sum(jnp.where(inside, start, 0), axis=0, keepdims=True)
-            spread = dot(by_traj[:, half * trajs : (half + 1) * trajs], jnp.where(inside, 1.0, 0.0), precision=exact)
-            weights = weights + jnp.sum(jnp.where(offset_ids == offset, spread, 0.0), axis=0, keepdims=True)
-    weights_ref[...] = weights
+            shards = pltpu.roll(notes, (trajs - half * trajs) % wide, 1) if half != 1 else notes
+            shards = jnp.where((places >= trajs) & (places < 2 * trajs), shards, 0.0)
+            shards = jnp.where(places == 2 * trajs, holder, shards)
+            facts = notes[4 * each + half : 4 * each + half + 1, :] + shards[4 * each + halves : 4 * each + halves + 1, :]
+            facts_ref[i * halves + half : i * halves + half + 1, :] = facts
+    facts = facts_ref[...]
+    down, across = [lax.broadcasted_iota(i32, (wide, wide), d) for d in (0, 1)]
+    starts = dot(facts, jnp.where((down < across) & (down < trajs), 1.0, 0.0))
+    row_ids = lax.broadcasted_iota(i32, (count * halves, total), 1)
+    of_row = lax.div(row_ids, per_half) == lax.broadcasted_iota(i32, (count * halves, total), 0)
+    of_row = jnp.where(of_row, 1.0, 0.0)
+    facts, starts = dot(facts, of_row, tn_dims), dot(starts, of_row, tn_dims)[:trajs]
+    place = lax.rem(lax.broadcasted_iota(i32, (1, total), 1), per_half).astype(f32)
+    inside = (place >= starts) & (place < starts + facts[:trajs])
+    offset = jnp.sum(jnp.where(inside, place - starts, 0.0), axis=0, keepdims=True)
+    shard = jnp.sum(jnp.where(inside, facts[trajs : 2 * trajs], 0.0), axis=0, keepdims=True)
+    slot = (facts[2 * trajs : 2 * trajs + 1] * longest + offset + 0.5).astype(i32)
+    chosen = jnp.where(lax.broadcasted_iota(i32, (wide, total), 0) == slot, 1.0, 0.0)
+    gates = dot(table_ref[...], chosen, precision=lax.Precision.HIGHEST)
+    weights_ref[...] = jnp.sum(jnp.where(holder_of == shard, gates, 0.0), axis=0, keepdims=True)
 
 
 def tile_copies(ref, held, tile, sems):
-    places = [pl.ds(start, tile) for start in range(0, held.shape[0], tile)]
+    places = [pl.ds(start, tile) for start in range(0, ref.shape[0], tile)]
     return [pltpu.make_async_copy(ref.at[p], held.at[p], sems.at[i]) for i, p in enumerate(places)]
 
 
@@ -297,16 +294,32 @@
     return (old.astype(f32) - (step_size * step) * dot(change, rows)).astype(bf16)
 
 
-def learner_kernel(parts, height, features, hidden, tile, part_ref, weight_ref, *refs):
-    units, (up_ref, down_ref, new_up_ref, new_down_ref, inputs, grads, up, down, new_up, new_down) = refs[:-13], refs[-13:-3]
-    row_sems, sems, out_sems = refs[-3:]
-    in_copies, grad_copies = gathered_copies(part_ref[0], parts, height, units, inputs, grads, row_sems)
-    up_copies = tile_copies(up_ref, up, tile, sems.at[0])
-    down_copies = tile_copies(down_ref, down, tile, sems.at[1])
-    up_outs = tile_copies(new_up, new_up_ref, tile, out_sems.at[0])
-    down_outs = tile_copies(new_down, new_down_ref, tile, out_sems.at[1])
+def cut_kernel(go_ref, up_ref, down_ref, first_ref, second_ref, held, sems):
+    rows, most = up_ref.shape[0], first_ref.shape[0]
+
+    @pl.when(go_ref[0] == 0)
+    def _():
+        moves = [
+            (up_ref, pl.ds(0, rows), first_ref.at[pl.ds(0, rows)]),
+            (down_ref.at[pl.ds(0, most - rows)], pl.ds(rows, most - rows), first_ref.at[pl.ds(rows, most - rows)]),
+            (down_ref.at[pl.ds(most - rows, 2 * rows - most)], pl.ds(most, 2 * rows - most), second_ref),
+        ]
+        ins = [pltpu.make_async_copy(a, held.at[p], sems.at[0, i]) for i, (a, p, _) in enumerate(moves)]
+        outs = [pltpu.make_async_copy(held.at[p], b, sems.at[1, i]) for i, (_, p, b) in enumerate(moves)]
+        start_all(ins)
+        for copy, out in zip(ins, outs):
+            copy.wait()
+            out.start()
+        wait_all(outs)
+
+
+def update_rows(features, hidden, tile, weight, in_copies, grad_copies, up_from, down_from, up_to, down_to, space):
+    inputs, grads, up, down, new_up, new_down, sems, out_sems = space
+    up_copies = tile_copies(up_from, up, tile, sems.at[0])
+    down_copies = tile_copies(down_from, down, tile, sems.at[1])
+    up_outs = tile_copies(new_up, up_to, tile, out_sems.at[0])
+    down_outs = tile_copies(new_down, down_to, tile, out_sems.at[1])
     start_all(up_copies[:1], in_copies, down_copies[:1], grad_copies, up_copies[1:], down_copies[1:])
-    weight = weight_ref[...]
     for i in range(len(up_copies)):
         here = pl.ds(i * tile, tile)
         up_copies[i].wait()
@@ -324,51 +337,31 @@
     wait_all(up_outs + down_outs)
 
 
-def forward_kernel(parts, height, features, tile, part_ref, weight_ref, *refs):
-    units, (up_ref, inputs, grads, activated, slopes, up, row_sems, sems) = refs[:-8], refs[-8:]
-    in_copies, grad_copies = gathered_copies(part_ref[0], parts, height, units, inputs, grads, row_sems)
-    up_copies = tile_copies(up_ref, up, tile, sems)
-    start_all(up_copies[:1], in_copies, up_copies[1:], grad_copies)
-    wait_all(in_copies)
-    for i, copy in enumerate(up_copies):
-        here = pl.ds(i * tile, tile)
-        copy.wait()
-        activated[here, :], slopes[here, :] = activation(features, up[here, :], inputs[...], weight_ref[...])
-    wait_all(grad_copies)
-
-
-def late_kernel(features, hidden, tile, go_ref, *refs):
-    refs, (up, down, inputs, grads, activated, slopes, new_up, new_down, row_sems, sems, out_sems) = refs[:-11], refs[-11:]
-    up_ref, down_ref, inputs_ref, grads_ref, activated_ref, slopes_ref, _, _, new_up_ref, new_down_ref = refs
+def learner_kernel(parts, height, features, hidden, tile, part_ref, weight_ref, *refs):
+    units, (up_ref, down_ref, new_up_ref, new_down_ref), row_sems, space = refs[:-13], refs[-13:-9], refs[-9], refs[-8:]
+    copies = gathered_copies(part_ref[0], parts, height, units, space[0], space[1], row_sems)
+    rows = (up_ref, down_ref, new_up_ref, new_down_ref)
+    update_rows(features, hidden, tile, weight_ref[...], *copies, *rows, space)
+
+
+def assemble_kernel(parts, height, part_ref, *refs):
+    units, (inputs_ref, grads_ref, sems) = refs[:-3], refs[-3:]
+    in_copies, grad_copies = gathered_copies(part_ref[0], parts, height, units, inputs_ref, grads_ref, sems)
+    start_all(in_copies, grad_copies)
+    wait_all(in_copies + grad_copies)
+
+
+def late_kernel(features, hidden, tile, places, go_ref, weight_ref, *refs):
+    inputs_ref, grads_ref, up_ref, down_ref, _, _, new_up_ref, new_down_ref, row_sems, *space = refs
+    count, to, up_at, down_at = places
 
     @pl.when(go_ref[0] == 1)
     def _():
-        up_copies = tile_copies(up_ref, up, tile, sems.at[0])
-        down_copies = tile_copies(down_ref, down, tile, sems.at[1])
-        active_copies = tile_copies(activated_ref, activated, tile, sems.at[2])
-        slope_copies = tile_copies(slopes_ref, slopes, tile, sems.at[3])
-        grad_copy = pltpu.make_async_copy(grads_ref, grads, row_sems.at[0])
-        in_copy = pltpu.make_async_copy(inputs_ref, inputs, row_sems.at[1])
-        up_outs = tile_copies(new_up, new_up_ref, tile, out_sems.at[0])
-        down_outs = tile_copies(new_down, new_down_ref, tile, out_sems.at[1])
-        start_all([grad_copy], down_copies[:1], slope_copies[:1], active_copies[:1], [in_copy])
-        start_all(up_copies[:1], down_copies[1:], slope_copies[1:], active_copies[1:], up_copies[1:])
-        grad_copy.wait()
-        for i in range(len(up_copies)):
-            here = pl.ds(i * tile, tile)
-            down_copies[i].wait()
-            slope_copies[i].wait()
-            hidden_grad = dot(down[here, :], grads[...], nt_dims) * hidden ** (-0.5)
-            pre_grad = (hidden_grad * slopes[here, :]).astype(bf16)
-            active_copies[i].wait()
-            new_down[here, :] = new_tile(down[here, :], hidden ** (-0.5), activated[here, :], grads[...])
-            down_outs[i].start()
-            if i == 0:
-                in_copy.wait()
-            up_copies[i].wait()
-            new_up[here, :] = new_tile(up[here, :], features ** (-0.5), pre_grad, inputs[...])
-            up_outs[i].start()
-        wait_all(up_outs + down_outs)
+        in_copies = [pltpu.make_async_copy(inputs_ref, space[0], row_sems.at[0])]
+        grad_copies = [pltpu.make_async_copy(grads_ref, space[1], row_sems.at[1])]
+        rows = [up_ref.at[pl.ds(up_at, count)], down_ref.at[pl.ds(down_at, count)]]
+        rows = rows + [ref.at[pl.ds(to, count)] for ref in (new_up_ref, new_down_ref)]
+        update_rows(features, hidden, tile, weight_ref[...], in_copies, grad_copies, *rows, space)
 
 
 def join_kernel(parts, row_count, part_ref, *refs):
@@ -453,9 +446,20 @@
     )(part_ref, routes, gates, decode_states, traj_inputs[0], traj_cotangents[0])
 
     crossed_rows = flipped(own_rows, "sect", 1)
-    up_sent, down_sent, crossed_rows = lax.optimization_barrier((up_here, down_here, crossed_rows))
-    up_there = lax.ppermute(up_sent, "sect", [(1, 0)])
-    down_there = lax.ppermute(down_sent, "sect", [(1, 0)])
+    up_sent, down_sent, _ = lax.optimization_barrier((up_here, down_here, own_rows))
+    cut = hidden_here + 2 * tile
+    pieces = pl.pallas_call(
+        cut_kernel,
+        out_shape=[jax.ShapeDtypeStruct((rows, features), bf16) for rows in (cut, tile)],
+        in_specs=[smem] + [stays] * 2,
+        out_specs=[stays] * 2,
+        scratch_shapes=[pltpu.VMEM((2 * hidden_here, features), bf16), pltpu.SemaphoreType.DMA((2, 3))],
+        compiler_params=fits(60),
+        cost_estimate=costs(1, 1),
+    )(go, up_sent, down_sent)
+    first_piece, second_piece, crossed_rows = lax.optimization_barrier((*pieces, crossed_rows))
+    first_there = lax.ppermute(first_piece, "sect", [(1, 0)])
+    second_there = lax.ppermute(second_piece, "sect", [(1, 0)])
 
     gain = norm_gain.reshape(1, features)
     def expert_forward(arrived, up_mat, down_mat):
@@ -513,16 +517,21 @@
         far = group // 2
         shifts = sorted(range(1, far), key=lambda s: (min(s, far - s), s))
 
-        def along(s):
+        def along(array, s):
             pairs = [(i, i // group * group + (i + 2 * s) % group) for i in range(experts)]
-            return lax.ppermute(unit, "exp", pairs)
-
-        near = jnp.concatenate([along(s) for s in shifts[:-1]])
-        sides = [flipped(unit, "exp", 1), flipped(near, "exp", 1)]
-        last = along(shifts[-1])
-        units = [jnp.concatenate([unit, sides[0], near]), sides[1], last, flipped(last, "exp", 1)]
-        places = [(0, 0), (1, 0)] + [(flip, s) for flip in range(2) for s in shifts[:-1]]
-        places = places + [(0, shifts[-1]), (1, shifts[-1])]
+            return lax.ppermute(array, "exp", pairs)
+
+        side = flipped(unit, "exp", 1)
+        near = [along(unit, s) for s in shifts[:-1]]
+        unit, side, *near = lax.optimization_barrier((unit, side, *near))
+        last = along(unit, shifts[-1])
+        sides = [flipped(n, "exp", 1) for n in near]
+        units = [
+            jnp.concatenate([unit, side, *near]),
+            jnp.concatenate(sides),
+            jnp.concatenate([last, flipped(last, "exp", 1)]),
+        ]
+        places = [(0, 0), (1, 0)] + [(f, s) for f in range(2) for s in shifts[:-1]] + [(f, shifts[-1]) for f in range(2)]
         sources = [(group, flip, 2 * s, o) for flip, s in places for o in others]
         return units, sources
 
@@ -539,6 +548,7 @@
             scratch_shapes=[
                 pltpu.VMEM((experts, note_rows, wide), bf16),
                 pltpu.VMEM((experts, wide), f32),
+                pltpu.VMEM((2 * experts, wide), f32),
                 pltpu.SemaphoreType.DMA((experts,)),
             ],
             compiler_params=fits(16),
@@ -548,13 +558,14 @@
 
     rows_like = jax.ShapeDtypeStruct((gathered, features), bf16)
     weight_like = jax.ShapeDtypeStruct((hidden_here, features), bf16)
-    active_like = jax.ShapeDtypeStruct((hidden_here, gathered), bf16)
-    slopes_like = jax.ShapeDtypeStruct((hidden_here, gathered), f32)
-    row_space = [pltpu.VMEM(rows_like.shape, bf16)] * 2
-    weight_space = pltpu.VMEM(weight_like.shape, bf16)
+    weights_like = jax.ShapeDtypeStruct((1, gathered), f32)
 
     def sems_of(*shape):
         return pltpu.SemaphoreType.DMA(shape)
+
+    def update_space(rows):
+        held = [pltpu.VMEM((gathered, features), bf16)] * 2 + [pltpu.VMEM((rows, features), bf16)] * 4
+        return held + [sems_of(2, rows // tile)] * 2
 
     def update(units, weights, up_mat, down_mat):
         return pl.pallas_call(
@@ -562,37 +573,26 @@
             out_shape=[weight_like] * 2,
             in_specs=[smem, vmem] + [anywhere] * (len(units) + 2),
             out_specs=[anywhere] * 2,
-            scratch_shapes=row_space + [weight_space] * 4 + [sems_of(2 * parts * experts), sems_of(2, 3), sems_of(2, 3)],
+            scratch_shapes=[sems_of(2 * parts * experts)] + update_space(hidden_here),
             compiler_params=fits(56),
             cost_estimate=costs(1, 1),
         )(part_ref, weights, *units, up_mat, down_mat)
 
-    def update_forward(units, weights):
+    def update_late(count, places, piece, new_up, new_down):
         return pl.pallas_call(
-            functools.partial(forward_kernel, parts, height, features, tile),
-            out_shape=[rows_like, rows_like, active_like, slopes_like],
-            in_specs=[smem, vmem] + [anywhere] * (len(units) + 1),
-            scratch_shapes=[weight_space, sems_of(2 * parts * experts), sems_of(3)],
-            compiler_params=fits(56),
-            cost_estimate=costs(1, 1),
-        )(part_ref, weights, *units, up_there)
-
-    def update_late(known, new_up, new_down):
-        space = [weight_space] * 2 + row_space + [pltpu.VMEM(a.shape, a.dtype) for a in (active_like, slopes_like)]
-        return pl.pallas_call(
-            functools.partial(late_kernel, features, hidden, tile),
+            functools.partial(late_kernel, features, hidden, tile, (count, *places)),
             out_shape=[weight_like] * 2,
-            in_specs=[smem] + [stays] * 8,
+            in_specs=[smem, vmem] + [stays] * 6,
             out_specs=[anywhere] * 2,
-            scratch_shapes=space + [weight_space] * 2 + [sems_of(2), sems_of(4, 3), sems_of(2, 3)],
-            input_output_aliases={7: 0, 8: 1},
+            scratch_shapes=[sems_of(2)] + update_space(count),
+            input_output_aliases={6: 0, 7: 1},
             compiler_params=fits(60),
             cost_estimate=costs(1, 1),
-        )(go, up_there, down_there, *known, new_up, new_down)
+        )(go, weights, inputs, grads, first_there, piece, new_up, new_down)
 
     final_like = jax.ShapeDtypeStruct((stacked, lanes), bf16)
     block_rows = height * max(1, experts // line)
-    gather_like = [jax.ShapeDtypeStruct((block_rows * n, share), bf16) for n in (line // 2, line // 2 - 2, 1, 1)]
+    gather_like = [jax.ShapeDtypeStruct((block_rows * n, share), bf16) for n in (line // 2, line // 2 - 2, 2)]
 
     sources = []
 
@@ -634,15 +634,24 @@
     states, payload, *rows = lax.cond(is_rollout, third_rollout, third_learner)
 
     def fourth_rollout():
-        return unset(final_like) + tuple(update_forward(*with_parts(rows, sources[0])))
+        units, weights = with_parts(rows, sources[0])
+        whole = pl.pallas_call(
+            functools.partial(assemble_kernel, parts, height),
+            out_shape=[rows_like] * 2,
+            in_specs=[smem] + [anywhere] * len(units),
+            scratch_shapes=[sems_of(2 * parts * experts)],
+            compiler_params=fits(32),
+            cost_estimate=costs(1, 1),
+        )(part_ref, *units)
+        return unset(final_like) + tuple(whole) + (weights,)
 
     def fourth_learner():
         now, sent = states, payload
         for step in range(half_steps + 1, steps):
             now, sent = decode_step(step, now, sent, new_up, new_down)
-        return (sent,) + unset(rows_like, rows_like, active_like, slopes_like)
-
-    mine, *known = lax.cond(is_rollout, fourth_rollout, fourth_learner)
+        return (sent,) + unset(rows_like, rows_like, weights_like)
+
+    mine, inputs, grads, weights = lax.cond(is_rollout, fourth_rollout, fourth_learner)
 
     pieces = [mine] + [shifted(mine, "dp", j) for j in range(1, parts)]
     left, right = pl.pallas_call(
@@ -652,8 +661,10 @@
         scratch_shapes=[pltpu.VMEM((row_count, features), bf16)],
         cost_estimate=costs(1, 1),
     )(part_ref, *pieces)
+    new_up, new_down = update_late(2 * tile, (0, 0, hidden_here), first_there, new_up, new_down)
+    left, new_up = lax.optimization_barrier((left, new_up))
     delivered = lax.ppermute(left, "sect", [(1, 0)])
-    new_up, new_down = update_late(known, new_up, new_down)
+    new_up, new_down = update_late(tile, (2 * tile, 2 * tile, 0), second_there, new_up, new_down)
     final_states = jnp.where(is_rollout, delivered, right)
     return final_states, new_up[None, None], new_down[None, None]
 

time: 168 us -> 160 us (0.952); the launches traced: 165 us -> 159 us
  Pallas kernels: 41.6 us -> 33.8 us
  waiting for transfers between devices: 60.3 us -> 67.4 us
  starting transfers between devices: 27.8 us -> 24.5 us
  local copies, waits for them, and re-layouts: 7.07 us -> 4.2 us
    ppermute x5, waiting for transfers between devices: 22.4 us -> 28.3 us  [the longest x3 24.1 us: along(): return lax.ppermute(array, 'exp', pairs)]
    ppermute x4 -> x5, waiting for transfers between devices: 13.3 us -> 7.72 us  [flipped(): lax.ppermute(array, axis, [(i, i ^ bit) for i in range(lax.axis_size(axis...]
    ppermute x1, starting transfers between devices: 6.21 us -> 1.28 us  [on_device(): states_there = lax.ppermute(states, 'sect', [(0, 1)])]
    ppermute x1, waiting for transfers between devices: 0.01 us -> 4.08 us  [on_device(): delivered = lax.ppermute(left, 'sect', [(1, 0)])]
    pallas_call x1, Pallas kernels: 5.11 us -> 1.5 us  [with_parts(): pl.pallas_call(functools.partial(weights_kernel, height, 2, learner_route...]
    pallas_call x2, Pallas kernels: 10.2 us -> 6.64 us  [expert_forward(): pl.pallas_call(functools.partial(expert_kernel, parts, slots, capacity, f...]
    ppermute x9 -> x8, waiting for transfers between devices: 6.64 us -> 9.29 us  [shifted(): lax.ppermute(array, axis, [(i, (i + by) % size) for i in range(size)])]
    ppermute x4 -> x5, starting transfers between devices: 6.61 us -> 8.06 us  [flipped(): lax.ppermute(array, axis, [(i, i ^ bit) for i in range(lax.axis_size(axis...]
  transfers between devices with their start and end apart: 22 -> 22, of which waited for: 14 -> 17; matrix products, arithmetic and copies ran while one was open for 3% -> 3% of each run, Pallas kernels for 24% -> 20%
where the time goes in v3:
time: 160 us; the launch traced here: 159 us
  waiting for transfers between devices  67.4 us (42%)
  Pallas kernels  33.8 us (21%)
  blocking collectives  25.1 us (16%)
  starting transfers between devices  24.5 us (15%)
  local copies, waits for them, and re-layouts  4.2 us (3%)
  other arithmetic  3.27 us (2%)
    all_to_all x2, blocking collectives, decode_step(): lax.all_to_all(payload, 'exp', split_axis=0, concat_axis=0, tiled=True)  25.1 us
    ppermute x3, waiting for transfers between devices, along(): return lax.ppermute(array, 'exp', pairs)  24.1 us
    all_to_all x2, waiting for transfers between devices, decode_step(): lax.all_to_all(summed, 'exp', split_axis=0, concat_axis=0, tiled=True)  15.2 us
    pallas_call x2, Pallas kernels, update_late(): pl.pallas_call(functools.partial(late_kernel, features, hidden, tile, (co...  14.7 us
    ppermute x8, waiting for transfers between devices, shifted(): lax.ppermute(array, axis, [(i, (i + by) % size) for i in range(size)])  9.29 us
    ppermute x5, starting transfers between devices, flipped(): lax.ppermute(array, axis, [(i, i ^ bit) for i in range(lax.axis_size(axis...  8.06 us
    ppermute x5, waiting for transfers between devices, flipped(): lax.ppermute(array, axis, [(i, i ^ bit) for i in range(lax.axis_size(axis...  7.72 us
    all_to_all x2, starting transfers between devices, decode_step(): lax.all_to_all(summed, 'exp', split_axis=0, concat_axis=0, tiled=True)  6.78 us
  transfers between devices with their start and end apart: 22, of which 17 were waited for; matrix products, arithmetic and copies ran while one was open for 3% of the time, Pallas kernels for 20%

profile of v3, /device:TPU:0, one launch (start us, length us, event | category | flops | bytes accessed | tf_op | source)
XLA Modules:
  0.0 159.2 jit_solution(4745884379160668930)
XLA Ops:
  0.6 2.5 %shard_map.139 = (s32[4,2,128]{2,1,0:T(2,128)S(1)}, f32[8,128]{1,0:T(8,128)S(1)}, f32[128,256]{1,0:T(8,128)}, bf16[384,256]{1,0:T(8,128)(2,1)}, bf16[64,1024]{1,0:T(8,128)(2,1)S(1)}) custom-call(s32[1]{0:T(128)} %bitcast.24.part_ref, s32[8,32]{1,0:T(8,128)} %bitcast.66, f32[8,32]{1,0:T(8,128)} %bitcast.67, bf16[32,2048]{1,0:T(8,128)(2,1)} %all_rows_ref.1, ...), custom_call_target="tpu_custom_call" | custom-call | flops 1 | bytes 1 | tf_op jit(solution)/shard_map/pallas_call | solution.py:433
  3.2 3.0 %collective-permute-start.28 = (bf16[64,1024]{1,0:T(8,128)(2,1)S(1)}, bf16[64,1024]{1,0:T(8,128)(2,1)}, u32[]{:S(2)}, u32[]{:S(2)}) collective-permute-start(bf16[64,1024]{1,0:T(8,128)(2,1)S(1)} %get-tuple-element.258), channel_id=1, source_target_pairs={{0,16},{16,0},{1,17},{17,1},{2,18},{18,2},{3,19},{19,3},{4,20},{20... | collective-permute-start | bytes 393224 | tf_op jit(solution)/shard_map/ppermute | solution.py:29
  6.2 0.0 copy-start.14
  6.2 0.0 copy-start.15
  6.2 0.1 shard_map.140
  6.3 3.5 %collective-permute-done.28 = bf16[64,1024]{1,0:T(8,128)(2,1)} collective-permute-done((bf16[64,1024]{1,0:T(8,128)(2,1)S(1)}, bf16[64,1024]{1,0:T(8,128)(2,1)}, u32[]{:S(2)}, u32[]{:S(2)}) %collective-permute-start.28) | collective-permute-done | bytes 131104 | tf_op jit(solution)/shard_map/ppermute | solution.py:29
  9.8 1.3 collective-permute-start.31
  11.1 1.3 collective-permute-start.33
  12.4 34.0 %conditional.4 = (f32[128,256]{1,0:T(8,128)}, bf16[384,256]{1,0:T(8,128)(2,1)}, bf16[576,1024]{1,0:T(8,128)(2,1)}, bf16[288,1024]{1,0:T(8,128)(2,1)}, bf16[288,1024]{1,0:T(8,128)(2,1)}) conditional(s32[]{:T(128)} %convert_element_type.43, (s32[128,2]{0,1:T(2,128)S(1)}, f32[128,2]{0,1:T(2,128)S(1)}, s32[1,2,4]{2,1,0:T(2,128)S(1)}, ...), branch_computations={%region_0.0_spmd, %region_1.0_spmd} | conditional | flops 7077889 | bytes 12976449 | solution.py:607
  12.5 13.9 %all_to_all.64 = bf16[8,48,256]{2,1,0:T(8,128)(2,1)S(1)} all-to-all(bf16[8,48,256]{2,1,0:T(8,128)(2,1)} %bitcast.3), channel_id=1, replica_groups=mesh['sect'=2,'exp'=8,'dp'=2] {'exp'}, dimensions={0} | all-to-all | bytes 393216 | tf_op jit(solution)/shard_map/cond/branch_1_fun/all_to_all | solution.py:484
  26.3 1.4 collective-permute-done.13.refs_1_
  27.8 3.3 %branch_1_fun.10 = (bf16[384,256]{1,0:T(8,128)(2,1)S(1)}, bf16[384,256]{1,0:T(8,128)(2,1)S(1)}) custom-call(s32[1]{0:T(128)} %get-tuple-element.135.part_ref, f32[1,2048]{1,0:T(1,128)S(1)} %get-tuple-element.136.gain_ref, bf16[384,256]{1,0:T(8,128)(2,1)S(1)} %bitcast.47, bf16[384,256]{1,0:T(8,128)(2,1)S(1)} %collective-permute-done.13.refs_1_, ...), custom_call_target="tpu_custom_call" | custom-call | flops 1 | bytes 1 | tf_op jit(solution)/shard_map/cond/branch_1_fun/pallas_call | solution.py:466
  31.1 0.2 collective-permute-start.14
  31.3 1.3 collective-permute-done.14
  32.6 0.7 add_convert_fusion
  33.3 3.4 %all-to-all-start.1 = ((bf16[8,48,256]{2,1,0:T(8,128)(2,1)}), bf16[8,48,256]{2,1,0:T(8,128)(2,1)S(1)}, u32[]{:S(2)}, u32[]{:S(2)}) async-start(bf16[8,48,256]{2,1,0:T(8,128)(2,1)} %bitcast.5), calls=%async_computation.1 | async-start | bytes 393216 | tf_op jit(solution)/shard_map/cond/branch_1_fun/all_to_all | solution.py:489
  36.8 0.9 copy.59.states_ref
  37.7 7.6 %all-to-all-done.1 = bf16[8,48,256]{2,1,0:T(8,128)(2,1)S(1)} async-done(((bf16[8,48,256]{2,1,0:T(8,128)(2,1)}), bf16[8,48,256]{2,1,0:T(8,128)(2,1)S(1)}, u32[]{:S(2)}, u32[]{:S(2)}) %all-to-all-start.1) | async-done | bytes 196640 | tf_op jit(solution)/shard_map/cond/branch_1_fun/all_to_all | solution.py:489
  45.2 1.2 branch_1_fun.11
  46.5 31.1 %conditional.5 = (f32[128,256]{1,0:T(8,128)}, bf16[768,2048]{1,0:T(8,128)(2,1)}, bf16[768,2048]{1,0:T(8,128)(2,1)}) conditional(s32[]{:T(128)} %convert_element_type.43, (s32[]{:T(128)}, bf16[576,1024]{1,0:T(8,128)(2,1)}, bf16[288,1024]{1,0:T(8,128)(2,1)}, bf16[288,1024]{1,0:T(8,128)(2,1)}, s32[1]{0:T(128)}, ...), branch_computations={%region_2.0_spmd, %region_3.0_spmd} | conditional | flops 393219 | bytes 18882816 | solution.py:619
  46.5 11.2 %all_to_all.65 = bf16[8,48,256]{2,1,0:T(8,128)(2,1)S(1)} all-to-all(bf16[8,48,256]{2,1,0:T(8,128)(2,1)} %bitcast.8), channel_id=1, replica_groups=mesh['sect'=2,'exp'=8,'dp'=2] {'exp'}, dimensions={0} | all-to-all | bytes 393216 | tf_op jit(solution)/shard_map/cond/branch_1_fun/all_to_all | solution.py:484
  57.7 1.4 collective-permute-done.15.refs_1_
  59.1 3.3 %branch_1_fun.13 = (bf16[384,256]{1,0:T(8,128)(2,1)S(1)}, bf16[384,256]{1,0:T(8,128)(2,1)S(1)}) custom-call(s32[1]{0:T(128)} %get-tuple-element.160.part_ref, f32[1,2048]{1,0:T(1,128)S(1)} %get-tuple-element.161.gain_ref, bf16[384,256]{1,0:T(8,128)(2,1)S(1)} %bitcast.49, bf16[384,256]{1,0:T(8,128)(2,1)S(1)} %collective-permute-done.15.refs_1_, ...), custom_call_target="tpu_custom_call" | custom-call | flops 1 | bytes 1 | tf_op jit(solution)/shard_map/cond/branch_1_fun/pallas_call | solution.py:466
  62.5 0.2 collective-permute-start.16
  62.7 1.3 collective-permute-done.16
  64.0 0.7 add_convert_fusion.1
  64.7 3.4 %all-to-all-start.3 = ((bf16[8,48,256]{2,1,0:T(8,128)(2,1)}), bf16[8,48,256]{2,1,0:T(8,128)(2,1)S(1)}, u32[]{:S(2)}, u32[]{:S(2)}) async-start(bf16[8,48,256]{2,1,0:T(8,128)(2,1)} %bitcast.10), calls=%async_computation.3 | async-start | bytes 393216 | tf_op jit(solution)/shard_map/cond/branch_1_fun/all_to_all | solution.py:489
  68.1 0.9 copy.60.states_ref
  69.0 7.6 %all-to-all-done.3 = bf16[8,48,256]{2,1,0:T(8,128)(2,1)S(1)} async-done(((bf16[8,48,256]{2,1,0:T(8,128)(2,1)}), bf16[8,48,256]{2,1,0:T(8,128)(2,1)S(1)}, u32[]{:S(2)}, u32[]{:S(2)}) %all-to-all-start.3) | async-done | bytes 196640 | tf_op jit(solution)/shard_map/cond/branch_1_fun/all_to_all | solution.py:489
  76.6 1.0 branch_1_fun.14
  77.5 1.3 collective-permute-start.29
  78.8 2.8 %collective-permute-done.29 = f32[128,256]{1,0:T(8,128)S(1)} collective-permute-done((f32[128,256]{1,0:T(8,128)}, f32[128,256]{1,0:T(8,128)S(1)}, u32[]{:S(2)}, u32[]{:S(2)}) %collective-permute-start.29) | collective-permute-done | bytes 131104 | tf_op jit(solution)/shard_map/ppermute | solution.py:620
  81.6 39.8 %conditional.6 = (f32[128,256]{1,0:T(8,128)S(1)}, bf16[384,256]{1,0:T(8,128)(2,1)}, bf16[576,1024]{1,0:T(8,128)(2,1)}, bf16[288,1024]{1,0:T(8,128)(2,1)S(1)}, bf16[288,1024]{1,0:T(8,128)(2,1)S(1)}) conditional(s32[]{:T(128)} %convert_element_type.43, (s32[4,2,128]{2,1,0:T(2,128)S(1)}, f32[128,256]{1,0:T(8,128)S(1)}, s32[1]{0:T(128)}, ...), branch_computations={%region_4.0_spmd, %region_5.0_spmd} | conditional | flops 7077889 | bytes 13238593 | solution.py:634
  81.7 1.1 branch_1_fun.16
  82.7 3.3 %collective-permute-start.21 = (bf16[144,1024]{1,0:T(8,128)(2,1)S(1)}, bf16[144,1024]{1,0:T(8,128)(2,1)S(1)}, u32[]{:S(2)}, u32[]{:S(2)}) collective-permute-start(bf16[144,1024]{1,0:T(8,128)(2,1)S(1)} %branch_1_fun.16), channel_id=1, source_target_pairs={{0,12},{2,14},{4,0},{6,2},{8,4},{10,6},{12,8},{14,10},{1,13},{3,15... | collective-permute-start | bytes 884744 | tf_op jit(solution)/shard_map/cond/branch_1_fun/ppermute | solution.py:522
  86.0 0.0 collective-permute-start.20
  86.0 1.5 collective-permute-start.19
  87.5 5.9 %collective-permute-done.21 = bf16[144,1024]{1,0:T(8,128)(2,1)S(1)} collective-permute-done((bf16[144,1024]{1,0:T(8,128)(2,1)S(1)}, bf16[144,1024]{1,0:T(8,128)(2,1)S(1)}, u32[]{:S(2)}, u32[]{:S(2)}) %collective-permute-start.21) | collective-permute-done | bytes 294944 | tf_op jit(solution)/shard_map/cond/branch_1_fun/ppermute | solution.py:522
  93.5 5.3 %collective-permute-done.20 = bf16[144,1024]{1,0:T(8,128)(2,1)S(1)} collective-permute-done((bf16[144,1024]{1,0:T(8,128)(2,1)S(1)}, bf16[144,1024]{1,0:T(8,128)(2,1)S(1)}, u32[]{:S(2)}, u32[]{:S(2)}) %collective-permute-start.20) | collective-permute-done | bytes 294944 | tf_op jit(solution)/shard_map/cond/branch_1_fun/ppermute | solution.py:522
  98.8 0.0 collective-permute-done.19
  98.8 1.6 %collective-permute-start.22 = (bf16[144,1024]{1,0:T(8,128)(2,1)S(1)}, bf16[144,1024]{1,0:T(8,128)(2,1)S(1)}, u32[]{:S(2)}, u32[]{:S(2)}) collective-permute-start(bf16[144,1024]{1,0:T(8,128)(2,1)S(1)} %collective-permute-done.20), channel_id=1, source_target_pairs={{0,2},{2,0},{4,6},{6,4},{8,10},{10,8},{12,14},{14,12},{1,3},{3,1},... | collective-permute-start | bytes 884744 | tf_op jit(solution)/shard_map/cond/branch_1_fun/ppermute | solution.py:29
  100.5 0.4 collective-permute-start.23
  100.9 12.8 %collective-permute-done.24 = bf16[144,1024]{1,0:T(8,128)(2,1)S(1)} collective-permute-done((bf16[144,1024]{1,0:T(8,128)(2,1)S(1)}, bf16[144,1024]{1,0:T(8,128)(2,1)S(1)}, u32[]{:S(2)}, u32[]{:S(2)}) %collective-permute-start.24) | collective-permute-done | bytes 294944 | tf_op jit(solution)/shard_map/cond/branch_1_fun/ppermute | solution.py:522
  113.6 1.5 collective-permute-start.25
  115.2 0.9 copy.40
  116.1 1.1 pad_maximum_fusion.3
  117.2 4.2 %collective-permute-done.25 = bf16[144,1024]{1,0:T(8,128)(2,1)S(1)} collective-permute-done((bf16[144,1024]{1,0:T(8,128)(2,1)S(1)}, bf16[144,1024]{1,0:T(8,128)(2,1)S(1)}, u32[]{:S(2)}, u32[]{:S(2)}) %collective-permute-start.25) | collective-permute-done | bytes 294944 | tf_op jit(solution)/shard_map/cond/branch_1_fun/ppermute | solution.py:29
  121.5 9.2 %conditional.7 = (bf16[128,256]{1,0:T(8,128)(2,1)S(1)}, bf16[512,2048]{1,0:T(8,128)(2,1)}, bf16[512,2048]{1,0:T(8,128)(2,1)}, f32[1,512]{1,0:T(1,128)S(1)}) conditional(s32[]{:T(128)} %convert_element_type.43, (bf16[384,256]{1,0:T(8,128)(2,1)}, s32[1]{0:T(128)}, f32[1,2048]{1,0:T(1,128)S(1)}, bf16[768,2048]{1,0:T(8,128)(2,1)}, ...), branch_computations={%region_6.0_spmd, %region_7.0_spmd} | conditional | flops 393219 | bytes 14155987 | solution.py:654
  121.5 0.8 copy-done.2
  122.3 0.5 collective-permute-start.4
  122.8 1.5 branch_1_fun.19
  124.3 2.1 %collective-permute-done.4.refs_4_ = bf16[288,1024]{1,0:T(8,128)(2,1)S(1)} collective-permute-done((bf16[288,1024]{1,0:T(8,128)(2,1)S(1)}, bf16[288,1024]{1,0:T(8,128)(2,1)S(1)}, u32[]{:S(2)}, u32[]{:S(2)}) %collective-permute-start.4) | collective-permute-done | bytes 589856 | tf_op jit(solution)/shard_map/cond/branch_1_fun/ppermute | solution.py:25
  126.5 0.6 collective-permute-done.5.refs_5_
  127.1 3.6 %branch_1_fun.18 = (bf16[512,2048]{1,0:T(8,128)(2,1)}, bf16[512,2048]{1,0:T(8,128)(2,1)}) custom-call(s32[1]{0:T(128)} %get-tuple-element.210.part_ref, bf16[576,1024]{1,0:T(8,128)(2,1)} %get-tuple-element.211.refs_0_, bf16[288,1024]{1,0:T(8,128)(2,1)S(1)} %get-tuple-element.212.refs_1_, bf16[288,1024]{1,0:T(8,128)(2,1)S(1)} %copy-done.3, ...), custom_call_target="tpu_custom_call" | custom-call | flops 1 | bytes 1 | tf_op jit(solution)/shard_map/cond/branch_1_fun/pallas_call | solution.py:638
  130.7 0.2 collective-permute-start.30
  130.9 1.1 collective-permute-done.30.refs_1_
  132.1 0.6 copy-done.11
  132.7 1.5 shard_map.141
  134.2 8.9 %shard_map.142 = (bf16[768,2048]{1,0:T(8,128)(2,1)}, bf16[768,2048]{1,0:T(8,128)(2,1)}) custom-call(s32[1]{0:T(128)} %bitcast.31.go_ref, f32[1,512]{1,0:T(1,128)S(1)} %get-tuple-element.282.weight_ref, bf16[512,2048]{1,0:T(8,128)(2,1)} %get-tuple-element.283.refs_0_, ...), custom_call_target="tpu_custom_call", output_to_operand_aliasing={{0}: (6, {}), {1}: (7, {})} | custom-call | flops 1 | bytes 1 | tf_op jit(solution)/shard_map/pallas_call | solution.py:582
  143.1 1.3 collective-permute-start.32
  144.4 4.2 %collective-permute-done.33.refs_3_ = bf16[256,2048]{1,0:T(8,128)(2,1)} collective-permute-done((bf16[256,2048]{1,0:T(8,128)(2,1)}, bf16[256,2048]{1,0:T(8,128)(2,1)}, u32[]{:S(2)}, u32[]{:S(2)}) %collective-permute-start.33) | collective-permute-done | bytes 1048608 | tf_op jit(solution)/shard_map/ppermute | solution.py:462
  148.7 5.8 %shard_map.143 = (bf16[768,2048]{1,0:T(8,128)(2,1)}, bf16[768,2048]{1,0:T(8,128)(2,1)}) custom-call(s32[1]{0:T(128)} %bitcast.31.go_ref, f32[1,512]{1,0:T(1,128)S(1)} %get-tuple-element.282.weight_ref, bf16[512,2048]{1,0:T(8,128)(2,1)} %get-tuple-element.283.refs_0_, ...), custom_call_target="tpu_custom_call", output_to_operand_aliasing={{0}: (6, {}), {1}: (7, {})} | custom-call | flops 1 | bytes 1 | tf_op jit(solution)/shard_map/pallas_call | solution.py:582
  154.5 4.1 %collective-permute-done.32 = bf16[32,1024]{1,0:T(8,128)(2,1)S(1)} collective-permute-done((bf16[32,1024]{1,0:T(8,128)(2,1)S(1)}, bf16[32,1024]{1,0:T(8,128)(2,1)S(1)}, u32[]{:S(2)}, u32[]{:S(2)}) %collective-permute-start.32) | collective-permute-done | bytes 65568 | tf_op jit(solution)/shard_map/ppermute | solution.py:666
  158.5 0.6 broadcast_select_fusion
  (36 shorter events, 0.1 us)
Async XLA Ops:
  3.2 9.3 %copy-start.7 = (bf16[64,1024]{1,0:T(8,128)(2,1)}, bf16[64,1024]{1,0:T(8,128)(2,1)S(1)}, u32[]{:S(2)}) copy-start(bf16[64,1024]{1,0:T(8,128)(2,1)S(1)} %get-tuple-element.258) | copy-start | bytes 393220
  3.2 6.6 %collective-permute-start.28 = (bf16[64,1024]{1,0:T(8,128)(2,1)S(1)}, bf16[64,1024]{1,0:T(8,128)(2,1)}, u32[]{:S(2)}, u32[]{:S(2)}) collective-permute-start(bf16[64,1024]{1,0:T(8,128)(2,1)S(1)} %get-tuple-element.258), channel_id=1, source_target_pairs={{0,16},{16,0},{1,17},{17,1},{2,18},{18,2},{3,19},{19,3},{4,20},{20... | collective-permute-start | bytes 393224 | tf_op jit(solution)/shard_map/ppermute | solution.py:29
  6.2 6.2 %copy-start.1 = (bf16[1,1,768,2048]{3,2,1,0:T(8,128)(2,1)S(1)}, bf16[1,1,768,2048]{3,2,1,0:T(8,128)(2,1)}, u32[]{:S(2)}) copy-start(bf16[1,1,768,2048]{3,2,1,0:T(8,128)(2,1)} %param.24) | copy-start | bytes 9437188
  6.2 6.2 %copy-start.9 = (f32[2048]{0:T(1024)S(1)}, f32[2048]{0:T(1024)}, u32[]{:S(2)}) copy-start(f32[2048]{0:T(1024)} %param.21) | copy-start | bytes 24580
  6.2 6.2 %copy-start.12 = (s32[128,2]{0,1:T(2,128)S(1)}, s32[128,2]{0,1:T(2,128)}, u32[]{:S(2)}) copy-start(s32[128,2]{0,1:T(2,128)} %param.30) | copy-start | bytes 3076
  6.2 6.2 %copy-start.13 = (f32[128,2]{0,1:T(2,128)S(1)}, f32[128,2]{0,1:T(2,128)}, u32[]{:S(2)}) copy-start(f32[128,2]{0,1:T(2,128)} %param.31) | copy-start | bytes 3076
  6.2 6.2 %copy-start.14 = (s32[1,2,4]{2,1,0:T(2,128)S(1)}, s32[1,2,4]{2,1,0:T(2,128)}, u32[]{:S(2)}) copy-start(s32[1,2,4]{2,1,0:T(2,128)} %param.28) | copy-start | bytes 100
  6.2 6.2 %copy-start.15 = (s32[1,8]{1,0:T(1,128)S(1)}, s32[1,8]{1,0:T(1,128)}, u32[]{:S(2)}) copy-start(s32[1,8]{1,0:T(1,128)} %param.29) | copy-start | bytes 100
  9.8 124.4 %collective-permute-start.31 = (bf16[1280,2048]{1,0:T(8,128)(2,1)}, bf16[1280,2048]{1,0:T(8,128)(2,1)}, u32[]{:S(2)}, u32[]{:S(2)}) collective-permute-start(bf16[1280,2048]{1,0:T(8,128)(2,1)} %get-tuple-element.285), channel_id=1, source_target_pairs={{16,0},{17,1},{18,2},{19,3},{20,4},{21,5},{22,6},{23,7},{24,8},{25... | collective-permute-start | bytes 15728648 | tf_op jit(solution)/shard_map/ppermute | solution.py:461
  11.1 137.6 %collective-permute-start.33 = (bf16[256,2048]{1,0:T(8,128)(2,1)}, bf16[256,2048]{1,0:T(8,128)(2,1)}, u32[]{:S(2)}, u32[]{:S(2)}) collective-permute-start(bf16[256,2048]{1,0:T(8,128)(2,1)} %get-tuple-element.289), channel_id=1, source_target_pairs={{16,0},{17,1},{18,2},{19,3},{20,4},{21,5},{22,6},{23,7},{24,8},{25... | collective-permute-start | bytes 3145736 | tf_op jit(solution)/shard_map/ppermute | solution.py:462
  26.3 1.4 collective-permute-start.13
  31.1 1.5 collective-permute-start.14
  33.3 11.9 %all-to-all-start.1 = ((bf16[8,48,256]{2,1,0:T(8,128)(2,1)}), bf16[8,48,256]{2,1,0:T(8,128)(2,1)S(1)}, u32[]{:S(2)}, u32[]{:S(2)}) async-start(bf16[8,48,256]{2,1,0:T(8,128)(2,1)} %bitcast.5), calls=%async_computation.1 | async-start | bytes 393216 | tf_op jit(solution)/shard_map/cond/branch_1_fun/all_to_all | solution.py:489
  46.5 35.2 %copy-start.8 = (bf16[64,1024]{1,0:T(8,128)(2,1)S(1)}, bf16[64,1024]{1,0:T(8,128)(2,1)}, u32[]{:S(2)}) copy-start(bf16[64,1024]{1,0:T(8,128)(2,1)} %copy-done.7) | copy-start | bytes 393220
  57.7 1.4 collective-permute-start.15
  62.5 1.5 collective-permute-start.16
  64.7 11.9 %all-to-all-start.3 = ((bf16[8,48,256]{2,1,0:T(8,128)(2,1)}), bf16[8,48,256]{2,1,0:T(8,128)(2,1)S(1)}, u32[]{:S(2)}, u32[]{:S(2)}) async-start(bf16[8,48,256]{2,1,0:T(8,128)(2,1)} %bitcast.10), calls=%async_computation.3 | async-start | bytes 393216 | tf_op jit(solution)/shard_map/cond/branch_1_fun/all_to_all | solution.py:489
  77.5 4.1 %collective-permute-start.29 = (f32[128,256]{1,0:T(8,128)}, f32[128,256]{1,0:T(8,128)S(1)}, u32[]{:S(2)}, u32[]{:S(2)}) collective-permute-start(f32[128,256]{1,0:T(8,128)} %get-tuple-element.272), channel_id=1, source_target_pairs={{0,16},{1,17},{2,18},{3,19},{4,20},{5,21},{6,22},{7,23},{8,24},{9,... | collective-permute-start | bytes 393224 | tf_op jit(solution)/shard_map/ppermute | solution.py:620
  82.7 10.8 %collective-permute-start.21 = (bf16[144,1024]{1,0:T(8,128)(2,1)S(1)}, bf16[144,1024]{1,0:T(8,128)(2,1)S(1)}, u32[]{:S(2)}, u32[]{:S(2)}) collective-permute-start(bf16[144,1024]{1,0:T(8,128)(2,1)S(1)} %branch_1_fun.16), channel_id=1, source_target_pairs={{0,12},{2,14},{4,0},{6,2},{8,4},{10,6},{12,8},{14,10},{1,13},{3,15... | collective-permute-start | bytes 884744 | tf_op jit(solution)/shard_map/cond/branch_1_fun/ppermute | solution.py:522
  86.0 12.8 %collective-permute-start.20 = (bf16[144,1024]{1,0:T(8,128)(2,1)S(1)}, bf16[144,1024]{1,0:T(8,128)(2,1)S(1)}, u32[]{:S(2)}, u32[]{:S(2)}) collective-permute-start(bf16[144,1024]{1,0:T(8,128)(2,1)S(1)} %branch_1_fun.16), channel_id=1, source_target_pairs={{0,4},{2,6},{4,8},{6,10},{8,12},{10,14},{12,0},{14,2},{1,5},{3,7},... | collective-permute-start | bytes 884744 | tf_op jit(solution)/shard_map/cond/branch_1_fun/ppermute | solution.py:522
  86.0 12.8 %collective-permute-start.19 = (bf16[144,1024]{1,0:T(8,128)(2,1)S(1)}, bf16[144,1024]{1,0:T(8,128)(2,1)S(1)}, u32[]{:S(2)}, u32[]{:S(2)}) collective-permute-start(bf16[144,1024]{1,0:T(8,128)(2,1)S(1)} %branch_1_fun.16), channel_id=1, source_target_pairs={{0,2},{2,0},{4,6},{6,4},{8,10},{10,8},{12,14},{14,12},{1,3},{3,1},... | collective-permute-start | bytes 884744 | tf_op jit(solution)/shard_map/cond/branch_1_fun/ppermute | solution.py:29
  98.8 14.8 %collective-permute-start.24 = (bf16[144,1024]{1,0:T(8,128)(2,1)S(1)}, bf16[144,1024]{1,0:T(8,128)(2,1)S(1)}, u32[]{:S(2)}, u32[]{:S(2)}) collective-permute-start(bf16[144,1024]{1,0:T(8,128)(2,1)S(1)} %branch_1_fun.16), channel_id=1, source_target_pairs={{0,8},{2,10},{4,12},{6,14},{8,0},{10,2},{12,4},{14,6},{1,9},{3,11}... | collective-permute-start | bytes 884744 | tf_op jit(solution)/shard_map/cond/branch_1_fun/ppermute | solution.py:522
  98.8 18.3 %collective-permute-start.22 = (bf16[144,1024]{1,0:T(8,128)(2,1)S(1)}, bf16[144,1024]{1,0:T(8,128)(2,1)S(1)}, u32[]{:S(2)}, u32[]{:S(2)}) collective-permute-start(bf16[144,1024]{1,0:T(8,128)(2,1)S(1)} %collective-permute-done.20), channel_id=1, source_target_pairs={{0,2},{2,0},{4,6},{6,4},{8,10},{10,8},{12,14},{14,12},{1,3},{3,1},... | collective-permute-start | bytes 884744 | tf_op jit(solution)/shard_map/cond/branch_1_fun/ppermute | solution.py:29
  100.5 16.7 %collective-permute-start.23 = (bf16[144,1024]{1,0:T(8,128)(2,1)S(1)}, bf16[144,1024]{1,0:T(8,128)(2,1)S(1)}, u32[]{:S(2)}, u32[]{:S(2)}) collective-permute-start(bf16[144,1024]{1,0:T(8,128)(2,1)S(1)} %collective-permute-done.21), channel_id=1, source_target_pairs={{0,2},{2,0},{4,6},{6,4},{8,10},{10,8},{12,14},{14,12},{1,3},{3,1},... | collective-permute-start | bytes 884744 | tf_op jit(solution)/shard_map/cond/branch_1_fun/ppermute | solution.py:29
  113.6 7.8 %collective-permute-start.25 = (bf16[144,1024]{1,0:T(8,128)(2,1)S(1)}, bf16[144,1024]{1,0:T(8,128)(2,1)S(1)}, u32[]{:S(2)}, u32[]{:S(2)}) collective-permute-start(bf16[144,1024]{1,0:T(8,128)(2,1)S(1)} %collective-permute-done.24), channel_id=1, source_target_pairs={{0,2},{2,0},{4,6},{6,4},{8,10},{10,8},{12,14},{14,12},{1,3},{3,1},... | collective-permute-start | bytes 884744 | tf_op jit(solution)/shard_map/cond/branch_1_fun/ppermute | solution.py:29
  121.5 0.8 copy-start.2
  122.3 4.7 %collective-permute-start.3 = (bf16[576,1024]{1,0:T(8,128)(2,1)}, bf16[576,1024]{1,0:T(8,128)(2,1)S(1)}, u32[]{:S(2)}, u32[]{:S(2)}) collective-permute-start(bf16[576,1024]{1,0:T(8,128)(2,1)} %get-tuple-element.211.refs_0_), channel_id=1, source_target_pairs={{0,1},{1,0},{2,3},{3,2},{4,5},{5,4},{6,7},{7,6},{8,9},{9,8},{10,11... | collective-permute-start | bytes 3538952 | tf_op jit(solution)/shard_map/cond/branch_1_fun/ppermute | solution.py:25
  122.3 4.2 %collective-permute-start.4 = (bf16[288,1024]{1,0:T(8,128)(2,1)S(1)}, bf16[288,1024]{1,0:T(8,128)(2,1)S(1)}, u32[]{:S(2)}, u32[]{:S(2)}) collective-permute-start(bf16[288,1024]{1,0:T(8,128)(2,1)S(1)} %get-tuple-element.212.refs_1_), channel_id=1, source_target_pairs={{0,1},{1,0},{2,3},{3,2},{4,5},{5,4},{6,7},{7,6},{8,9},{9,8},{10,11... | collective-permute-start | bytes 1769480 | tf_op jit(solution)/shard_map/cond/branch_1_fun/ppermute | solution.py:25
  122.8 4.2 %collective-permute-start.5 = (bf16[288,1024]{1,0:T(8,128)(2,1)}, bf16[288,1024]{1,0:T(8,128)(2,1)S(1)}, u32[]{:S(2)}, u32[]{:S(2)}) collective-permute-start(bf16[288,1024]{1,0:T(8,128)(2,1)} %copy-done.2), channel_id=1, source_target_pairs={{0,1},{1,0},{2,3},{3,2},{4,5},{5,4},{6,7},{7,6},{8,9},{9,8},{10,11... | collective-permute-start | bytes 1769480 | tf_op jit(solution)/shard_map/cond/branch_1_fun/ppermute | solution.py:25
  122.8 4.2 %copy-start.3 = (bf16[288,1024]{1,0:T(8,128)(2,1)S(1)}, bf16[288,1024]{1,0:T(8,128)(2,1)}, u32[]{:S(2)}) copy-start(bf16[288,1024]{1,0:T(8,128)(2,1)} %copy-done.2) | copy-start | bytes 1769476 | tf_op jit(solution)/shard_map/cond
  130.7 1.3 collective-permute-start.30
  132.1 0.6 copy-start.11
  134.2 8.9 %copy-start.16 = (bf16[32,1024]{1,0:T(8,128)(2,1)S(1)}, bf16[32,1024]{1,0:T(8,128)(2,1)}, u32[]{:S(2)}) copy-start(bf16[32,1024]{1,0:T(8,128)(2,1)} %get-tuple-element.287) | copy-start | bytes 196612
  143.1 15.4 %collective-permute-start.32 = (bf16[32,1024]{1,0:T(8,128)(2,1)S(1)}, bf16[32,1024]{1,0:T(8,128)(2,1)S(1)}, u32[]{:S(2)}, u32[]{:S(2)}) collective-permute-start(bf16[32,1024]{1,0:T(8,128)(2,1)S(1)} %copy-done.16), channel_id=1, source_target_pairs={{16,0},{17,1},{18,2},{19,3},{20,4},{21,5},{22,6},{23,7},{24,8},{25... | collective-permute-start | bytes 196616 | tf_op jit(solution)/shard_map/ppermute | solution.py:666
  148.7 9.9 %copy-start.10 = (bf16[32,1024]{1,0:T(8,128)(2,1)S(1)}, bf16[32,1024]{1,0:T(8,128)(2,1)}, u32[]{:S(2)}) copy-start(bf16[32,1024]{1,0:T(8,128)(2,1)} %get-tuple-element.288) | copy-start | bytes 196612

commit v4 on v3

--- a/solution.py
+++ b/solution.py
@@ -364,6 +364,14 @@
         update_rows(features, hidden, tile, weight_ref[...], in_copies, grad_copies, *rows, space)
 
 
+def hold_kernel(go_ref, array_ref, held_ref, sem):
+    @pl.when(go_ref[0] == 0)
+    def _():
+        copy = pltpu.make_async_copy(array_ref, held_ref, sem)
+        copy.start()
+        copy.wait()
+
+
 def join_kernel(parts, row_count, part_ref, *refs):
     pieces, (left_ref, right_ref, joined_ref) = refs[:parts], refs[parts:]
     width = pieces[0].shape[1]
@@ -619,6 +627,16 @@
     states, new_up, new_down = lax.cond(is_rollout, second_rollout, second_learner)
     states_there = lax.ppermute(states, "sect", [(0, 1)])
 
+    held_up = pl.pallas_call(
+        hold_kernel,
+        out_shape=weight_like,
+        in_specs=[smem, stays],
+        out_specs=vmem,
+        scratch_shapes=[pltpu.SemaphoreType.DMA],
+        compiler_params=fits(16),
+        cost_estimate=costs(1, 1),
+    )(go, new_up)
+
     def third_rollout():
         return (states, payload) + tuple(learner_rows([own_rows, crossed_rows])[0])
 
@@ -629,7 +647,7 @@
             compiler_params=fits(16),
             cost_estimate=costs(1, 1),
         )(targets, states_there)
-        return decode_step(half_steps, states_there, sent, new_up, new_down) + unset(*gather_like)
+        return decode_step(half_steps, states_there, sent, held_up, new_down) + unset(*gather_like)
 
     states, payload, *rows = lax.cond(is_rollout, third_rollout, third_learner)
 
@@ -648,7 +666,7 @@
     def fourth_learner():
         now, sent = states, payload
         for step in range(half_steps + 1, steps):
-            now, sent = decode_step(step, now, sent, new_up, new_down)
+            now, sent = decode_step(step, now, sent, held_up, new_down)
         return (sent,) + unset(rows_like, rows_like, weights_like)
 
     mine, inputs, grads, weights = lax.cond(is_rollout, fourth_rollout, fourth_learner)
@@ -662,9 +680,9 @@
         cost_estimate=costs(1, 1),
     )(part_ref, *pieces)
     new_up, new_down = update_late(2 * tile, (0, 0, hidden_here), first_there, new_up, new_down)
-    left, new_up = lax.optimization_barrier((left, new_up))
     delivered = lax.ppermute(left, "sect", [(1, 0)])
     new_up, new_down = update_late(tile, (2 * tile, 2 * tile, 0), second_there, new_up, new_down)
+    right, new_up = lax.optimization_barrier((right, new_up))
     final_states = jnp.where(is_rollout, delivered, right)
     return final_states, new_up[None, None], new_down[None, None]
 

time: 160 us -> 158 us (0.988)
  waiting for transfers between devices: 67.4 us -> 65.4 us
  other arithmetic: 3.27 us -> 4.93 us
    ppermute x1, waiting for transfers between devices: 4.08 us -> 2.32 us  [on_device(): delivered = lax.ppermute(left, 'sect', [(1, 0)])]
    cond x7 -> x9, local copies, waits for them, and re-layouts: 3.53 us -> 2.73 us
  transfers between devices with their start and end apart: 22 -> 22, of which waited for: 17 -> 17; matrix products, arithmetic and copies ran while one was open for 3% -> 4% of each run, Pallas kernels for 20% -> 20%
where the time goes in v4:
time: 158 us; the launch traced here: 157 us
  waiting for transfers between devices  65.4 us (41%)
  Pallas kernels  33.3 us (21%)
  blocking collectives  25 us (16%)
  starting transfers between devices  24.5 us (16%)
  other arithmetic  4.93 us (3%)
  local copies, waits for them, and re-layouts  3.39 us (2%)
    all_to_all x2, blocking collectives, decode_step(): lax.all_to_all(payload, 'exp', split_axis=0, concat_axis=0, tiled=True)  25 us
    ppermute x3, waiting for transfers between devices, along(): return lax.ppermute(array, 'exp', pairs)  24 us
    all_to_all x2, waiting for transfers between devices, decode_step(): lax.all_to_all(summed, 'exp', split_axis=0, concat_axis=0, tiled=True)  15.2 us
    pallas_call x2, Pallas kernels, update_late(): pl.pallas_call(functools.partial(late_kernel, features, hidden, tile, (co...  14.7 us
    ppermute x8, waiting for transfers between devices, shifted(): lax.ppermute(array, axis, [(i, (i + by) % size) for i in range(size)])  9.45 us
    ppermute x5, starting transfers between devices, flipped(): lax.ppermute(array, axis, [(i, i ^ bit) for i in range(lax.axis_size(axis...  8.09 us
    ppermute x5, waiting for transfers between devices, flipped(): lax.ppermute(array, axis, [(i, i ^ bit) for i in range(lax.axis_size(axis...  6.87 us
    all_to_all x2, starting transfers between devices, decode_step(): lax.all_to_all(summed, 'exp', split_axis=0, concat_axis=0, tiled=True)  6.78 us
  transfers between devices with their start and end apart: 22, of which 17 were waited for; matrix products, arithmetic and copies ran while one was open for 4% of the time, Pallas kernels for 20%

profile of v4, /device:TPU:0, one launch (start us, length us, event | category | flops | bytes accessed | tf_op | source)
XLA Modules:
  0.0 157.4 jit_solution(5073417005677794717)
XLA Ops:
  0.6 2.5 %shard_map.139 = (s32[4,2,128]{2,1,0:T(2,128)S(1)}, f32[8,128]{1,0:T(8,128)S(1)}, f32[128,256]{1,0:T(8,128)}, bf16[384,256]{1,0:T(8,128)(2,1)}, bf16[64,1024]{1,0:T(8,128)(2,1)S(1)}) custom-call(s32[1]{0:T(128)} %bitcast.24.part_ref, s32[8,32]{1,0:T(8,128)} %bitcast.66, f32[8,32]{1,0:T(8,128)} %bitcast.67, bf16[32,2048]{1,0:T(8,128)(2,1)} %all_rows_ref.1, ...), custom_call_target="tpu_custom_call" | custom-call | flops 1 | bytes 1 | tf_op jit(solution)/shard_map/pallas_call | solution.py:441
  3.2 3.0 %collective-permute-start.28 = (bf16[64,1024]{1,0:T(8,128)(2,1)S(1)}, bf16[64,1024]{1,0:T(8,128)(2,1)}, u32[]{:S(2)}, u32[]{:S(2)}) collective-permute-start(bf16[64,1024]{1,0:T(8,128)(2,1)S(1)} %get-tuple-element.258), channel_id=1, source_target_pairs={{0,16},{16,0},{1,17},{17,1},{2,18},{18,2},{3,19},{19,3},{4,20},{20... | collective-permute-start | bytes 393224 | tf_op jit(solution)/shard_map/ppermute | solution.py:29
  6.2 0.0 copy-start.18
  6.2 0.0 copy-start.19
  6.2 0.1 shard_map.140
  6.3 3.5 %collective-permute-done.28 = bf16[64,1024]{1,0:T(8,128)(2,1)} collective-permute-done((bf16[64,1024]{1,0:T(8,128)(2,1)S(1)}, bf16[64,1024]{1,0:T(8,128)(2,1)}, u32[]{:S(2)}, u32[]{:S(2)}) %collective-permute-start.28) | collective-permute-done | bytes 131104 | tf_op jit(solution)/shard_map/ppermute | solution.py:29
  9.8 1.3 collective-permute-start.32
  11.0 1.3 collective-permute-start.33
  12.4 34.0 %conditional.4 = (f32[128,256]{1,0:T(8,128)}, bf16[384,256]{1,0:T(8,128)(2,1)}, bf16[576,1024]{1,0:T(8,128)(2,1)}, bf16[288,1024]{1,0:T(8,128)(2,1)}, bf16[288,1024]{1,0:T(8,128)(2,1)}) conditional(s32[]{:T(128)} %convert_element_type.43, (s32[128,2]{0,1:T(2,128)S(1)}, f32[128,2]{0,1:T(2,128)S(1)}, s32[1,2,4]{2,1,0:T(2,128)S(1)}, ...), branch_computations={%region_0.0_spmd, %region_1.0_spmd} | conditional | flops 7077889 | bytes 12976449 | solution.py:615
  12.4 13.9 %all_to_all.64 = bf16[8,48,256]{2,1,0:T(8,128)(2,1)S(1)} all-to-all(bf16[8,48,256]{2,1,0:T(8,128)(2,1)} %bitcast.3), channel_id=1, replica_groups=mesh['sect'=2,'exp'=8,'dp'=2] {'exp'}, dimensions={0} | all-to-all | bytes 393216 | tf_op jit(solution)/shard_map/cond/branch_1_fun/all_to_all | solution.py:492
  26.3 1.4 collective-permute-done.13.refs_1_
  27.8 3.3 %branch_1_fun.10 = (bf16[384,256]{1,0:T(8,128)(2,1)S(1)}, bf16[384,256]{1,0:T(8,128)(2,1)S(1)}) custom-call(s32[1]{0:T(128)} %get-tuple-element.135.part_ref, f32[1,2048]{1,0:T(1,128)S(1)} %get-tuple-element.136.gain_ref, bf16[384,256]{1,0:T(8,128)(2,1)S(1)} %bitcast.47, bf16[384,256]{1,0:T(8,128)(2,1)S(1)} %collective-permute-done.13.refs_1_, ...), custom_call_target="tpu_custom_call" | custom-call | flops 1 | bytes 1 | tf_op jit(solution)/shard_map/cond/branch_1_fun/pallas_call | solution.py:474
  31.1 0.2 collective-permute-start.14
  31.3 1.3 collective-permute-done.14
  32.6 0.7 add_convert_fusion
  33.3 3.4 %all-to-all-start.1 = ((bf16[8,48,256]{2,1,0:T(8,128)(2,1)}), bf16[8,48,256]{2,1,0:T(8,128)(2,1)S(1)}, u32[]{:S(2)}, u32[]{:S(2)}) async-start(bf16[8,48,256]{2,1,0:T(8,128)(2,1)} %bitcast.5), calls=%async_computation.1 | async-start | bytes 393216 | tf_op jit(solution)/shard_map/cond/branch_1_fun/all_to_all | solution.py:497
  36.7 0.9 copy.59.states_ref
  37.6 7.6 %all-to-all-done.1 = bf16[8,48,256]{2,1,0:T(8,128)(2,1)S(1)} async-done(((bf16[8,48,256]{2,1,0:T(8,128)(2,1)}), bf16[8,48,256]{2,1,0:T(8,128)(2,1)S(1)}, u32[]{:S(2)}, u32[]{:S(2)}) %all-to-all-start.1) | async-done | bytes 196640 | tf_op jit(solution)/shard_map/cond/branch_1_fun/all_to_all | solution.py:497
  45.2 1.2 branch_1_fun.11
  46.4 30.9 %conditional.5 = (f32[128,256]{1,0:T(8,128)}, bf16[768,2048]{1,0:T(8,128)(2,1)}, bf16[768,2048]{1,0:T(8,128)(2,1)}) conditional(s32[]{:T(128)} %convert_element_type.43, (s32[]{:T(128)}, bf16[576,1024]{1,0:T(8,128)(2,1)}, bf16[288,1024]{1,0:T(8,128)(2,1)}, bf16[288,1024]{1,0:T(8,128)(2,1)}, s32[1]{0:T(128)}, ...), branch_computations={%region_2.0_spmd, %region_3.0_spmd} | conditional | flops 393219 | bytes 18882816 | solution.py:627
  46.4 11.1 %all_to_all.65 = bf16[8,48,256]{2,1,0:T(8,128)(2,1)S(1)} all-to-all(bf16[8,48,256]{2,1,0:T(8,128)(2,1)} %bitcast.8), channel_id=1, replica_groups=mesh['sect'=2,'exp'=8,'dp'=2] {'exp'}, dimensions={0} | all-to-all | bytes 393216 | tf_op jit(solution)/shard_map/cond/branch_1_fun/all_to_all | solution.py:492
  57.5 1.4 collective-permute-done.15.refs_1_
  59.0 3.3 %branch_1_fun.13 = (bf16[384,256]{1,0:T(8,128)(2,1)S(1)}, bf16[384,256]{1,0:T(8,128)(2,1)S(1)}) custom-call(s32[1]{0:T(128)} %get-tuple-element.160.part_ref, f32[1,2048]{1,0:T(1,128)S(1)} %get-tuple-element.161.gain_ref, bf16[384,256]{1,0:T(8,128)(2,1)S(1)} %bitcast.49, bf16[384,256]{1,0:T(8,128)(2,1)S(1)} %collective-permute-done.15.refs_1_, ...), custom_call_target="tpu_custom_call" | custom-call | flops 1 | bytes 1 | tf_op jit(solution)/shard_map/cond/branch_1_fun/pallas_call | solution.py:474
  62.3 0.2 collective-permute-start.16
  62.5 1.3 collective-permute-done.16
  63.8 0.7 add_convert_fusion.1
  64.5 3.4 %all-to-all-start.3 = ((bf16[8,48,256]{2,1,0:T(8,128)(2,1)}), bf16[8,48,256]{2,1,0:T(8,128)(2,1)S(1)}, u32[]{:S(2)}, u32[]{:S(2)}) async-start(bf16[8,48,256]{2,1,0:T(8,128)(2,1)} %bitcast.10), calls=%async_computation.3 | async-start | bytes 393216 | tf_op jit(solution)/shard_map/cond/branch_1_fun/all_to_all | solution.py:497
  67.9 0.9 copy.60.states_ref
  68.8 7.6 %all-to-all-done.3 = bf16[8,48,256]{2,1,0:T(8,128)(2,1)S(1)} async-done(((bf16[8,48,256]{2,1,0:T(8,128)(2,1)}), bf16[8,48,256]{2,1,0:T(8,128)(2,1)S(1)}, u32[]{:S(2)}, u32[]{:S(2)}) %all-to-all-start.3) | async-done | bytes 196640 | tf_op jit(solution)/shard_map/cond/branch_1_fun/all_to_all | solution.py:497
  76.4 1.0 branch_1_fun.14
  77.4 1.3 collective-permute-start.29
  78.7 2.9 %collective-permute-done.29 = f32[128,256]{1,0:T(8,128)S(1)} collective-permute-done((f32[128,256]{1,0:T(8,128)}, f32[128,256]{1,0:T(8,128)S(1)}, u32[]{:S(2)}, u32[]{:S(2)}) %collective-permute-start.29) | collective-permute-done | bytes 131104 | tf_op jit(solution)/shard_map/ppermute | solution.py:628
  81.6 40.7 %conditional.6 = (f32[128,256]{1,0:T(8,128)S(1)}, bf16[384,256]{1,0:T(8,128)(2,1)}, bf16[576,1024]{1,0:T(8,128)(2,1)}, bf16[288,1024]{1,0:T(8,128)(2,1)}, bf16[288,1024]{1,0:T(8,128)(2,1)}) conditional(s32[]{:T(128)} %convert_element_type.43, (s32[4,2,128]{2,1,0:T(2,128)S(1)}, f32[128,256]{1,0:T(8,128)S(1)}, s32[1]{0:T(128)}, ...), branch_computations={%region_4.0_spmd, %region_5.0_spmd} | conditional | flops 7077889 | bytes 13238593 | solution.py:652
  81.6 1.1 branch_1_fun.16
  82.6 3.3 %collective-permute-start.21 = (bf16[144,1024]{1,0:T(8,128)(2,1)S(1)}, bf16[144,1024]{1,0:T(8,128)(2,1)S(1)}, u32[]{:S(2)}, u32[]{:S(2)}) collective-permute-start(bf16[144,1024]{1,0:T(8,128)(2,1)S(1)} %branch_1_fun.16), channel_id=1, source_target_pairs={{0,12},{2,14},{4,0},{6,2},{8,4},{10,6},{12,8},{14,10},{1,13},{3,15... | collective-permute-start | bytes 884744 | tf_op jit(solution)/shard_map/cond/branch_1_fun/ppermute | solution.py:530
  86.0 1.5 collective-permute-start.19
  87.5 5.9 %collective-permute-done.21 = bf16[144,1024]{1,0:T(8,128)(2,1)S(1)} collective-permute-done((bf16[144,1024]{1,0:T(8,128)(2,1)S(1)}, bf16[144,1024]{1,0:T(8,128)(2,1)S(1)}, u32[]{:S(2)}, u32[]{:S(2)}) %collective-permute-start.21) | collective-permute-done | bytes 294944 | tf_op jit(solution)/shard_map/cond/branch_1_fun/ppermute | solution.py:530
  93.4 5.3 %collective-permute-done.20 = bf16[144,1024]{1,0:T(8,128)(2,1)S(1)} collective-permute-done((bf16[144,1024]{1,0:T(8,128)(2,1)S(1)}, bf16[144,1024]{1,0:T(8,128)(2,1)S(1)}, u32[]{:S(2)}, u32[]{:S(2)}) %collective-permute-start.20) | collective-permute-done | bytes 294944 | tf_op jit(solution)/shard_map/cond/branch_1_fun/ppermute | solution.py:530
  98.8 1.6 %collective-permute-start.22 = (bf16[144,1024]{1,0:T(8,128)(2,1)S(1)}, bf16[144,1024]{1,0:T(8,128)(2,1)S(1)}, u32[]{:S(2)}, u32[]{:S(2)}) collective-permute-start(bf16[144,1024]{1,0:T(8,128)(2,1)S(1)} %collective-permute-done.20), channel_id=1, source_target_pairs={{0,2},{2,0},{4,6},{6,4},{8,10},{10,8},{12,14},{14,12},{1,3},{3,1},... | collective-permute-start | bytes 884744 | tf_op jit(solution)/shard_map/cond/branch_1_fun/ppermute | solution.py:29
  100.4 0.4 collective-permute-start.23
  100.8 12.8 %collective-permute-done.24 = bf16[144,1024]{1,0:T(8,128)(2,1)S(1)} collective-permute-done((bf16[144,1024]{1,0:T(8,128)(2,1)S(1)}, bf16[144,1024]{1,0:T(8,128)(2,1)S(1)}, u32[]{:S(2)}, u32[]{:S(2)}) %collective-permute-start.24) | collective-permute-done | bytes 294944 | tf_op jit(solution)/shard_map/cond/branch_1_fun/ppermute | solution.py:530
  113.6 1.5 collective-permute-start.25
  115.1 0.9 copy.40
  116.0 1.1 pad_maximum_fusion.3
  117.1 0.9 pad_maximum_fusion.4
  118.0 3.4 %collective-permute-done.25 = bf16[144,1024]{1,0:T(8,128)(2,1)S(1)} collective-permute-done((bf16[144,1024]{1,0:T(8,128)(2,1)S(1)}, bf16[144,1024]{1,0:T(8,128)(2,1)S(1)}, u32[]{:S(2)}, u32[]{:S(2)}) %collective-permute-start.25) | collective-permute-done | bytes 294944 | tf_op jit(solution)/shard_map/cond/branch_1_fun/ppermute | solution.py:29
  121.4 0.9 pad_maximum_fusion.5
  122.3 7.8 %conditional.7 = (bf16[128,256]{1,0:T(8,128)(2,1)}, bf16[512,2048]{1,0:T(8,128)(2,1)}, bf16[512,2048]{1,0:T(8,128)(2,1)}, f32[1,512]{1,0:T(1,128)S(1)}) conditional(s32[]{:T(128)} %convert_element_type.43, (bf16[384,256]{1,0:T(8,128)(2,1)}, s32[1]{0:T(128)}, f32[1,2048]{1,0:T(1,128)S(1)}, bf16[768,2048]{1,0:T(8,128)(2,1)S(1)}, ...), branch_computations={%region_6.0_spmd, %region_7.0_spmd} | conditional | flops 393219 | bytes 18874604 | solution.py:672
  122.3 0.5 collective-permute-start.4
  122.8 0.0 collective-permute-start.5
  122.8 1.5 branch_1_fun.19
  124.3 1.8 %collective-permute-done.4.refs_4_ = bf16[288,1024]{1,0:T(8,128)(2,1)S(1)} collective-permute-done((bf16[288,1024]{1,0:T(8,128)(2,1)}, bf16[288,1024]{1,0:T(8,128)(2,1)S(1)}, u32[]{:S(2)}, u32[]{:S(2)}) %collective-permute-start.4) | collective-permute-done | bytes 589856 | tf_op jit(solution)/shard_map/cond/branch_1_fun/ppermute | solution.py:25
  126.2 0.8 collective-permute-done.5.refs_5_
  127.0 3.0 %branch_1_fun.18 = (bf16[512,2048]{1,0:T(8,128)(2,1)}, bf16[512,2048]{1,0:T(8,128)(2,1)}) custom-call(s32[1]{0:T(128)} %get-tuple-element.210.part_ref, bf16[576,1024]{1,0:T(8,128)(2,1)S(1)} %copy-done.2, bf16[288,1024]{1,0:T(8,128)(2,1)S(1)} %copy-done.3, bf16[288,1024]{1,0:T(8,128)(2,1)S(1)} %copy-done.4, ...), custom_call_target="tpu_custom_call" | custom-call | flops 1 | bytes 1 | tf_op jit(solution)/shard_map/cond/branch_1_fun/pallas_call | solution.py:656
  130.1 0.2 collective-permute-start.30
  130.3 1.3 collective-permute-done.30.refs_1_
  131.6 0.6 copy-done.15
  132.2 1.5 shard_map.142
  133.8 1.3 collective-permute-start.31
  135.1 8.9 %shard_map.143 = (bf16[768,2048]{1,0:T(8,128)(2,1)}, bf16[768,2048]{1,0:T(8,128)(2,1)}) custom-call(s32[1]{0:T(128)} %bitcast.31.go_ref, f32[1,512]{1,0:T(1,128)S(1)} %get-tuple-element.283.weight_ref, bf16[512,2048]{1,0:T(8,128)(2,1)} %get-tuple-element.284.refs_0_, ...), custom_call_target="tpu_custom_call", output_to_operand_aliasing={{0}: (6, {}), {1}: (7, {})} | custom-call | flops 1 | bytes 1 | tf_op jit(solution)/shard_map/pallas_call | solution.py:590
  144.0 4.6 %collective-permute-done.33.refs_3_ = bf16[256,2048]{1,0:T(8,128)(2,1)} collective-permute-done((bf16[256,2048]{1,0:T(8,128)(2,1)}, bf16[256,2048]{1,0:T(8,128)(2,1)}, u32[]{:S(2)}, u32[]{:S(2)}) %collective-permute-start.33) | collective-permute-done | bytes 1048608 | tf_op jit(solution)/shard_map/ppermute | solution.py:470
  148.7 5.8 %shard_map.144 = (bf16[768,2048]{1,0:T(8,128)(2,1)}, bf16[768,2048]{1,0:T(8,128)(2,1)}) custom-call(s32[1]{0:T(128)} %bitcast.31.go_ref, f32[1,512]{1,0:T(1,128)S(1)} %get-tuple-element.283.weight_ref, bf16[512,2048]{1,0:T(8,128)(2,1)} %get-tuple-element.284.refs_0_, ...), custom_call_target="tpu_custom_call", output_to_operand_aliasing={{0}: (6, {}), {1}: (7, {})} | custom-call | flops 1 | bytes 1 | tf_op jit(solution)/shard_map/pallas_call | solution.py:590
  154.4 2.3 %collective-permute-done.31 = bf16[32,1024]{1,0:T(8,128)(2,1)S(1)} collective-permute-done((bf16[32,1024]{1,0:T(8,128)(2,1)}, bf16[32,1024]{1,0:T(8,128)(2,1)S(1)}, u32[]{:S(2)}, u32[]{:S(2)}) %collective-permute-start.31) | collective-permute-done | bytes 65568 | tf_op jit(solution)/shard_map/ppermute | solution.py:683
  156.8 0.6 broadcast_select_fusion
  (37 shorter events, 0.1 us)
Async XLA Ops:
  3.1 9.3 %copy-start.8 = (bf16[64,1024]{1,0:T(8,128)(2,1)}, bf16[64,1024]{1,0:T(8,128)(2,1)S(1)}, u32[]{:S(2)}) copy-start(bf16[64,1024]{1,0:T(8,128)(2,1)S(1)} %get-tuple-element.258) | copy-start | bytes 393220
  3.2 6.6 %collective-permute-start.28 = (bf16[64,1024]{1,0:T(8,128)(2,1)S(1)}, bf16[64,1024]{1,0:T(8,128)(2,1)}, u32[]{:S(2)}, u32[]{:S(2)}) collective-permute-start(bf16[64,1024]{1,0:T(8,128)(2,1)S(1)} %get-tuple-element.258), channel_id=1, source_target_pairs={{0,16},{16,0},{1,17},{17,1},{2,18},{18,2},{3,19},{19,3},{4,20},{20... | collective-permute-start | bytes 393224 | tf_op jit(solution)/shard_map/ppermute | solution.py:29
  6.2 6.2 %copy-start.1 = (bf16[1,1,768,2048]{3,2,1,0:T(8,128)(2,1)S(1)}, bf16[1,1,768,2048]{3,2,1,0:T(8,128)(2,1)}, u32[]{:S(2)}) copy-start(bf16[1,1,768,2048]{3,2,1,0:T(8,128)(2,1)} %param.24) | copy-start | bytes 9437188
  6.2 6.2 %copy-start.11 = (f32[2048]{0:T(1024)S(1)}, f32[2048]{0:T(1024)}, u32[]{:S(2)}) copy-start(f32[2048]{0:T(1024)} %param.21) | copy-start | bytes 24580
  6.2 6.2 %copy-start.16 = (s32[128,2]{0,1:T(2,128)S(1)}, s32[128,2]{0,1:T(2,128)}, u32[]{:S(2)}) copy-start(s32[128,2]{0,1:T(2,128)} %param.30) | copy-start | bytes 3076
  6.2 6.2 %copy-start.17 = (f32[128,2]{0,1:T(2,128)S(1)}, f32[128,2]{0,1:T(2,128)}, u32[]{:S(2)}) copy-start(f32[128,2]{0,1:T(2,128)} %param.31) | copy-start | bytes 3076
  6.2 6.2 %copy-start.18 = (s32[1,2,4]{2,1,0:T(2,128)S(1)}, s32[1,2,4]{2,1,0:T(2,128)}, u32[]{:S(2)}) copy-start(s32[1,2,4]{2,1,0:T(2,128)} %param.28) | copy-start | bytes 100
  6.2 6.2 %copy-start.19 = (s32[1,8]{1,0:T(1,128)S(1)}, s32[1,8]{1,0:T(1,128)}, u32[]{:S(2)}) copy-start(s32[1,8]{1,0:T(1,128)} %param.29) | copy-start | bytes 100
  9.8 125.3 %collective-permute-start.32 = (bf16[1280,2048]{1,0:T(8,128)(2,1)}, bf16[1280,2048]{1,0:T(8,128)(2,1)}, u32[]{:S(2)}, u32[]{:S(2)}) collective-permute-start(bf16[1280,2048]{1,0:T(8,128)(2,1)} %get-tuple-element.286), channel_id=1, source_target_pairs={{16,0},{17,1},{18,2},{19,3},{20,4},{21,5},{22,6},{23,7},{24,8},{25... | collective-permute-start | bytes 15728648 | tf_op jit(solution)/shard_map/ppermute | solution.py:469
  11.0 137.6 %collective-permute-start.33 = (bf16[256,2048]{1,0:T(8,128)(2,1)}, bf16[256,2048]{1,0:T(8,128)(2,1)}, u32[]{:S(2)}, u32[]{:S(2)}) collective-permute-start(bf16[256,2048]{1,0:T(8,128)(2,1)} %get-tuple-element.287), channel_id=1, source_target_pairs={{16,0},{17,1},{18,2},{19,3},{20,4},{21,5},{22,6},{23,7},{24,8},{25... | collective-permute-start | bytes 3145736 | tf_op jit(solution)/shard_map/ppermute | solution.py:470
  26.3 1.4 collective-permute-start.13
  31.1 1.5 collective-permute-start.14
  33.3 11.9 %all-to-all-start.1 = ((bf16[8,48,256]{2,1,0:T(8,128)(2,1)}), bf16[8,48,256]{2,1,0:T(8,128)(2,1)S(1)}, u32[]{:S(2)}, u32[]{:S(2)}) async-start(bf16[8,48,256]{2,1,0:T(8,128)(2,1)} %bitcast.5), calls=%async_computation.1 | async-start | bytes 393216 | tf_op jit(solution)/shard_map/cond/branch_1_fun/all_to_all | solution.py:497
  57.5 1.4 collective-permute-start.15
  62.3 1.5 collective-permute-start.16
  64.5 11.9 %all-to-all-start.3 = ((bf16[8,48,256]{2,1,0:T(8,128)(2,1)}), bf16[8,48,256]{2,1,0:T(8,128)(2,1)S(1)}, u32[]{:S(2)}, u32[]{:S(2)}) async-start(bf16[8,48,256]{2,1,0:T(8,128)(2,1)} %bitcast.10), calls=%async_computation.3 | async-start | bytes 393216 | tf_op jit(solution)/shard_map/cond/branch_1_fun/all_to_all | solution.py:497
  77.4 4.2 %collective-permute-start.29 = (f32[128,256]{1,0:T(8,128)}, f32[128,256]{1,0:T(8,128)S(1)}, u32[]{:S(2)}, u32[]{:S(2)}) collective-permute-start(f32[128,256]{1,0:T(8,128)} %get-tuple-element.272), channel_id=1, source_target_pairs={{0,16},{1,17},{2,18},{3,19},{4,20},{5,21},{6,22},{7,23},{8,24},{9,... | collective-permute-start | bytes 393224 | tf_op jit(solution)/shard_map/ppermute | solution.py:628
  78.7 2.9 %copy-start.9 = (bf16[64,1024]{1,0:T(8,128)(2,1)S(1)}, bf16[64,1024]{1,0:T(8,128)(2,1)}, u32[]{:S(2)}) copy-start(bf16[64,1024]{1,0:T(8,128)(2,1)} %copy-done.8) | copy-start | bytes 393220
  82.6 10.8 %collective-permute-start.21 = (bf16[144,1024]{1,0:T(8,128)(2,1)S(1)}, bf16[144,1024]{1,0:T(8,128)(2,1)S(1)}, u32[]{:S(2)}, u32[]{:S(2)}) collective-permute-start(bf16[144,1024]{1,0:T(8,128)(2,1)S(1)} %branch_1_fun.16), channel_id=1, source_target_pairs={{0,12},{2,14},{4,0},{6,2},{8,4},{10,6},{12,8},{14,10},{1,13},{3,15... | collective-permute-start | bytes 884744 | tf_op jit(solution)/shard_map/cond/branch_1_fun/ppermute | solution.py:530
  86.0 12.8 %collective-permute-start.20 = (bf16[144,1024]{1,0:T(8,128)(2,1)S(1)}, bf16[144,1024]{1,0:T(8,128)(2,1)S(1)}, u32[]{:S(2)}, u32[]{:S(2)}) collective-permute-start(bf16[144,1024]{1,0:T(8,128)(2,1)S(1)} %branch_1_fun.16), channel_id=1, source_target_pairs={{0,4},{2,6},{4,8},{6,10},{8,12},{10,14},{12,0},{14,2},{1,5},{3,7},... | collective-permute-start | bytes 884744 | tf_op jit(solution)/shard_map/cond/branch_1_fun/ppermute | solution.py:530
  86.0 12.8 %collective-permute-start.19 = (bf16[144,1024]{1,0:T(8,128)(2,1)S(1)}, bf16[144,1024]{1,0:T(8,128)(2,1)S(1)}, u32[]{:S(2)}, u32[]{:S(2)}) collective-permute-start(bf16[144,1024]{1,0:T(8,128)(2,1)S(1)} %branch_1_fun.16), channel_id=1, source_target_pairs={{0,2},{2,0},{4,6},{6,4},{8,10},{10,8},{12,14},{14,12},{1,3},{3,1},... | collective-permute-start | bytes 884744 | tf_op jit(solution)/shard_map/cond/branch_1_fun/ppermute | solution.py:29
  98.8 14.8 %collective-permute-start.24 = (bf16[144,1024]{1,0:T(8,128)(2,1)S(1)}, bf16[144,1024]{1,0:T(8,128)(2,1)S(1)}, u32[]{:S(2)}, u32[]{:S(2)}) collective-permute-start(bf16[144,1024]{1,0:T(8,128)(2,1)S(1)} %branch_1_fun.16), channel_id=1, source_target_pairs={{0,8},{2,10},{4,12},{6,14},{8,0},{10,2},{12,4},{14,6},{1,9},{3,11}... | collective-permute-start | bytes 884744 | tf_op jit(solution)/shard_map/cond/branch_1_fun/ppermute | solution.py:530
  98.8 18.4 %collective-permute-start.22 = (bf16[144,1024]{1,0:T(8,128)(2,1)S(1)}, bf16[144,1024]{1,0:T(8,128)(2,1)S(1)}, u32[]{:S(2)}, u32[]{:S(2)}) collective-permute-start(bf16[144,1024]{1,0:T(8,128)(2,1)S(1)} %collective-permute-done.20), channel_id=1, source_target_pairs={{0,2},{2,0},{4,6},{6,4},{8,10},{10,8},{12,14},{14,12},{1,3},{3,1},... | collective-permute-start | bytes 884744 | tf_op jit(solution)/shard_map/cond/branch_1_fun/ppermute | solution.py:29
  100.4 16.7 %collective-permute-start.23 = (bf16[144,1024]{1,0:T(8,128)(2,1)S(1)}, bf16[144,1024]{1,0:T(8,128)(2,1)S(1)}, u32[]{:S(2)}, u32[]{:S(2)}) collective-permute-start(bf16[144,1024]{1,0:T(8,128)(2,1)S(1)} %collective-permute-done.21), channel_id=1, source_target_pairs={{0,2},{2,0},{4,6},{6,4},{8,10},{10,8},{12,14},{14,12},{1,3},{3,1},... | collective-permute-start | bytes 884744 | tf_op jit(solution)/shard_map/cond/branch_1_fun/ppermute | solution.py:29
  113.6 7.8 %collective-permute-start.25 = (bf16[144,1024]{1,0:T(8,128)(2,1)S(1)}, bf16[144,1024]{1,0:T(8,128)(2,1)S(1)}, u32[]{:S(2)}, u32[]{:S(2)}) collective-permute-start(bf16[144,1024]{1,0:T(8,128)(2,1)S(1)} %collective-permute-done.24), channel_id=1, source_target_pairs={{0,2},{2,0},{4,6},{6,4},{8,10},{10,8},{12,14},{14,12},{1,3},{3,1},... | collective-permute-start | bytes 884744 | tf_op jit(solution)/shard_map/cond/branch_1_fun/ppermute | solution.py:29
  122.3 4.8 %copy-start.2 = (bf16[576,1024]{1,0:T(8,128)(2,1)S(1)}, bf16[576,1024]{1,0:T(8,128)(2,1)}, u32[]{:S(2)}) copy-start(bf16[576,1024]{1,0:T(8,128)(2,1)} %get-tuple-element.211.refs_0_) | copy-start | bytes 3538948 | tf_op jit(solution)/shard_map/cond
  122.3 4.7 %collective-permute-start.3 = (bf16[576,1024]{1,0:T(8,128)(2,1)}, bf16[576,1024]{1,0:T(8,128)(2,1)S(1)}, u32[]{:S(2)}, u32[]{:S(2)}) collective-permute-start(bf16[576,1024]{1,0:T(8,128)(2,1)} %get-tuple-element.211.refs_0_), channel_id=1, source_target_pairs={{0,1},{1,0},{2,3},{3,2},{4,5},{5,4},{6,7},{7,6},{8,9},{9,8},{10,11... | collective-permute-start | bytes 3538952 | tf_op jit(solution)/shard_map/cond/branch_1_fun/ppermute | solution.py:25
  122.3 3.9 %collective-permute-start.4 = (bf16[288,1024]{1,0:T(8,128)(2,1)}, bf16[288,1024]{1,0:T(8,128)(2,1)S(1)}, u32[]{:S(2)}, u32[]{:S(2)}) collective-permute-start(bf16[288,1024]{1,0:T(8,128)(2,1)} %get-tuple-element.212.refs_1_), channel_id=1, source_target_pairs={{0,1},{1,0},{2,3},{3,2},{4,5},{5,4},{6,7},{7,6},{8,9},{9,8},{10,11... | collective-permute-start | bytes 1769480 | tf_op jit(solution)/shard_map/cond/branch_1_fun/ppermute | solution.py:25
  122.8 4.2 %collective-permute-start.5 = (bf16[288,1024]{1,0:T(8,128)(2,1)}, bf16[288,1024]{1,0:T(8,128)(2,1)S(1)}, u32[]{:S(2)}, u32[]{:S(2)}) collective-permute-start(bf16[288,1024]{1,0:T(8,128)(2,1)} %get-tuple-element.213.refs_2_), channel_id=1, source_target_pairs={{0,1},{1,0},{2,3},{3,2},{4,5},{5,4},{6,7},{7,6},{8,9},{9,8},{10,11... | collective-permute-start | bytes 1769480 | tf_op jit(solution)/shard_map/cond/branch_1_fun/ppermute | solution.py:25
  122.8 4.2 %copy-start.3 = (bf16[288,1024]{1,0:T(8,128)(2,1)S(1)}, bf16[288,1024]{1,0:T(8,128)(2,1)}, u32[]{:S(2)}) copy-start(bf16[288,1024]{1,0:T(8,128)(2,1)} %get-tuple-element.212.refs_1_) | copy-start | bytes 1769476 | tf_op jit(solution)/shard_map/cond
  122.8 4.2 %copy-start.4 = (bf16[288,1024]{1,0:T(8,128)(2,1)S(1)}, bf16[288,1024]{1,0:T(8,128)(2,1)}, u32[]{:S(2)}) copy-start(bf16[288,1024]{1,0:T(8,128)(2,1)} %get-tuple-element.213.refs_2_) | copy-start | bytes 1769476 | tf_op jit(solution)/shard_map/cond
  130.1 1.5 collective-permute-start.30
  131.6 0.6 copy-start.15
  133.8 23.0 %collective-permute-start.31 = (bf16[32,1024]{1,0:T(8,128)(2,1)}, bf16[32,1024]{1,0:T(8,128)(2,1)S(1)}, u32[]{:S(2)}, u32[]{:S(2)}) collective-permute-start(bf16[32,1024]{1,0:T(8,128)(2,1)} %get-tuple-element.281), channel_id=1, source_target_pairs={{16,0},{17,1},{18,2},{19,3},{20,4},{21,5},{22,6},{23,7},{24,8},{25... | collective-permute-start | bytes 196616 | tf_op jit(solution)/shard_map/ppermute | solution.py:683
  148.7 8.1 %copy-start.14 = (bf16[32,1024]{1,0:T(8,128)(2,1)S(1)}, bf16[32,1024]{1,0:T(8,128)(2,1)}, u32[]{:S(2)}) copy-start(bf16[32,1024]{1,0:T(8,128)(2,1)} %get-tuple-element.291) | copy-start | bytes 196612

commit v5 on v4

--- a/solution.py
+++ b/solution.py
@@ -351,17 +351,55 @@
     wait_all(in_copies + grad_copies)
 
 
-def late_kernel(features, hidden, tile, places, go_ref, weight_ref, *refs):
-    inputs_ref, grads_ref, up_ref, down_ref, _, _, new_up_ref, new_down_ref, row_sems, *space = refs
-    count, to, up_at, down_at = places
+def late_kernel(features, hidden, tile, count, go_ref, weight_ref, *refs):
+    inputs_ref, grads_ref, piece_ref, _, _, new_up_ref, new_down_ref, slopes_ref, gradient_ref = refs[:9]
+    row_sems, ahead, slopes, gradient, ahead_sems, *space = refs[9:]
+    hidden_here = new_up_ref.shape[0]
 
     @pl.when(go_ref[0] == 1)
     def _():
+        ahead_copy = pltpu.make_async_copy(piece_ref.at[pl.ds(count, tile)], ahead, ahead_sems.at[0])
         in_copies = [pltpu.make_async_copy(inputs_ref, space[0], row_sems.at[0])]
         grad_copies = [pltpu.make_async_copy(grads_ref, space[1], row_sems.at[1])]
-        rows = [up_ref.at[pl.ds(up_at, count)], down_ref.at[pl.ds(down_at, count)]]
-        rows = rows + [ref.at[pl.ds(to, count)] for ref in (new_up_ref, new_down_ref)]
+        rows = [piece_ref.at[pl.ds(start, count)] for start in (0, hidden_here)]
+        rows = rows + [ref.at[pl.ds(0, count)] for ref in (new_up_ref, new_down_ref)]
+        ahead_copy.start()
         update_rows(features, hidden, tile, weight_ref[...], in_copies, grad_copies, *rows, space)
+        ahead_copy.wait()
+        activated, slopes[...] = activation(features, ahead[...], space[0][...], weight_ref[...])
+        gradient[...] = dot(activated, space[1][...])
+        outs = [
+            pltpu.make_async_copy(slopes, slopes_ref, ahead_sems.at[1]),
+            pltpu.make_async_copy(gradient, gradient_ref, ahead_sems.at[2]),
+        ]
+        start_all(outs)
+        wait_all(outs)
+
+
+def last_kernel(features, hidden, go_ref, *refs):
+    inputs_ref, grads_ref, first_ref, down_ref, slopes_ref, gradient_ref, _, _, new_up_ref, new_down_ref = refs[:10]
+    inputs, grads, up, down, slopes, gradient, new_up, new_down, sems, out_sems = refs[10:]
+    tile = down_ref.shape[0]
+    place = pl.ds(new_up_ref.shape[0] - tile, tile)
+
+    @pl.when(go_ref[0] == 1)
+    def _():
+        moves = [(down_ref, down), (grads_ref, grads), (slopes_ref, slopes), (inputs_ref, inputs)]
+        moves = moves + [(first_ref.at[place], up), (gradient_ref, gradient)]
+        copies = [pltpu.make_async_copy(a, b, sems.at[i]) for i, (a, b) in enumerate(moves)]
+        up_out = pltpu.make_async_copy(new_up, new_up_ref.at[place], out_sems.at[0])
+        down_out = pltpu.make_async_copy(new_down, new_down_ref.at[place], out_sems.at[1])
+        start_all(copies)
+        wait_all(copies[:3])
+        hidden_grad = dot(down[...], grads[...], nt_dims) * hidden ** (-0.5)
+        pre_grad = (hidden_grad * slopes[...]).astype(bf16)
+        wait_all(copies[3:5])
+        new_up[...] = new_tile(up[...], features ** (-0.5), pre_grad, inputs[...])
+        up_out.start()
+        copies[5].wait()
+        new_down[...] = (down[...].astype(f32) - (step_size * hidden ** (-0.5)) * gradient[...]).astype(bf16)
+        down_out.start()
+        wait_all([up_out, down_out])
 
 
 def hold_kernel(go_ref, array_ref, held_ref, sem):
@@ -390,13 +428,14 @@
     pass
 
 
-def unset(*like):
+def unset(after, *like):
     arrays = pl.pallas_call(
         unset_kernel,
         out_shape=[jax.ShapeDtypeStruct(a.shape, a.dtype) for a in like],
+        in_specs=[anywhere],
         out_specs=[anywhere] * len(like),
         cost_estimate=costs(1, 1),
-    )()
+    )(after)
     return tuple(arrays)
 
 
@@ -586,26 +625,52 @@
             cost_estimate=costs(1, 1),
         )(part_ref, weights, *units, up_mat, down_mat)
 
-    def update_late(count, places, piece, new_up, new_down):
+    slopes_like = jax.ShapeDtypeStruct((tile, gathered), f32)
+    gradient_like = jax.ShapeDtypeStruct((tile, features), f32)
+
+    def spaces(*like):
+        return [pltpu.VMEM(a.shape, a.dtype) for a in like]
+
+    def update_late(new_up, new_down):
+        piece_like = jax.ShapeDtypeStruct((tile, features), bf16)
         return pl.pallas_call(
-            functools.partial(late_kernel, features, hidden, tile, (count, *places)),
+            functools.partial(late_kernel, features, hidden, tile, 2 * tile),
+            out_shape=[weight_like] * 2 + [slopes_like, gradient_like],
+            in_specs=[smem, vmem] + [stays] * 5,
+            out_specs=[anywhere] * 4,
+            scratch_shapes=[sems_of(2)]
+            + spaces(piece_like, slopes_like, gradient_like)
+            + [sems_of(3)]
+            + update_space(2 * tile),
+            input_output_aliases={5: 0, 6: 1},
+            compiler_params=fits(60),
+            cost_estimate=costs(1, 1),
+        )(go, weights, inputs, grads, first_there, new_up, new_down)
+
+    def update_last(slopes, gradient, new_up, new_down):
+        piece_like = jax.ShapeDtypeStruct((tile, features), bf16)
+        return pl.pallas_call(
+            functools.partial(last_kernel, features, hidden),
             out_shape=[weight_like] * 2,
-            in_specs=[smem, vmem] + [stays] * 6,
+            in_specs=[smem] + [stays] * 8,
             out_specs=[anywhere] * 2,
-            scratch_shapes=[sems_of(2)] + update_space(count),
-            input_output_aliases={6: 0, 7: 1},
+            scratch_shapes=spaces(rows_like, rows_like, piece_like, piece_like, slopes_like, gradient_like)
+            + spaces(piece_like, piece_like)
+            + [sems_of(6), sems_of(2)],
+            input_output_aliases={7: 0, 8: 1},
             compiler_params=fits(60),
             cost_estimate=costs(1, 1),
-        )(go, weights, inputs, grads, first_there, piece, new_up, new_down)
-
-    final_like = jax.ShapeDtypeStruct((stacked, lanes), bf16)
+        )(go, inputs, grads, first_there, second_there, slopes, gradient, new_up, new_down)
+
+    half_like = jax.ShapeDtypeStruct((row_count, features // 2), bf16)
     block_rows = height * max(1, experts // line)
     gather_like = [jax.ShapeDtypeStruct((block_rows * n, share), bf16) for n in (line // 2, line // 2 - 2, 2)]
 
     sources = []
 
     def first_rollout():
-        return decode_step(0, states, payload, up_here, down_here) + unset(*gather_like)
+        now, sent = decode_step(0, states, payload, up_here, down_here)
+        return (now, sent) + unset(sent, *gather_like)
 
     def first_learner():
         units, places = learner_rows([crossed_rows, own_rows])
@@ -618,7 +683,7 @@
         now, sent = states, payload
         for step in range(1, half_steps):
             now, sent = decode_step(step, now, sent, up_here, down_here)
-        return (now,) + tuple(unset(up_here, down_here))
+        return (now,) + unset(now, up_here, down_here)
 
     def second_learner():
         units, weights = with_parts(rows, sources[0])
@@ -647,7 +712,8 @@
             compiler_params=fits(16),
             cost_estimate=costs(1, 1),
         )(targets, states_there)
-        return decode_step(half_steps, states_there, sent, held_up, new_down) + unset(*gather_like)
+        now, sent = decode_step(half_steps, states_there, sent, held_up, new_down)
+        return (now, sent) + unset(sent, *gather_like)
 
     states, payload, *rows = lax.cond(is_rollout, third_rollout, third_learner)
 
@@ -658,30 +724,30 @@
             out_shape=[rows_like] * 2,
             in_specs=[smem] + [anywhere] * len(units),
             scratch_shapes=[sems_of(2 * parts * experts)],
-            compiler_params=fits(32),
+            compiler_params=fits(62),
             cost_estimate=costs(1, 1),
         )(part_ref, *units)
-        return unset(final_like) + tuple(whole) + (weights,)
+        return unset(weights, half_like, half_like) + tuple(whole) + (weights,)
 
     def fourth_learner():
         now, sent = states, payload
         for step in range(half_steps + 1, steps):
             now, sent = decode_step(step, now, sent, held_up, new_down)
-        return (sent,) + unset(rows_like, rows_like, weights_like)
-
-    mine, inputs, grads, weights = lax.cond(is_rollout, fourth_rollout, fourth_learner)
-
-    pieces = [mine] + [shifted(mine, "dp", j) for j in range(1, parts)]
-    left, right = pl.pallas_call(
-        functools.partial(join_kernel, parts, row_count),
-        out_shape=[jax.ShapeDtypeStruct((row_count, features // 2), bf16)] * 2,
-        in_specs=[smem] + [vmem] * parts,
-        scratch_shapes=[pltpu.VMEM((row_count, features), bf16)],
-        cost_estimate=costs(1, 1),
-    )(part_ref, *pieces)
-    new_up, new_down = update_late(2 * tile, (0, 0, hidden_here), first_there, new_up, new_down)
+        pieces = [sent] + [shifted(sent, "dp", j) for j in range(1, parts)]
+        left, right = pl.pallas_call(
+            functools.partial(join_kernel, parts, row_count),
+            out_shape=[half_like] * 2,
+            in_specs=[smem] + [vmem] * parts,
+            scratch_shapes=[pltpu.VMEM((row_count, features), bf16)],
+            cost_estimate=costs(1, 1),
+        )(part_ref, *pieces)
+        return (left, right) + unset(left, rows_like, rows_like, weights_like)
+
+    left, right, inputs, grads, weights = lax.cond(is_rollout, fourth_rollout, fourth_learner)
+
+    new_up, new_down, slopes, gradient = update_late(new_up, new_down)
     delivered = lax.ppermute(left, "sect", [(1, 0)])
-    new_up, new_down = update_late(tile, (2 * tile, 2 * tile, 0), second_there, new_up, new_down)
+    new_up, new_down = update_last(slopes, gradient, new_up, new_down)
     right, new_up = lax.optimization_barrier((right, new_up))
     final_states = jnp.where(is_rollout, delivered, right)
     return final_states, new_up[None, None], new_down[None, None]

time: 158 us -> 155 us (0.981)
  waiting for transfers between devices: 65.4 us -> 59.8 us
  Pallas kernels: 33.3 us -> 36.7 us
    ppermute x1, waiting for transfers between devices: 2.32 us -> 0.01 us  [on_device(): delivered = lax.ppermute(left, 'sect', [(1, 0)])]
    ppermute x8 -> x7, waiting for transfers between devices: 9.45 us -> 7.7 us  [shifted(): lax.ppermute(array, axis, [(i, (i + by) % size) for i in range(size)])]
    ppermute x1, waiting for transfers between devices: 4.65 us -> 2.92 us  [on_device(): second_there = lax.ppermute(second_piece, 'sect', [(1, 0)])]
    pallas_call x3 -> x2, Pallas kernels: 16.2 us -> 17.9 us  [the longest x1 12.9 us: update_late(): pl.pallas_call(functools.partial(late_kernel, features, hidden, tile, 2 *...]
  transfers between devices with their start and end apart: 22 -> 21, of which waited for: 17 -> 15; matrix products, arithmetic and copies ran while one was open for 4% -> 5% of each run, Pallas kernels for 20% -> 22%
where the time goes in v5:
time: 155 us; the launch traced here: 154 us
  waiting for transfers between devices  59.8 us (39%)
  Pallas kernels  36.7 us (24%)
  blocking collectives  25 us (16%)
  starting transfers between devices  24.3 us (16%)
  other arithmetic  4.96 us (3%)
  local copies, waits for them, and re-layouts  2.76 us (2%)
    all_to_all x2, blocking collectives, decode_step(): lax.all_to_all(payload, 'exp', split_axis=0, concat_axis=0, tiled=True)  25 us
    ppermute x3, waiting for transfers between devices, along(): return lax.ppermute(array, 'exp', pairs)  24 us
    all_to_all x2, waiting for transfers between devices, decode_step(): lax.all_to_all(summed, 'exp', split_axis=0, concat_axis=0, tiled=True)  15.2 us
    pallas_call x1, Pallas kernels, update_late(): pl.pallas_call(functools.partial(late_kernel, features, hidden, tile, 2 *...  12.9 us
    ppermute x5, starting transfers between devices, flipped(): lax.ppermute(array, axis, [(i, i ^ bit) for i in range(lax.axis_size(axis...  8.07 us
    ppermute x7, waiting for transfers between devices, shifted(): lax.ppermute(array, axis, [(i, (i + by) % size) for i in range(size)])  7.7 us
    ppermute x5, waiting for transfers between devices, flipped(): lax.ppermute(array, axis, [(i, i ^ bit) for i in range(lax.axis_size(axis...  6.87 us
    all_to_all x2, starting transfers between devices, decode_step(): lax.all_to_all(summed, 'exp', split_axis=0, concat_axis=0, tiled=True)  6.78 us
  transfers between devices with their start and end apart: 21, of which 15 were waited for; matrix products, arithmetic and copies ran while one was open for 5% of the time, Pallas kernels for 22%

profile of v5, /device:TPU:0, one launch (start us, length us, event | category | flops | bytes accessed | tf_op | source)
XLA Modules:
  0.0 154.4 jit_solution(18343936754575187125)
XLA Ops:
  0.6 2.5 %shard_map.139 = (s32[4,2,128]{2,1,0:T(2,128)S(1)}, f32[8,128]{1,0:T(8,128)S(1)}, f32[128,256]{1,0:T(8,128)}, bf16[384,256]{1,0:T(8,128)(2,1)}, bf16[64,1024]{1,0:T(8,128)(2,1)S(1)}) custom-call(s32[1]{0:T(128)} %bitcast.24.part_ref, s32[8,32]{1,0:T(8,128)} %bitcast.68, f32[8,32]{1,0:T(8,128)} %bitcast.69, bf16[32,2048]{1,0:T(8,128)(2,1)} %all_rows_ref.1, ...), custom_call_target="tpu_custom_call" | custom-call | flops 1 | bytes 1 | tf_op jit(solution)/shard_map/pallas_call | solution.py:480
  3.2 3.0 %collective-permute-start.29 = (bf16[64,1024]{1,0:T(8,128)(2,1)S(1)}, bf16[64,1024]{1,0:T(8,128)(2,1)}, u32[]{:S(2)}, u32[]{:S(2)}) collective-permute-start(bf16[64,1024]{1,0:T(8,128)(2,1)S(1)} %get-tuple-element.263), channel_id=1, source_target_pairs={{0,16},{16,0},{1,17},{17,1},{2,18},{18,2},{3,19},{19,3},{4,20},{20... | collective-permute-start | bytes 393224 | tf_op jit(solution)/shard_map/ppermute | solution.py:29
  6.2 0.0 copy-start.14
  6.2 0.0 copy-start.15
  6.2 0.1 shard_map.140
  6.3 3.5 %collective-permute-done.29 = bf16[64,1024]{1,0:T(8,128)(2,1)} collective-permute-done((bf16[64,1024]{1,0:T(8,128)(2,1)S(1)}, bf16[64,1024]{1,0:T(8,128)(2,1)}, u32[]{:S(2)}, u32[]{:S(2)}) %collective-permute-start.29) | collective-permute-done | bytes 131104 | tf_op jit(solution)/shard_map/ppermute | solution.py:29
  9.8 1.3 collective-permute-start.32
  11.1 1.3 collective-permute-start.33
  12.4 34.0 %conditional.4 = (f32[128,256]{1,0:T(8,128)}, bf16[384,256]{1,0:T(8,128)(2,1)}, bf16[576,1024]{1,0:T(8,128)(2,1)}, bf16[288,1024]{1,0:T(8,128)(2,1)}, bf16[288,1024]{1,0:T(8,128)(2,1)}) conditional(s32[]{:T(128)} %convert_element_type.43, (s32[128,2]{0,1:T(2,128)S(1)}, f32[128,2]{0,1:T(2,128)S(1)}, s32[1,2,4]{2,1,0:T(2,128)S(1)}, ...), branch_computations={%region_0.0_spmd, %region_1.0_spmd} | conditional | flops 7077889 | bytes 12976449 | solution.py:680
  12.5 13.9 %all_to_all.64 = bf16[8,48,256]{2,1,0:T(8,128)(2,1)S(1)} all-to-all(bf16[8,48,256]{2,1,0:T(8,128)(2,1)} %bitcast.3), channel_id=1, replica_groups=mesh['sect'=2,'exp'=8,'dp'=2] {'exp'}, dimensions={0} | all-to-all | bytes 393216 | tf_op jit(solution)/shard_map/cond/branch_1_fun/all_to_all | solution.py:531
  26.3 0.0 collective-permute-start.13
  26.3 1.4 collective-permute-done.13.refs_1_
  27.8 3.3 %branch_1_fun.10 = (bf16[384,256]{1,0:T(8,128)(2,1)S(1)}, bf16[384,256]{1,0:T(8,128)(2,1)S(1)}) custom-call(s32[1]{0:T(128)} %get-tuple-element.135.part_ref, f32[1,2048]{1,0:T(1,128)S(1)} %get-tuple-element.136.gain_ref, bf16[384,256]{1,0:T(8,128)(2,1)S(1)} %bitcast.47, bf16[384,256]{1,0:T(8,128)(2,1)S(1)} %collective-permute-done.13.refs_1_, ...), custom_call_target="tpu_custom_call" | custom-call | flops 1 | bytes 1 | tf_op jit(solution)/shard_map/cond/branch_1_fun/pallas_call | solution.py:513
  31.1 0.2 collective-permute-start.14
  31.3 1.3 collective-permute-done.14
  32.6 0.7 add_convert_fusion
  33.3 3.4 %all-to-all-start.1 = ((bf16[8,48,256]{2,1,0:T(8,128)(2,1)}), bf16[8,48,256]{2,1,0:T(8,128)(2,1)S(1)}, u32[]{:S(2)}, u32[]{:S(2)}) async-start(bf16[8,48,256]{2,1,0:T(8,128)(2,1)} %bitcast.5), calls=%async_computation.1 | async-start | bytes 393216 | tf_op jit(solution)/shard_map/cond/branch_1_fun/all_to_all | solution.py:536
  36.7 0.9 copy.61.states_ref
  37.7 7.6 %all-to-all-done.1 = bf16[8,48,256]{2,1,0:T(8,128)(2,1)S(1)} async-done(((bf16[8,48,256]{2,1,0:T(8,128)(2,1)}), bf16[8,48,256]{2,1,0:T(8,128)(2,1)S(1)}, u32[]{:S(2)}, u32[]{:S(2)}) %all-to-all-start.1) | async-done | bytes 196640 | tf_op jit(solution)/shard_map/cond/branch_1_fun/all_to_all | solution.py:536
  45.2 1.2 branch_1_fun.11
  46.5 30.9 %conditional.5 = (f32[128,256]{1,0:T(8,128)}, bf16[768,2048]{1,0:T(8,128)(2,1)}, bf16[768,2048]{1,0:T(8,128)(2,1)}) conditional(s32[]{:T(128)} %convert_element_type.43, (s32[]{:T(128)}, bf16[576,1024]{1,0:T(8,128)(2,1)}, bf16[288,1024]{1,0:T(8,128)(2,1)}, bf16[288,1024]{1,0:T(8,128)(2,1)}, s32[1]{0:T(128)}, ...), branch_computations={%region_2.0_spmd, %region_3.0_spmd} | conditional | flops 393219 | bytes 18882816 | solution.py:692
  46.5 11.1 %all_to_all.65 = bf16[8,48,256]{2,1,0:T(8,128)(2,1)S(1)} all-to-all(bf16[8,48,256]{2,1,0:T(8,128)(2,1)} %bitcast.8), channel_id=1, replica_groups=mesh['sect'=2,'exp'=8,'dp'=2] {'exp'}, dimensions={0} | all-to-all | bytes 393216 | tf_op jit(solution)/shard_map/cond/branch_1_fun/all_to_all | solution.py:531
  57.5 0.0 collective-permute-start.15
  57.5 1.4 collective-permute-done.15.refs_1_
  59.0 3.3 %branch_1_fun.13 = (bf16[384,256]{1,0:T(8,128)(2,1)S(1)}, bf16[384,256]{1,0:T(8,128)(2,1)S(1)}) custom-call(s32[1]{0:T(128)} %get-tuple-element.160.part_ref, f32[1,2048]{1,0:T(1,128)S(1)} %get-tuple-element.161.gain_ref, bf16[384,256]{1,0:T(8,128)(2,1)S(1)} %bitcast.49, bf16[384,256]{1,0:T(8,128)(2,1)S(1)} %collective-permute-done.15.refs_1_, ...), custom_call_target="tpu_custom_call" | custom-call | flops 1 | bytes 1 | tf_op jit(solution)/shard_map/cond/branch_1_fun/pallas_call | solution.py:513
  62.3 0.2 collective-permute-start.16
  62.5 1.3 collective-permute-done.16
  63.8 0.7 add_convert_fusion.1
  64.5 3.4 %all-to-all-start.3 = ((bf16[8,48,256]{2,1,0:T(8,128)(2,1)}), bf16[8,48,256]{2,1,0:T(8,128)(2,1)S(1)}, u32[]{:S(2)}, u32[]{:S(2)}) async-start(bf16[8,48,256]{2,1,0:T(8,128)(2,1)} %bitcast.10), calls=%async_computation.3 | async-start | bytes 393216 | tf_op jit(solution)/shard_map/cond/branch_1_fun/all_to_all | solution.py:536
  67.9 0.9 copy.62.states_ref
  68.9 7.6 %all-to-all-done.3 = bf16[8,48,256]{2,1,0:T(8,128)(2,1)S(1)} async-done(((bf16[8,48,256]{2,1,0:T(8,128)(2,1)}), bf16[8,48,256]{2,1,0:T(8,128)(2,1)S(1)}, u32[]{:S(2)}, u32[]{:S(2)}) %all-to-all-start.3) | async-done | bytes 196640 | tf_op jit(solution)/shard_map/cond/branch_1_fun/all_to_all | solution.py:536
  76.4 1.0 branch_1_fun.14
  77.4 1.3 collective-permute-start.30
  78.7 3.2 %collective-permute-done.30 = f32[128,256]{1,0:T(8,128)S(1)} collective-permute-done((f32[128,256]{1,0:T(8,128)}, f32[128,256]{1,0:T(8,128)S(1)}, u32[]{:S(2)}, u32[]{:S(2)}) %collective-permute-start.30) | collective-permute-done | bytes 131104 | tf_op jit(solution)/shard_map/ppermute | solution.py:693
  81.9 40.5 %conditional.6 = (f32[128,256]{1,0:T(8,128)S(1)}, bf16[384,256]{1,0:T(8,128)(2,1)}, bf16[576,1024]{1,0:T(8,128)(2,1)}, bf16[288,1024]{1,0:T(8,128)(2,1)}, bf16[288,1024]{1,0:T(8,128)(2,1)}) conditional(s32[]{:T(128)} %convert_element_type.43, (s32[4,2,128]{2,1,0:T(2,128)S(1)}, f32[128,256]{1,0:T(8,128)S(1)}, s32[1]{0:T(128)}, ...), branch_computations={%region_4.0_spmd, %region_5.0_spmd} | conditional | flops 7077889 | bytes 13238593 | solution.py:718
  81.9 1.1 branch_1_fun.16
  82.9 3.2 %collective-permute-start.21 = (bf16[144,1024]{1,0:T(8,128)(2,1)S(1)}, bf16[144,1024]{1,0:T(8,128)(2,1)S(1)}, u32[]{:S(2)}, u32[]{:S(2)}) collective-permute-start(bf16[144,1024]{1,0:T(8,128)(2,1)S(1)} %branch_1_fun.16), channel_id=1, source_target_pairs={{0,12},{2,14},{4,0},{6,2},{8,4},{10,6},{12,8},{14,10},{1,13},{3,15... | collective-permute-start | bytes 884744 | tf_op jit(solution)/shard_map/cond/branch_1_fun/ppermute | solution.py:569
  86.1 0.0 collective-permute-start.20
  86.1 1.5 collective-permute-start.19
  87.7 5.9 %collective-permute-done.21 = bf16[144,1024]{1,0:T(8,128)(2,1)S(1)} collective-permute-done((bf16[144,1024]{1,0:T(8,128)(2,1)S(1)}, bf16[144,1024]{1,0:T(8,128)(2,1)S(1)}, u32[]{:S(2)}, u32[]{:S(2)}) %collective-permute-start.21) | collective-permute-done | bytes 294944 | tf_op jit(solution)/shard_map/cond/branch_1_fun/ppermute | solution.py:569
  93.6 5.3 %collective-permute-done.20 = bf16[144,1024]{1,0:T(8,128)(2,1)S(1)} collective-permute-done((bf16[144,1024]{1,0:T(8,128)(2,1)S(1)}, bf16[144,1024]{1,0:T(8,128)(2,1)S(1)}, u32[]{:S(2)}, u32[]{:S(2)}) %collective-permute-start.20) | collective-permute-done | bytes 294944 | tf_op jit(solution)/shard_map/cond/branch_1_fun/ppermute | solution.py:569
  98.9 0.1 collective-permute-start.24
  99.0 1.5 collective-permute-start.22
  100.6 0.5 collective-permute-start.23
  101.0 12.7 %collective-permute-done.24 = bf16[144,1024]{1,0:T(8,128)(2,1)S(1)} collective-permute-done((bf16[144,1024]{1,0:T(8,128)(2,1)S(1)}, bf16[144,1024]{1,0:T(8,128)(2,1)S(1)}, u32[]{:S(2)}, u32[]{:S(2)}) %collective-permute-start.24) | collective-permute-done | bytes 294944 | tf_op jit(solution)/shard_map/cond/branch_1_fun/ppermute | solution.py:569
  113.7 1.5 collective-permute-start.25
  115.3 0.9 copy.40
  116.2 1.1 pad_maximum_fusion.3
  117.3 0.0 collective-permute-done.22
  117.3 0.9 pad_maximum_fusion.4
  118.2 3.4 %collective-permute-done.25 = bf16[144,1024]{1,0:T(8,128)(2,1)S(1)} collective-permute-done((bf16[144,1024]{1,0:T(8,128)(2,1)S(1)}, bf16[144,1024]{1,0:T(8,128)(2,1)S(1)}, u32[]{:S(2)}, u32[]{:S(2)}) %collective-permute-start.25) | collective-permute-done | bytes 294944 | tf_op jit(solution)/shard_map/cond/branch_1_fun/ppermute | solution.py:29
  121.5 0.9 pad_maximum_fusion.5
  122.4 9.1 %conditional.7 = (bf16[32,1024]{1,0:T(8,128)(2,1)S(1)}, bf16[32,1024]{1,0:T(8,128)(2,1)S(1)}, bf16[512,2048]{1,0:T(8,128)(2,1)}, bf16[512,2048]{1,0:T(8,128)(2,1)}, f32[1,512]{1,0:T(1,128)}) conditional(s32[]{:T(128)} %convert_element_type.43, (bf16[384,256]{1,0:T(8,128)(2,1)}, s32[1]{0:T(128)}, f32[1,2048]{1,0:T(1,128)S(1)}, ...), branch_computations={%region_6.0_spmd, %region_7.0_spmd} | conditional | flops 393220 | bytes 16515291 | solution.py:746
  122.4 0.5 collective-permute-start.4
  122.9 0.1 collective-permute-start.5
  123.0 2.0 %branch_1_fun.17.refs_0_ = f32[1,512]{1,0:T(1,128)} custom-call(s32[1]{0:T(128)} %bitcast.23.me_ref, bf16[576,1024]{1,0:T(8,128)(2,1)} %get-tuple-element.213.refs_0_, bf16[288,1024]{1,0:T(8,128)(2,1)} %get-tuple-element.214.refs_1_, bf16[288,1024]{1,0:T(8,128)(2,1)} %get-tuple-element.215.refs_2_), custom_call_target="tpu_custom_call" | custom-call | flops 1 | bytes 1 | tf_op jit(solution)/shard_map/cond/branch_1_fun/pallas_call | solution.py:589
  125.1 1.4 collective-permute-done.4.refs_4_
  126.5 0.8 collective-permute-done.5.refs_5_
  127.3 4.2 %branch_1_fun.19 = (bf16[512,2048]{1,0:T(8,128)(2,1)}, bf16[512,2048]{1,0:T(8,128)(2,1)}) custom-call(s32[1]{0:T(128)} %get-tuple-element.218.part_ref, bf16[576,1024]{1,0:T(8,128)(2,1)S(1)} %copy-done.3, bf16[288,1024]{1,0:T(8,128)(2,1)S(1)} %copy-done.4, bf16[288,1024]{1,0:T(8,128)(2,1)} %get-tuple-element.215.refs_2_, ...), custom_call_target="tpu_custom_call" | custom-call | flops 1 | bytes 1 | tf_op jit(solution)/shard_map/cond/branch_1_fun/pallas_call | solution.py:722
  131.6 1.3 collective-permute-start.31
  132.9 12.9 %shard_map.142 = (bf16[768,2048]{1,0:T(8,128)(2,1)}, bf16[768,2048]{1,0:T(8,128)(2,1)}, f32[256,512]{1,0:T(8,128)}, f32[256,2048]{1,0:T(8,128)}) custom-call(s32[1]{0:T(128)} %bitcast.31.go_ref, f32[1,512]{1,0:T(1,128)} %get-tuple-element.291.weight_ref, bf16[512,2048]{1,0:T(8,128)(2,1)} %get-tuple-element.287.refs_0_, ...), custom_call_target="tpu_custom_call", output_to_operand_aliasing={{0}: (5, {}), {1}: (6, {})} | custom-call | flops 1 | bytes 1 | tf_op jit(solution)/shard_map/pallas_call | solution.py:636
  145.8 2.9 %collective-permute-done.33.refs_3_ = bf16[256,2048]{1,0:T(8,128)(2,1)} collective-permute-done((bf16[256,2048]{1,0:T(8,128)(2,1)}, bf16[256,2048]{1,0:T(8,128)(2,1)}, u32[]{:S(2)}, u32[]{:S(2)}) %collective-permute-start.33) | collective-permute-done | bytes 1048608 | tf_op jit(solution)/shard_map/ppermute | solution.py:509
  148.7 5.0 %shard_map.143 = (bf16[768,2048]{1,0:T(8,128)(2,1)}, bf16[768,2048]{1,0:T(8,128)(2,1)}) custom-call(s32[1]{0:T(128)} %bitcast.31.go_ref, bf16[512,2048]{1,0:T(8,128)(2,1)} %get-tuple-element.287.refs_0_, bf16[512,2048]{1,0:T(8,128)(2,1)} %get-tuple-element.288.refs_1_, ...), custom_call_target="tpu_custom_call", output_to_operand_aliasing={{0}: (7, {}), {1}: (8, {})} | custom-call | flops 1 | bytes 1 | tf_op jit(solution)/shard_map/pallas_call | solution.py:652
  153.7 0.6 broadcast_select_fusion
  (28 shorter events, 0.1 us)
Async XLA Ops:
  3.2 9.3 %copy-start.8 = (bf16[64,1024]{1,0:T(8,128)(2,1)}, bf16[64,1024]{1,0:T(8,128)(2,1)S(1)}, u32[]{:S(2)}) copy-start(bf16[64,1024]{1,0:T(8,128)(2,1)S(1)} %get-tuple-element.263) | copy-start | bytes 393220
  3.2 6.6 %collective-permute-start.29 = (bf16[64,1024]{1,0:T(8,128)(2,1)S(1)}, bf16[64,1024]{1,0:T(8,128)(2,1)}, u32[]{:S(2)}, u32[]{:S(2)}) collective-permute-start(bf16[64,1024]{1,0:T(8,128)(2,1)S(1)} %get-tuple-element.263), channel_id=1, source_target_pairs={{0,16},{16,0},{1,17},{17,1},{2,18},{18,2},{3,19},{19,3},{4,20},{20... | collective-permute-start | bytes 393224 | tf_op jit(solution)/shard_map/ppermute | solution.py:29
  6.2 6.2 %copy-start.2 = (bf16[1,1,768,2048]{3,2,1,0:T(8,128)(2,1)S(1)}, bf16[1,1,768,2048]{3,2,1,0:T(8,128)(2,1)}, u32[]{:S(2)}) copy-start(bf16[1,1,768,2048]{3,2,1,0:T(8,128)(2,1)} %param.24) | copy-start | bytes 9437188
  6.2 6.2 %copy-start.10 = (f32[2048]{0:T(1024)S(1)}, f32[2048]{0:T(1024)}, u32[]{:S(2)}) copy-start(f32[2048]{0:T(1024)} %param.21) | copy-start | bytes 24580
  6.2 6.2 %copy-start.12 = (s32[128,2]{0,1:T(2,128)S(1)}, s32[128,2]{0,1:T(2,128)}, u32[]{:S(2)}) copy-start(s32[128,2]{0,1:T(2,128)} %param.30) | copy-start | bytes 3076
  6.2 6.2 %copy-start.13 = (f32[128,2]{0,1:T(2,128)S(1)}, f32[128,2]{0,1:T(2,128)}, u32[]{:S(2)}) copy-start(f32[128,2]{0,1:T(2,128)} %param.31) | copy-start | bytes 3076
  6.2 6.2 %copy-start.14 = (s32[1,2,4]{2,1,0:T(2,128)S(1)}, s32[1,2,4]{2,1,0:T(2,128)}, u32[]{:S(2)}) copy-start(s32[1,2,4]{2,1,0:T(2,128)} %param.28) | copy-start | bytes 100
  6.2 6.2 %copy-start.15 = (s32[1,8]{1,0:T(1,128)S(1)}, s32[1,8]{1,0:T(1,128)}, u32[]{:S(2)}) copy-start(s32[1,8]{1,0:T(1,128)} %param.29) | copy-start | bytes 100
  9.8 123.1 %collective-permute-start.32 = (bf16[1280,2048]{1,0:T(8,128)(2,1)}, bf16[1280,2048]{1,0:T(8,128)(2,1)}, u32[]{:S(2)}, u32[]{:S(2)}) collective-permute-start(bf16[1280,2048]{1,0:T(8,128)(2,1)} %get-tuple-element.289), channel_id=1, source_target_pairs={{16,0},{17,1},{18,2},{19,3},{20,4},{21,5},{22,6},{23,7},{24,8},{25... | collective-permute-start | bytes 15728648 | tf_op jit(solution)/shard_map/ppermute | solution.py:508
  11.1 137.6 %collective-permute-start.33 = (bf16[256,2048]{1,0:T(8,128)(2,1)}, bf16[256,2048]{1,0:T(8,128)(2,1)}, u32[]{:S(2)}, u32[]{:S(2)}) collective-permute-start(bf16[256,2048]{1,0:T(8,128)(2,1)} %get-tuple-element.290), channel_id=1, source_target_pairs={{16,0},{17,1},{18,2},{19,3},{20,4},{21,5},{22,6},{23,7},{24,8},{25... | collective-permute-start | bytes 3145736 | tf_op jit(solution)/shard_map/ppermute | solution.py:509
  26.3 1.4 collective-permute-start.13
  31.1 1.5 collective-permute-start.14
  33.3 11.9 %all-to-all-start.1 = ((bf16[8,48,256]{2,1,0:T(8,128)(2,1)}), bf16[8,48,256]{2,1,0:T(8,128)(2,1)S(1)}, u32[]{:S(2)}, u32[]{:S(2)}) async-start(bf16[8,48,256]{2,1,0:T(8,128)(2,1)} %bitcast.5), calls=%async_computation.1 | async-start | bytes 393216 | tf_op jit(solution)/shard_map/cond/branch_1_fun/all_to_all | solution.py:536
  57.5 1.4 collective-permute-start.15
  62.3 1.5 collective-permute-start.16
  64.5 11.9 %all-to-all-start.3 = ((bf16[8,48,256]{2,1,0:T(8,128)(2,1)}), bf16[8,48,256]{2,1,0:T(8,128)(2,1)S(1)}, u32[]{:S(2)}, u32[]{:S(2)}) async-start(bf16[8,48,256]{2,1,0:T(8,128)(2,1)} %bitcast.10), calls=%async_computation.3 | async-start | bytes 393216 | tf_op jit(solution)/shard_map/cond/branch_1_fun/all_to_all | solution.py:536
  77.4 4.5 %collective-permute-start.30 = (f32[128,256]{1,0:T(8,128)}, f32[128,256]{1,0:T(8,128)S(1)}, u32[]{:S(2)}, u32[]{:S(2)}) collective-permute-start(f32[128,256]{1,0:T(8,128)} %get-tuple-element.277), channel_id=1, source_target_pairs={{0,16},{1,17},{2,18},{3,19},{4,20},{5,21},{6,22},{7,23},{8,24},{9,... | collective-permute-start | bytes 393224 | tf_op jit(solution)/shard_map/ppermute | solution.py:693
  78.7 3.2 %copy-start.9 = (bf16[64,1024]{1,0:T(8,128)(2,1)S(1)}, bf16[64,1024]{1,0:T(8,128)(2,1)}, u32[]{:S(2)}) copy-start(bf16[64,1024]{1,0:T(8,128)(2,1)} %copy-done.8) | copy-start | bytes 393220
  82.9 10.7 %collective-permute-start.21 = (bf16[144,1024]{1,0:T(8,128)(2,1)S(1)}, bf16[144,1024]{1,0:T(8,128)(2,1)S(1)}, u32[]{:S(2)}, u32[]{:S(2)}) collective-permute-start(bf16[144,1024]{1,0:T(8,128)(2,1)S(1)} %branch_1_fun.16), channel_id=1, source_target_pairs={{0,12},{2,14},{4,0},{6,2},{8,4},{10,6},{12,8},{14,10},{1,13},{3,15... | collective-permute-start | bytes 884744 | tf_op jit(solution)/shard_map/cond/branch_1_fun/ppermute | solution.py:569
  86.1 12.8 %collective-permute-start.20 = (bf16[144,1024]{1,0:T(8,128)(2,1)S(1)}, bf16[144,1024]{1,0:T(8,128)(2,1)S(1)}, u32[]{:S(2)}, u32[]{:S(2)}) collective-permute-start(bf16[144,1024]{1,0:T(8,128)(2,1)S(1)} %branch_1_fun.16), channel_id=1, source_target_pairs={{0,4},{2,6},{4,8},{6,10},{8,12},{10,14},{12,0},{14,2},{1,5},{3,7},... | collective-permute-start | bytes 884744 | tf_op jit(solution)/shard_map/cond/branch_1_fun/ppermute | solution.py:569
  86.1 12.8 %collective-permute-start.19 = (bf16[144,1024]{1,0:T(8,128)(2,1)S(1)}, bf16[144,1024]{1,0:T(8,128)(2,1)S(1)}, u32[]{:S(2)}, u32[]{:S(2)}) collective-permute-start(bf16[144,1024]{1,0:T(8,128)(2,1)S(1)} %branch_1_fun.16), channel_id=1, source_target_pairs={{0,2},{2,0},{4,6},{6,4},{8,10},{10,8},{12,14},{14,12},{1,3},{3,1},... | collective-permute-start | bytes 884744 | tf_op jit(solution)/shard_map/cond/branch_1_fun/ppermute | solution.py:29
  98.9 14.8 %collective-permute-start.24 = (bf16[144,1024]{1,0:T(8,128)(2,1)S(1)}, bf16[144,1024]{1,0:T(8,128)(2,1)S(1)}, u32[]{:S(2)}, u32[]{:S(2)}) collective-permute-start(bf16[144,1024]{1,0:T(8,128)(2,1)S(1)} %branch_1_fun.16), channel_id=1, source_target_pairs={{0,8},{2,10},{4,12},{6,14},{8,0},{10,2},{12,4},{14,6},{1,9},{3,11}... | collective-permute-start | bytes 884744 | tf_op jit(solution)/shard_map/cond/branch_1_fun/ppermute | solution.py:569
  99.0 18.3 %collective-permute-start.22 = (bf16[144,1024]{1,0:T(8,128)(2,1)S(1)}, bf16[144,1024]{1,0:T(8,128)(2,1)S(1)}, u32[]{:S(2)}, u32[]{:S(2)}) collective-permute-start(bf16[144,1024]{1,0:T(8,128)(2,1)S(1)} %collective-permute-done.20), channel_id=1, source_target_pairs={{0,2},{2,0},{4,6},{6,4},{8,10},{10,8},{12,14},{14,12},{1,3},{3,1},... | collective-permute-start | bytes 884744 | tf_op jit(solution)/shard_map/cond/branch_1_fun/ppermute | solution.py:29
  100.6 16.7 %collective-permute-start.23 = (bf16[144,1024]{1,0:T(8,128)(2,1)S(1)}, bf16[144,1024]{1,0:T(8,128)(2,1)S(1)}, u32[]{:S(2)}, u32[]{:S(2)}) collective-permute-start(bf16[144,1024]{1,0:T(8,128)(2,1)S(1)} %collective-permute-done.21), channel_id=1, source_target_pairs={{0,2},{2,0},{4,6},{6,4},{8,10},{10,8},{12,14},{14,12},{1,3},{3,1},... | collective-permute-start | bytes 884744 | tf_op jit(solution)/shard_map/cond/branch_1_fun/ppermute | solution.py:29
  113.7 7.8 %collective-permute-start.25 = (bf16[144,1024]{1,0:T(8,128)(2,1)S(1)}, bf16[144,1024]{1,0:T(8,128)(2,1)S(1)}, u32[]{:S(2)}, u32[]{:S(2)}) collective-permute-start(bf16[144,1024]{1,0:T(8,128)(2,1)S(1)} %collective-permute-done.24), channel_id=1, source_target_pairs={{0,2},{2,0},{4,6},{6,4},{8,10},{10,8},{12,14},{14,12},{1,3},{3,1},... | collective-permute-start | bytes 884744 | tf_op jit(solution)/shard_map/cond/branch_1_fun/ppermute | solution.py:29
  122.4 4.9 %copy-start.3 = (bf16[576,1024]{1,0:T(8,128)(2,1)S(1)}, bf16[576,1024]{1,0:T(8,128)(2,1)}, u32[]{:S(2)}) copy-start(bf16[576,1024]{1,0:T(8,128)(2,1)} %get-tuple-element.213.refs_0_) | copy-start | bytes 3538948 | tf_op jit(solution)/shard_map/cond
  122.4 4.9 %copy-start.4 = (bf16[288,1024]{1,0:T(8,128)(2,1)S(1)}, bf16[288,1024]{1,0:T(8,128)(2,1)}, u32[]{:S(2)}) copy-start(bf16[288,1024]{1,0:T(8,128)(2,1)} %get-tuple-element.214.refs_1_) | copy-start | bytes 1769476 | tf_op jit(solution)/shard_map/cond
  122.4 4.9 %collective-permute-start.3 = (bf16[576,1024]{1,0:T(8,128)(2,1)}, bf16[576,1024]{1,0:T(8,128)(2,1)}, u32[]{:S(2)}, u32[]{:S(2)}) collective-permute-start(bf16[576,1024]{1,0:T(8,128)(2,1)} %get-tuple-element.213.refs_0_), channel_id=1, source_target_pairs={{0,1},{1,0},{2,3},{3,2},{4,5},{5,4},{6,7},{7,6},{8,9},{9,8},{10,11... | collective-permute-start | bytes 3538952 | tf_op jit(solution)/shard_map/cond/branch_1_fun/ppermute | solution.py:25
  122.4 4.0 %collective-permute-start.4 = (bf16[288,1024]{1,0:T(8,128)(2,1)}, bf16[288,1024]{1,0:T(8,128)(2,1)}, u32[]{:S(2)}, u32[]{:S(2)}) collective-permute-start(bf16[288,1024]{1,0:T(8,128)(2,1)} %get-tuple-element.214.refs_1_), channel_id=1, source_target_pairs={{0,1},{1,0},{2,3},{3,2},{4,5},{5,4},{6,7},{7,6},{8,9},{9,8},{10,11... | collective-permute-start | bytes 1769480 | tf_op jit(solution)/shard_map/cond/branch_1_fun/ppermute | solution.py:25
  122.9 4.4 %collective-permute-start.5 = (bf16[288,1024]{1,0:T(8,128)(2,1)}, bf16[288,1024]{1,0:T(8,128)(2,1)}, u32[]{:S(2)}, u32[]{:S(2)}) collective-permute-start(bf16[288,1024]{1,0:T(8,128)(2,1)} %get-tuple-element.215.refs_2_), channel_id=1, source_target_pairs={{0,1},{1,0},{2,3},{3,2},{4,5},{5,4},{6,7},{7,6},{8,9},{9,8},{10,11... | collective-permute-start | bytes 1769480 | tf_op jit(solution)/shard_map/cond/branch_1_fun/ppermute | solution.py:25
  131.6 22.2 %collective-permute-start.31 = (bf16[32,1024]{1,0:T(8,128)(2,1)S(1)}, bf16[32,1024]{1,0:T(8,128)(2,1)S(1)}, u32[]{:S(2)}, u32[]{:S(2)}) collective-permute-start(bf16[32,1024]{1,0:T(8,128)(2,1)S(1)} %get-tuple-element.285), channel_id=1, source_target_pairs={{16,0},{17,1},{18,2},{19,3},{20,4},{21,5},{22,6},{23,7},{24,8},{25... | collective-permute-start | bytes 196616 | tf_op jit(solution)/shard_map/ppermute | solution.py:749

commit v6 on v5

--- a/solution.py
+++ b/solution.py
@@ -48,8 +48,8 @@
 
 
 def prepare_kernel(
-    experts, capacity, part_ref, routes_ref, gates_ref, all_rows_ref, inputs_ref, grads_ref,
-    targets_ref, tiled_ref, states_ref, payload_ref, own_ref, rows_ref, sems,
+    experts, capacity, part_ref, all_routes_ref, all_gates_ref, all_rows_ref, inputs_ref, grads_ref,
+    targets_ref, tiled_ref, states_ref, payload_ref, sent_ref, rows_ref, own_ref, routes_ref, gates_ref, sems,
 ):
     row_count, share = rows_ref.shape
     steps, routes_each = targets_ref.shape[:2]
@@ -62,8 +62,12 @@
         pltpu.make_async_copy(inputs_ref.at[:, own], own_ref.at[pl.ds(0, held)], sems.at[1]),
         pltpu.make_async_copy(grads_ref.at[:, own], own_ref.at[pl.ds(held, held)], sems.at[2]),
     ]
-    row_copy.start()
-    for copy in copies:
+    table_copies = [
+        pltpu.make_async_copy(all_routes_ref, routes_ref, sems.at[3]),
+        pltpu.make_async_copy(all_gates_ref, gates_ref, sems.at[4]),
+    ]
+    out_copy = pltpu.make_async_copy(own_ref, sent_ref, sems.at[5])
+    for copy in table_copies + copies + [row_copy]:
         copy.start()
     before = lax.broadcasted_iota(i32, (row_count, stacked), 0)
     after = lax.rem(lax.broadcasted_iota(i32, (row_count, stacked), 1), row_count)
@@ -73,6 +77,9 @@
     block_of = lax.div(lax.broadcasted_iota(i32, (1, stacked), 1), row_count)
     expert_ids = lax.broadcasted_iota(i32, (experts, row_count), 0)
     tall_ids = lax.broadcasted_iota(i32, (experts, stacked), 0)
+    for copy in table_copies + copies:
+        copy.wait()
+    out_copy.start()
     routes = dot(routes_ref[...].astype(f32), repeat, precision=lax.Precision.HIGHEST)
     routes = (routes + 0.5).astype(i32)
     tiled_ref[...] = dot(gates_ref[...], repeat, precision=lax.Precision.HIGHEST)
@@ -92,8 +99,7 @@
         columns = slice(block * width, (block + 1) * width)
         states_ref[block * row_count : (block + 1) * row_count, :] = rows_ref[:, columns].astype(f32)
     payload_ref[...] = dot(one_hot(payload_ref.shape[0], targets_ref.at[0]), states_ref[...].astype(bf16)).astype(bf16)
-    for copy in copies:
-        copy.wait()
+    out_copy.wait()
 
 
 def dispatch_kernel(step, targets_ref, states_ref, payload_ref):
@@ -486,8 +492,15 @@
             jax.ShapeDtypeStruct((moved, lanes), bf16),
             jax.ShapeDtypeStruct((2 * per_half, share), bf16),
         ],
-        in_specs=[smem, vmem, vmem] + [stays] * 3,
-        scratch_shapes=[pltpu.VMEM((row_count, share), bf16), pltpu.SemaphoreType.DMA((3,))],
+        in_specs=[smem] + [stays] * 5,
+        out_specs=[vmem] * 4 + [stays],
+        scratch_shapes=[
+            pltpu.VMEM((row_count, share), bf16),
+            pltpu.VMEM((2 * per_half, share), bf16),
+            pltpu.VMEM(routes.shape, i32),
+            pltpu.VMEM(gates.shape, f32),
+            pltpu.SemaphoreType.DMA((6,)),
+        ],
         compiler_params=fits(60),
         cost_estimate=costs(1, 1),
     )(part_ref, routes, gates, decode_states, traj_inputs[0], traj_cotangents[0])

time: 155 us -> 155 us (level)
  no operation moved by 1% of the time
where the time goes in v6:
time: 155 us; the launch traced here: 154 us
  waiting for transfers between devices  59.8 us (39%)
  Pallas kernels  36.4 us (23%)
  blocking collectives  25 us (16%)
  starting transfers between devices  24.3 us (16%)
  other arithmetic  4.96 us (3%)
  local copies, waits for them, and re-layouts  2.76 us (2%)
    all_to_all x2, blocking collectives, decode_step(): lax.all_to_all(payload, 'exp', split_axis=0, concat_axis=0, tiled=True)  25 us
    ppermute x3, waiting for transfers between devices, along(): return lax.ppermute(array, 'exp', pairs)  24 us
    all_to_all x2, waiting for transfers between devices, decode_step(): lax.all_to_all(summed, 'exp', split_axis=0, concat_axis=0, tiled=True)  15.2 us
    pallas_call x1, Pallas kernels, update_late(): pl.pallas_call(functools.partial(late_kernel, features, hidden, tile, 2 *...  12.9 us
    ppermute x5, starting transfers between devices, flipped(): lax.ppermute(array, axis, [(i, i ^ bit) for i in range(lax.axis_size(axis...  8.06 us
    ppermute x7, waiting for transfers between devices, shifted(): lax.ppermute(array, axis, [(i, (i + by) % size) for i in range(size)])  7.69 us
    ppermute x5, waiting for transfers between devices, flipped(): lax.ppermute(array, axis, [(i, i ^ bit) for i in range(lax.axis_size(axis...  6.87 us
    all_to_all x2, starting transfers between devices, decode_step(): lax.all_to_all(summed, 'exp', split_axis=0, concat_axis=0, tiled=True)  6.78 us
  transfers between devices with their start and end apart: 21, of which 15 were waited for; matrix products, arithmetic and copies ran while one was open for 5% of the time, Pallas kernels for 22%

profile of v6, /device:TPU:0, one launch (start us, length us, event | category | flops | bytes accessed | tf_op | source)
XLA Modules:
  0.0 154.1 jit_solution(7149881846993008780)
XLA Ops:
  0.6 2.2 %shard_map.139 = (s32[4,2,128]{2,1,0:T(2,128)S(1)}, f32[8,128]{1,0:T(8,128)S(1)}, f32[128,256]{1,0:T(8,128)}, bf16[384,256]{1,0:T(8,128)(2,1)}, bf16[64,1024]{1,0:T(8,128)(2,1)S(1)}) custom-call(s32[1]{0:T(128)} %bitcast.24.part_ref, s32[8,32]{1,0:T(8,128)} %bitcast.68, f32[8,32]{1,0:T(8,128)} %bitcast.69, bf16[32,2048]{1,0:T(8,128)(2,1)} %all_rows_ref.1, ...), custom_call_target="tpu_custom_call" | custom-call | flops 1 | bytes 1 | tf_op jit(solution)/shard_map/pallas_call | solution.py:486
  2.9 3.0 %collective-permute-start.29 = (bf16[64,1024]{1,0:T(8,128)(2,1)S(1)}, bf16[64,1024]{1,0:T(8,128)(2,1)}, u32[]{:S(2)}, u32[]{:S(2)}) collective-permute-start(bf16[64,1024]{1,0:T(8,128)(2,1)S(1)} %get-tuple-element.263), channel_id=1, source_target_pairs={{0,16},{16,0},{1,17},{17,1},{2,18},{18,2},{3,19},{19,3},{4,20},{20... | collective-permute-start | bytes 393224 | tf_op jit(solution)/shard_map/ppermute | solution.py:29
  5.9 0.0 copy-start.14
  5.9 0.0 copy-start.15
  5.9 0.1 shard_map.140
  6.0 3.5 %collective-permute-done.29 = bf16[64,1024]{1,0:T(8,128)(2,1)} collective-permute-done((bf16[64,1024]{1,0:T(8,128)(2,1)S(1)}, bf16[64,1024]{1,0:T(8,128)(2,1)}, u32[]{:S(2)}, u32[]{:S(2)}) %collective-permute-start.29) | collective-permute-done | bytes 131104 | tf_op jit(solution)/shard_map/ppermute | solution.py:29
  9.5 1.3 collective-permute-start.32
  10.8 1.3 collective-permute-start.33
  12.2 34.0 %conditional.4 = (f32[128,256]{1,0:T(8,128)}, bf16[384,256]{1,0:T(8,128)(2,1)}, bf16[576,1024]{1,0:T(8,128)(2,1)}, bf16[288,1024]{1,0:T(8,128)(2,1)}, bf16[288,1024]{1,0:T(8,128)(2,1)}) conditional(s32[]{:T(128)} %convert_element_type.43, (s32[128,2]{0,1:T(2,128)S(1)}, f32[128,2]{0,1:T(2,128)S(1)}, s32[1,2,4]{2,1,0:T(2,128)S(1)}, ...), branch_computations={%region_0.0_spmd, %region_1.0_spmd} | conditional | flops 7077889 | bytes 12976449 | solution.py:693
  12.2 13.9 %all_to_all.64 = bf16[8,48,256]{2,1,0:T(8,128)(2,1)S(1)} all-to-all(bf16[8,48,256]{2,1,0:T(8,128)(2,1)} %bitcast.3), channel_id=1, replica_groups=mesh['sect'=2,'exp'=8,'dp'=2] {'exp'}, dimensions={0} | all-to-all | bytes 393216 | tf_op jit(solution)/shard_map/cond/branch_1_fun/all_to_all | solution.py:544
  26.1 1.4 collective-permute-done.13.refs_1_
  27.5 3.3 %branch_1_fun.10 = (bf16[384,256]{1,0:T(8,128)(2,1)S(1)}, bf16[384,256]{1,0:T(8,128)(2,1)S(1)}) custom-call(s32[1]{0:T(128)} %get-tuple-element.135.part_ref, f32[1,2048]{1,0:T(1,128)S(1)} %get-tuple-element.136.gain_ref, bf16[384,256]{1,0:T(8,128)(2,1)S(1)} %bitcast.47, bf16[384,256]{1,0:T(8,128)(2,1)S(1)} %collective-permute-done.13.refs_1_, ...), custom_call_target="tpu_custom_call" | custom-call | flops 1 | bytes 1 | tf_op jit(solution)/shard_map/cond/branch_1_fun/pallas_call | solution.py:526
  30.8 0.2 collective-permute-start.14
  31.0 1.3 collective-permute-done.14
  32.3 0.7 add_convert_fusion
  33.1 3.4 %all-to-all-start.1 = ((bf16[8,48,256]{2,1,0:T(8,128)(2,1)}), bf16[8,48,256]{2,1,0:T(8,128)(2,1)S(1)}, u32[]{:S(2)}, u32[]{:S(2)}) async-start(bf16[8,48,256]{2,1,0:T(8,128)(2,1)} %bitcast.5), calls=%async_computation.1 | async-start | bytes 393216 | tf_op jit(solution)/shard_map/cond/branch_1_fun/all_to_all | solution.py:549
  36.5 0.9 copy.61.states_ref
  37.4 7.6 %all-to-all-done.1 = bf16[8,48,256]{2,1,0:T(8,128)(2,1)S(1)} async-done(((bf16[8,48,256]{2,1,0:T(8,128)(2,1)}), bf16[8,48,256]{2,1,0:T(8,128)(2,1)S(1)}, u32[]{:S(2)}, u32[]{:S(2)}) %all-to-all-start.1) | async-done | bytes 196640 | tf_op jit(solution)/shard_map/cond/branch_1_fun/all_to_all | solution.py:549
  44.9 1.2 branch_1_fun.11
  46.2 30.9 %conditional.5 = (f32[128,256]{1,0:T(8,128)}, bf16[768,2048]{1,0:T(8,128)(2,1)}, bf16[768,2048]{1,0:T(8,128)(2,1)}) conditional(s32[]{:T(128)} %convert_element_type.43, (s32[]{:T(128)}, bf16[576,1024]{1,0:T(8,128)(2,1)}, bf16[288,1024]{1,0:T(8,128)(2,1)}, bf16[288,1024]{1,0:T(8,128)(2,1)}, s32[1]{0:T(128)}, ...), branch_computations={%region_2.0_spmd, %region_3.0_spmd} | conditional | flops 393219 | bytes 18882816 | solution.py:705
  46.2 11.1 %all_to_all.65 = bf16[8,48,256]{2,1,0:T(8,128)(2,1)S(1)} all-to-all(bf16[8,48,256]{2,1,0:T(8,128)(2,1)} %bitcast.8), channel_id=1, replica_groups=mesh['sect'=2,'exp'=8,'dp'=2] {'exp'}, dimensions={0} | all-to-all | bytes 393216 | tf_op jit(solution)/shard_map/cond/branch_1_fun/all_to_all | solution.py:544
  57.3 0.0 collective-permute-start.15
  57.3 1.4 collective-permute-done.15.refs_1_
  58.7 3.3 %branch_1_fun.13 = (bf16[384,256]{1,0:T(8,128)(2,1)S(1)}, bf16[384,256]{1,0:T(8,128)(2,1)S(1)}) custom-call(s32[1]{0:T(128)} %get-tuple-element.160.part_ref, f32[1,2048]{1,0:T(1,128)S(1)} %get-tuple-element.161.gain_ref, bf16[384,256]{1,0:T(8,128)(2,1)S(1)} %bitcast.49, bf16[384,256]{1,0:T(8,128)(2,1)S(1)} %collective-permute-done.15.refs_1_, ...), custom_call_target="tpu_custom_call" | custom-call | flops 1 | bytes 1 | tf_op jit(solution)/shard_map/cond/branch_1_fun/pallas_call | solution.py:526
  62.0 0.2 collective-permute-start.16
  62.3 1.3 collective-permute-done.16
  63.5 0.7 add_convert_fusion.1
  64.3 3.4 %all-to-all-start.3 = ((bf16[8,48,256]{2,1,0:T(8,128)(2,1)}), bf16[8,48,256]{2,1,0:T(8,128)(2,1)S(1)}, u32[]{:S(2)}, u32[]{:S(2)}) async-start(bf16[8,48,256]{2,1,0:T(8,128)(2,1)} %bitcast.10), calls=%async_computation.3 | async-start | bytes 393216 | tf_op jit(solution)/shard_map/cond/branch_1_fun/all_to_all | solution.py:549
  67.7 0.9 copy.62.states_ref
  68.6 7.6 %all-to-all-done.3 = bf16[8,48,256]{2,1,0:T(8,128)(2,1)S(1)} async-done(((bf16[8,48,256]{2,1,0:T(8,128)(2,1)}), bf16[8,48,256]{2,1,0:T(8,128)(2,1)S(1)}, u32[]{:S(2)}, u32[]{:S(2)}) %all-to-all-start.3) | async-done | bytes 196640 | tf_op jit(solution)/shard_map/cond/branch_1_fun/all_to_all | solution.py:549
  76.2 1.0 branch_1_fun.14
  77.1 1.3 collective-permute-start.30
  78.4 3.2 %collective-permute-done.30 = f32[128,256]{1,0:T(8,128)S(1)} collective-permute-done((f32[128,256]{1,0:T(8,128)}, f32[128,256]{1,0:T(8,128)S(1)}, u32[]{:S(2)}, u32[]{:S(2)}) %collective-permute-start.30) | collective-permute-done | bytes 131104 | tf_op jit(solution)/shard_map/ppermute | solution.py:706
  81.6 40.5 %conditional.6 = (f32[128,256]{1,0:T(8,128)S(1)}, bf16[384,256]{1,0:T(8,128)(2,1)}, bf16[576,1024]{1,0:T(8,128)(2,1)}, bf16[288,1024]{1,0:T(8,128)(2,1)}, bf16[288,1024]{1,0:T(8,128)(2,1)}) conditional(s32[]{:T(128)} %convert_element_type.43, (s32[4,2,128]{2,1,0:T(2,128)S(1)}, f32[128,256]{1,0:T(8,128)S(1)}, s32[1]{0:T(128)}, ...), branch_computations={%region_4.0_spmd, %region_5.0_spmd} | conditional | flops 7077889 | bytes 13238593 | solution.py:731
  81.6 1.1 branch_1_fun.16
  82.7 3.2 %collective-permute-start.21 = (bf16[144,1024]{1,0:T(8,128)(2,1)S(1)}, bf16[144,1024]{1,0:T(8,128)(2,1)S(1)}, u32[]{:S(2)}, u32[]{:S(2)}) collective-permute-start(bf16[144,1024]{1,0:T(8,128)(2,1)S(1)} %branch_1_fun.16), channel_id=1, source_target_pairs={{0,12},{2,14},{4,0},{6,2},{8,4},{10,6},{12,8},{14,10},{1,13},{3,15... | collective-permute-start | bytes 884744 | tf_op jit(solution)/shard_map/cond/branch_1_fun/ppermute | solution.py:582
  85.9 1.5 collective-permute-start.19
  87.4 5.9 %collective-permute-done.21 = bf16[144,1024]{1,0:T(8,128)(2,1)S(1)} collective-permute-done((bf16[144,1024]{1,0:T(8,128)(2,1)S(1)}, bf16[144,1024]{1,0:T(8,128)(2,1)S(1)}, u32[]{:S(2)}, u32[]{:S(2)}) %collective-permute-start.21) | collective-permute-done | bytes 294944 | tf_op jit(solution)/shard_map/cond/branch_1_fun/ppermute | solution.py:582
  93.3 5.3 %collective-permute-done.20 = bf16[144,1024]{1,0:T(8,128)(2,1)S(1)} collective-permute-done((bf16[144,1024]{1,0:T(8,128)(2,1)S(1)}, bf16[144,1024]{1,0:T(8,128)(2,1)S(1)}, u32[]{:S(2)}, u32[]{:S(2)}) %collective-permute-start.20) | collective-permute-done | bytes 294944 | tf_op jit(solution)/shard_map/cond/branch_1_fun/ppermute | solution.py:582
  98.6 0.0 collective-permute-done.19
  98.6 0.1 collective-permute-start.24
  98.7 1.5 collective-permute-start.22
  100.3 0.5 collective-permute-start.23
  100.8 12.7 %collective-permute-done.24 = bf16[144,1024]{1,0:T(8,128)(2,1)S(1)} collective-permute-done((bf16[144,1024]{1,0:T(8,128)(2,1)S(1)}, bf16[144,1024]{1,0:T(8,128)(2,1)S(1)}, u32[]{:S(2)}, u32[]{:S(2)}) %collective-permute-start.24) | collective-permute-done | bytes 294944 | tf_op jit(solution)/shard_map/cond/branch_1_fun/ppermute | solution.py:582
  113.5 1.5 collective-permute-start.25
  115.0 0.9 copy.40
  115.9 1.1 pad_maximum_fusion.3
  117.0 0.0 collective-permute-done.22
  117.0 0.0 collective-permute-done.23
  117.0 0.9 pad_maximum_fusion.4
  117.9 3.4 %collective-permute-done.25 = bf16[144,1024]{1,0:T(8,128)(2,1)S(1)} collective-permute-done((bf16[144,1024]{1,0:T(8,128)(2,1)S(1)}, bf16[144,1024]{1,0:T(8,128)(2,1)S(1)}, u32[]{:S(2)}, u32[]{:S(2)}) %collective-permute-start.25) | collective-permute-done | bytes 294944 | tf_op jit(solution)/shard_map/cond/branch_1_fun/ppermute | solution.py:29
  121.2 0.9 pad_maximum_fusion.5
  122.1 9.1 %conditional.7 = (bf16[32,1024]{1,0:T(8,128)(2,1)S(1)}, bf16[32,1024]{1,0:T(8,128)(2,1)S(1)}, bf16[512,2048]{1,0:T(8,128)(2,1)}, bf16[512,2048]{1,0:T(8,128)(2,1)}, f32[1,512]{1,0:T(1,128)}) conditional(s32[]{:T(128)} %convert_element_type.43, (bf16[384,256]{1,0:T(8,128)(2,1)}, s32[1]{0:T(128)}, f32[1,2048]{1,0:T(1,128)S(1)}, ...), branch_computations={%region_6.0_spmd, %region_7.0_spmd} | conditional | flops 393220 | bytes 16515291 | solution.py:759
  122.1 0.5 collective-permute-start.4
  122.6 0.1 collective-permute-start.5
  122.7 2.0 %branch_1_fun.17.refs_0_ = f32[1,512]{1,0:T(1,128)} custom-call(s32[1]{0:T(128)} %bitcast.23.me_ref, bf16[576,1024]{1,0:T(8,128)(2,1)} %get-tuple-element.213.refs_0_, bf16[288,1024]{1,0:T(8,128)(2,1)} %get-tuple-element.214.refs_1_, bf16[288,1024]{1,0:T(8,128)(2,1)} %get-tuple-element.215.refs_2_), custom_call_target="tpu_custom_call" | custom-call | flops 1 | bytes 1 | tf_op jit(solution)/shard_map/cond/branch_1_fun/pallas_call | solution.py:602
  124.8 1.4 collective-permute-done.4.refs_4_
  126.2 0.8 collective-permute-done.5.refs_5_
  127.0 4.2 %branch_1_fun.19 = (bf16[512,2048]{1,0:T(8,128)(2,1)}, bf16[512,2048]{1,0:T(8,128)(2,1)}) custom-call(s32[1]{0:T(128)} %get-tuple-element.218.part_ref, bf16[576,1024]{1,0:T(8,128)(2,1)S(1)} %copy-done.3, bf16[288,1024]{1,0:T(8,128)(2,1)S(1)} %copy-done.4, bf16[288,1024]{1,0:T(8,128)(2,1)} %get-tuple-element.215.refs_2_, ...), custom_call_target="tpu_custom_call" | custom-call | flops 1 | bytes 1 | tf_op jit(solution)/shard_map/cond/branch_1_fun/pallas_call | solution.py:735
  131.3 1.3 collective-permute-start.31
  132.6 12.9 %shard_map.142 = (bf16[768,2048]{1,0:T(8,128)(2,1)}, bf16[768,2048]{1,0:T(8,128)(2,1)}, f32[256,512]{1,0:T(8,128)}, f32[256,2048]{1,0:T(8,128)}) custom-call(s32[1]{0:T(128)} %bitcast.31.go_ref, f32[1,512]{1,0:T(1,128)} %get-tuple-element.291.weight_ref, bf16[512,2048]{1,0:T(8,128)(2,1)} %get-tuple-element.287.refs_0_, ...), custom_call_target="tpu_custom_call", output_to_operand_aliasing={{0}: (5, {}), {1}: (6, {})} | custom-call | flops 1 | bytes 1 | tf_op jit(solution)/shard_map/pallas_call | solution.py:649
  145.5 2.9 %collective-permute-done.33.refs_3_ = bf16[256,2048]{1,0:T(8,128)(2,1)} collective-permute-done((bf16[256,2048]{1,0:T(8,128)(2,1)}, bf16[256,2048]{1,0:T(8,128)(2,1)}, u32[]{:S(2)}, u32[]{:S(2)}) %collective-permute-start.33) | collective-permute-done | bytes 1048608 | tf_op jit(solution)/shard_map/ppermute | solution.py:522
  148.4 5.0 %shard_map.143 = (bf16[768,2048]{1,0:T(8,128)(2,1)}, bf16[768,2048]{1,0:T(8,128)(2,1)}) custom-call(s32[1]{0:T(128)} %bitcast.31.go_ref, bf16[512,2048]{1,0:T(8,128)(2,1)} %get-tuple-element.287.refs_0_, bf16[512,2048]{1,0:T(8,128)(2,1)} %get-tuple-element.288.refs_1_, ...), custom_call_target="tpu_custom_call", output_to_operand_aliasing={{0}: (7, {}), {1}: (8, {})} | custom-call | flops 1 | bytes 1 | tf_op jit(solution)/shard_map/pallas_call | solution.py:665
  153.5 0.6 broadcast_select_fusion
  (28 shorter events, 0.1 us)
Async XLA Ops:
  2.9 9.3 %copy-start.8 = (bf16[64,1024]{1,0:T(8,128)(2,1)}, bf16[64,1024]{1,0:T(8,128)(2,1)S(1)}, u32[]{:S(2)}) copy-start(bf16[64,1024]{1,0:T(8,128)(2,1)S(1)} %get-tuple-element.263) | copy-start | bytes 393220
  2.9 6.6 %collective-permute-start.29 = (bf16[64,1024]{1,0:T(8,128)(2,1)S(1)}, bf16[64,1024]{1,0:T(8,128)(2,1)}, u32[]{:S(2)}, u32[]{:S(2)}) collective-permute-start(bf16[64,1024]{1,0:T(8,128)(2,1)S(1)} %get-tuple-element.263), channel_id=1, source_target_pairs={{0,16},{16,0},{1,17},{17,1},{2,18},{18,2},{3,19},{19,3},{4,20},{20... | collective-permute-start | bytes 393224 | tf_op jit(solution)/shard_map/ppermute | solution.py:29
  5.9 6.2 %copy-start.2 = (bf16[1,1,768,2048]{3,2,1,0:T(8,128)(2,1)S(1)}, bf16[1,1,768,2048]{3,2,1,0:T(8,128)(2,1)}, u32[]{:S(2)}) copy-start(bf16[1,1,768,2048]{3,2,1,0:T(8,128)(2,1)} %param.24) | copy-start | bytes 9437188
  5.9 6.2 %copy-start.10 = (f32[2048]{0:T(1024)S(1)}, f32[2048]{0:T(1024)}, u32[]{:S(2)}) copy-start(f32[2048]{0:T(1024)} %param.21) | copy-start | bytes 24580
  5.9 6.2 %copy-start.12 = (s32[128,2]{0,1:T(2,128)S(1)}, s32[128,2]{0,1:T(2,128)}, u32[]{:S(2)}) copy-start(s32[128,2]{0,1:T(2,128)} %param.30) | copy-start | bytes 3076
  5.9 6.2 %copy-start.13 = (f32[128,2]{0,1:T(2,128)S(1)}, f32[128,2]{0,1:T(2,128)}, u32[]{:S(2)}) copy-start(f32[128,2]{0,1:T(2,128)} %param.31) | copy-start | bytes 3076
  5.9 6.2 %copy-start.14 = (s32[1,2,4]{2,1,0:T(2,128)S(1)}, s32[1,2,4]{2,1,0:T(2,128)}, u32[]{:S(2)}) copy-start(s32[1,2,4]{2,1,0:T(2,128)} %param.28) | copy-start | bytes 100
  5.9 6.2 %copy-start.15 = (s32[1,8]{1,0:T(1,128)S(1)}, s32[1,8]{1,0:T(1,128)}, u32[]{:S(2)}) copy-start(s32[1,8]{1,0:T(1,128)} %param.29) | copy-start | bytes 100
  9.5 123.1 %collective-permute-start.32 = (bf16[1280,2048]{1,0:T(8,128)(2,1)}, bf16[1280,2048]{1,0:T(8,128)(2,1)}, u32[]{:S(2)}, u32[]{:S(2)}) collective-permute-start(bf16[1280,2048]{1,0:T(8,128)(2,1)} %get-tuple-element.289), channel_id=1, source_target_pairs={{16,0},{17,1},{18,2},{19,3},{20,4},{21,5},{22,6},{23,7},{24,8},{25... | collective-permute-start | bytes 15728648 | tf_op jit(solution)/shard_map/ppermute | solution.py:521
  10.8 137.6 %collective-permute-start.33 = (bf16[256,2048]{1,0:T(8,128)(2,1)}, bf16[256,2048]{1,0:T(8,128)(2,1)}, u32[]{:S(2)}, u32[]{:S(2)}) collective-permute-start(bf16[256,2048]{1,0:T(8,128)(2,1)} %get-tuple-element.290), channel_id=1, source_target_pairs={{16,0},{17,1},{18,2},{19,3},{20,4},{21,5},{22,6},{23,7},{24,8},{25... | collective-permute-start | bytes 3145736 | tf_op jit(solution)/shard_map/ppermute | solution.py:522
  26.1 1.4 collective-permute-start.13
  30.8 1.5 collective-permute-start.14
  33.1 11.9 %all-to-all-start.1 = ((bf16[8,48,256]{2,1,0:T(8,128)(2,1)}), bf16[8,48,256]{2,1,0:T(8,128)(2,1)S(1)}, u32[]{:S(2)}, u32[]{:S(2)}) async-start(bf16[8,48,256]{2,1,0:T(8,128)(2,1)} %bitcast.5), calls=%async_computation.1 | async-start | bytes 393216 | tf_op jit(solution)/shard_map/cond/branch_1_fun/all_to_all | solution.py:549
  57.3 1.4 collective-permute-start.15
  62.0 1.5 collective-permute-start.16
  64.3 11.9 %all-to-all-start.3 = ((bf16[8,48,256]{2,1,0:T(8,128)(2,1)}), bf16[8,48,256]{2,1,0:T(8,128)(2,1)S(1)}, u32[]{:S(2)}, u32[]{:S(2)}) async-start(bf16[8,48,256]{2,1,0:T(8,128)(2,1)} %bitcast.10), calls=%async_computation.3 | async-start | bytes 393216 | tf_op jit(solution)/shard_map/cond/branch_1_fun/all_to_all | solution.py:549
  77.1 4.5 %collective-permute-start.30 = (f32[128,256]{1,0:T(8,128)}, f32[128,256]{1,0:T(8,128)S(1)}, u32[]{:S(2)}, u32[]{:S(2)}) collective-permute-start(f32[128,256]{1,0:T(8,128)} %get-tuple-element.277), channel_id=1, source_target_pairs={{0,16},{1,17},{2,18},{3,19},{4,20},{5,21},{6,22},{7,23},{8,24},{9,... | collective-permute-start | bytes 393224 | tf_op jit(solution)/shard_map/ppermute | solution.py:706
  78.4 3.2 %copy-start.9 = (bf16[64,1024]{1,0:T(8,128)(2,1)S(1)}, bf16[64,1024]{1,0:T(8,128)(2,1)}, u32[]{:S(2)}) copy-start(bf16[64,1024]{1,0:T(8,128)(2,1)} %copy-done.8) | copy-start | bytes 393220
  82.7 10.6 %collective-permute-start.21 = (bf16[144,1024]{1,0:T(8,128)(2,1)S(1)}, bf16[144,1024]{1,0:T(8,128)(2,1)S(1)}, u32[]{:S(2)}, u32[]{:S(2)}) collective-permute-start(bf16[144,1024]{1,0:T(8,128)(2,1)S(1)} %branch_1_fun.16), channel_id=1, source_target_pairs={{0,12},{2,14},{4,0},{6,2},{8,4},{10,6},{12,8},{14,10},{1,13},{3,15... | collective-permute-start | bytes 884744 | tf_op jit(solution)/shard_map/cond/branch_1_fun/ppermute | solution.py:582
  85.8 12.8 %collective-permute-start.20 = (bf16[144,1024]{1,0:T(8,128)(2,1)S(1)}, bf16[144,1024]{1,0:T(8,128)(2,1)S(1)}, u32[]{:S(2)}, u32[]{:S(2)}) collective-permute-start(bf16[144,1024]{1,0:T(8,128)(2,1)S(1)} %branch_1_fun.16), channel_id=1, source_target_pairs={{0,4},{2,6},{4,8},{6,10},{8,12},{10,14},{12,0},{14,2},{1,5},{3,7},... | collective-permute-start | bytes 884744 | tf_op jit(solution)/shard_map/cond/branch_1_fun/ppermute | solution.py:582
  85.9 12.8 %collective-permute-start.19 = (bf16[144,1024]{1,0:T(8,128)(2,1)S(1)}, bf16[144,1024]{1,0:T(8,128)(2,1)S(1)}, u32[]{:S(2)}, u32[]{:S(2)}) collective-permute-start(bf16[144,1024]{1,0:T(8,128)(2,1)S(1)} %branch_1_fun.16), channel_id=1, source_target_pairs={{0,2},{2,0},{4,6},{6,4},{8,10},{10,8},{12,14},{14,12},{1,3},{3,1},... | collective-permute-start | bytes 884744 | tf_op jit(solution)/shard_map/cond/branch_1_fun/ppermute | solution.py:29
  98.6 14.8 %collective-permute-start.24 = (bf16[144,1024]{1,0:T(8,128)(2,1)S(1)}, bf16[144,1024]{1,0:T(8,128)(2,1)S(1)}, u32[]{:S(2)}, u32[]{:S(2)}) collective-permute-start(bf16[144,1024]{1,0:T(8,128)(2,1)S(1)} %branch_1_fun.16), channel_id=1, source_target_pairs={{0,8},{2,10},{4,12},{6,14},{8,0},{10,2},{12,4},{14,6},{1,9},{3,11}... | collective-permute-start | bytes 884744 | tf_op jit(solution)/shard_map/cond/branch_1_fun/ppermute | solution.py:582
  98.7 18.3 %collective-permute-start.22 = (bf16[144,1024]{1,0:T(8,128)(2,1)S(1)}, bf16[144,1024]{1,0:T(8,128)(2,1)S(1)}, u32[]{:S(2)}, u32[]{:S(2)}) collective-permute-start(bf16[144,1024]{1,0:T(8,128)(2,1)S(1)} %collective-permute-done.20), channel_id=1, source_target_pairs={{0,2},{2,0},{4,6},{6,4},{8,10},{10,8},{12,14},{14,12},{1,3},{3,1},... | collective-permute-start | bytes 884744 | tf_op jit(solution)/shard_map/cond/branch_1_fun/ppermute | solution.py:29
  100.3 16.7 %collective-permute-start.23 = (bf16[144,1024]{1,0:T(8,128)(2,1)S(1)}, bf16[144,1024]{1,0:T(8,128)(2,1)S(1)}, u32[]{:S(2)}, u32[]{:S(2)}) collective-permute-start(bf16[144,1024]{1,0:T(8,128)(2,1)S(1)} %collective-permute-done.21), channel_id=1, source_target_pairs={{0,2},{2,0},{4,6},{6,4},{8,10},{10,8},{12,14},{14,12},{1,3},{3,1},... | collective-permute-start | bytes 884744 | tf_op jit(solution)/shard_map/cond/branch_1_fun/ppermute | solution.py:29
  113.5 7.8 %collective-permute-start.25 = (bf16[144,1024]{1,0:T(8,128)(2,1)S(1)}, bf16[144,1024]{1,0:T(8,128)(2,1)S(1)}, u32[]{:S(2)}, u32[]{:S(2)}) collective-permute-start(bf16[144,1024]{1,0:T(8,128)(2,1)S(1)} %collective-permute-done.24), channel_id=1, source_target_pairs={{0,2},{2,0},{4,6},{6,4},{8,10},{10,8},{12,14},{14,12},{1,3},{3,1},... | collective-permute-start | bytes 884744 | tf_op jit(solution)/shard_map/cond/branch_1_fun/ppermute | solution.py:29
  122.1 4.9 %copy-start.3 = (bf16[576,1024]{1,0:T(8,128)(2,1)S(1)}, bf16[576,1024]{1,0:T(8,128)(2,1)}, u32[]{:S(2)}) copy-start(bf16[576,1024]{1,0:T(8,128)(2,1)} %get-tuple-element.213.refs_0_) | copy-start | bytes 3538948 | tf_op jit(solution)/shard_map/cond
  122.1 4.9 %copy-start.4 = (bf16[288,1024]{1,0:T(8,128)(2,1)S(1)}, bf16[288,1024]{1,0:T(8,128)(2,1)}, u32[]{:S(2)}) copy-start(bf16[288,1024]{1,0:T(8,128)(2,1)} %get-tuple-element.214.refs_1_) | copy-start | bytes 1769476 | tf_op jit(solution)/shard_map/cond
  122.1 4.9 %collective-permute-start.3 = (bf16[576,1024]{1,0:T(8,128)(2,1)}, bf16[576,1024]{1,0:T(8,128)(2,1)}, u32[]{:S(2)}, u32[]{:S(2)}) collective-permute-start(bf16[576,1024]{1,0:T(8,128)(2,1)} %get-tuple-element.213.refs_0_), channel_id=1, source_target_pairs={{0,1},{1,0},{2,3},{3,2},{4,5},{5,4},{6,7},{7,6},{8,9},{9,8},{10,11... | collective-permute-start | bytes 3538952 | tf_op jit(solution)/shard_map/cond/branch_1_fun/ppermute | solution.py:25
  122.1 4.0 %collective-permute-start.4 = (bf16[288,1024]{1,0:T(8,128)(2,1)}, bf16[288,1024]{1,0:T(8,128)(2,1)}, u32[]{:S(2)}, u32[]{:S(2)}) collective-permute-start(bf16[288,1024]{1,0:T(8,128)(2,1)} %get-tuple-element.214.refs_1_), channel_id=1, source_target_pairs={{0,1},{1,0},{2,3},{3,2},{4,5},{5,4},{6,7},{7,6},{8,9},{9,8},{10,11... | collective-permute-start | bytes 1769480 | tf_op jit(solution)/shard_map/cond/branch_1_fun/ppermute | solution.py:25
  122.6 4.4 %collective-permute-start.5 = (bf16[288,1024]{1,0:T(8,128)(2,1)}, bf16[288,1024]{1,0:T(8,128)(2,1)}, u32[]{:S(2)}, u32[]{:S(2)}) collective-permute-start(bf16[288,1024]{1,0:T(8,128)(2,1)} %get-tuple-element.215.refs_2_), channel_id=1, source_target_pairs={{0,1},{1,0},{2,3},{3,2},{4,5},{5,4},{6,7},{7,6},{8,9},{9,8},{10,11... | collective-permute-start | bytes 1769480 | tf_op jit(solution)/shard_map/cond/branch_1_fun/ppermute | solution.py:25
  131.3 22.2 %collective-permute-start.31 = (bf16[32,1024]{1,0:T(8,128)(2,1)S(1)}, bf16[32,1024]{1,0:T(8,128)(2,1)S(1)}, u32[]{:S(2)}, u32[]{:S(2)}) collective-permute-start(bf16[32,1024]{1,0:T(8,128)(2,1)S(1)} %get-tuple-element.285), channel_id=1, source_target_pairs={{16,0},{17,1},{18,2},{19,3},{20,4},{21,5},{22,6},{23,7},{24,8},{25... | collective-permute-start | bytes 196616 | tf_op jit(solution)/shard_map/ppermute | solution.py:762

commit v7 on v6

--- a/solution.py
+++ b/solution.py
@@ -390,22 +390,30 @@
 
     @pl.when(go_ref[0] == 1)
     def _():
-        moves = [(down_ref, down), (grads_ref, grads), (slopes_ref, slopes), (inputs_ref, inputs)]
-        moves = moves + [(first_ref.at[place], up), (gradient_ref, gradient)]
+        sides = [pl.ds(start, features // 2) for start in (0, features // 2)]
+        moves = [(ref.at[:, c], held.at[:, c]) for c in sides for ref, held in ((down_ref, down), (grads_ref, grads))]
+        moves = moves + [(slopes_ref, slopes)]
+        for c in sides:
+            moves = moves + [(inputs_ref.at[:, c], inputs.at[:, c]), (first_ref.at[place, c], up.at[:, c])]
+        moves = moves + [(gradient_ref, gradient)]
         copies = [pltpu.make_async_copy(a, b, sems.at[i]) for i, (a, b) in enumerate(moves)]
-        up_out = pltpu.make_async_copy(new_up, new_up_ref.at[place], out_sems.at[0])
-        down_out = pltpu.make_async_copy(new_down, new_down_ref.at[place], out_sems.at[1])
+        outs = [pltpu.make_async_copy(new_up.at[:, c], new_up_ref.at[place, c], out_sems.at[i]) for i, c in enumerate(sides)]
+        outs = outs + [pltpu.make_async_copy(new_down, new_down_ref.at[place], out_sems.at[2])]
         start_all(copies)
-        wait_all(copies[:3])
-        hidden_grad = dot(down[...], grads[...], nt_dims) * hidden ** (-0.5)
-        pre_grad = (hidden_grad * slopes[...]).astype(bf16)
-        wait_all(copies[3:5])
-        new_up[...] = new_tile(up[...], features ** (-0.5), pre_grad, inputs[...])
-        up_out.start()
-        copies[5].wait()
+        hidden_grad = jnp.zeros((tile, grads.shape[0]), f32)
+        for i, c in enumerate(sides):
+            wait_all(copies[2 * i : 2 * i + 2])
+            hidden_grad = hidden_grad + dot(down[:, c], grads[:, c], nt_dims)
+        copies[4].wait()
+        pre_grad = (hidden_grad * hidden ** (-0.5) * slopes[...]).astype(bf16)
+        for i, c in enumerate(sides):
+            wait_all(copies[2 * i + 5 : 2 * i + 7])
+            new_up[:, c] = new_tile(up[:, c], features ** (-0.5), pre_grad, inputs[:, c])
+            outs[i].start()
+        copies[9].wait()
         new_down[...] = (down[...].astype(f32) - (step_size * hidden ** (-0.5)) * gradient[...]).astype(bf16)
-        down_out.start()
-        wait_all([up_out, down_out])
+        outs[2].start()
+        wait_all(outs)
 
 
 def hold_kernel(go_ref, array_ref, held_ref, sem):
@@ -669,7 +677,7 @@
             out_specs=[anywhere] * 2,
             scratch_shapes=spaces(rows_like, rows_like, piece_like, piece_like, slopes_like, gradient_like)
             + spaces(piece_like, piece_like)
-            + [sems_of(6), sems_of(2)],
+            + [sems_of(10), sems_of(3)],
             input_output_aliases={7: 0, 8: 1},
             compiler_params=fits(60),
             cost_estimate=costs(1, 1),

time: 155 us -> 155 us (level)
  no operation moved by 1% of the time
where the time goes in v7:
time: 155 us; the launch traced here: 154 us
  waiting for transfers between devices  59.8 us (39%)
  Pallas kernels  36.3 us (23%)
  blocking collectives  25 us (16%)
  starting transfers between devices  24.3 us (16%)
  other arithmetic  4.96 us (3%)
  local copies, waits for them, and re-layouts  2.76 us (2%)
    all_to_all x2, blocking collectives, decode_step(): lax.all_to_all(payload, 'exp', split_axis=0, concat_axis=0, tiled=True)  25 us
    ppermute x3, waiting for transfers between devices, along(): return lax.ppermute(array, 'exp', pairs)  24 us
    all_to_all x2, waiting for transfers between devices, decode_step(): lax.all_to_all(summed, 'exp', split_axis=0, concat_axis=0, tiled=True)  15.2 us
    pallas_call x1, Pallas kernels, update_late(): pl.pallas_call(functools.partial(late_kernel, features, hidden, tile, 2 *...  12.9 us
    ppermute x5, starting transfers between devices, flipped(): lax.ppermute(array, axis, [(i, i ^ bit) for i in range(lax.axis_size(axis...  8.06 us
    ppermute x7, waiting for transfers between devices, shifted(): lax.ppermute(array, axis, [(i, (i + by) % size) for i in range(size)])  7.69 us
    ppermute x5, waiting for transfers between devices, flipped(): lax.ppermute(array, axis, [(i, i ^ bit) for i in range(lax.axis_size(axis...  6.87 us
    all_to_all x2, starting transfers between devices, decode_step(): lax.all_to_all(summed, 'exp', split_axis=0, concat_axis=0, tiled=True)  6.78 us
  transfers between devices with their start and end apart: 21, of which 15 were waited for; matrix products, arithmetic and copies ran while one was open for 5% of the time, Pallas kernels for 22%

profile of v7, /device:TPU:0, one launch (start us, length us, event | category | flops | bytes accessed | tf_op | source)
XLA Modules:
  0.0 154.0 jit_solution(14072429991473267725)
XLA Ops:
  0.6 2.2 %shard_map.139 = (s32[4,2,128]{2,1,0:T(2,128)S(1)}, f32[8,128]{1,0:T(8,128)S(1)}, f32[128,256]{1,0:T(8,128)}, bf16[384,256]{1,0:T(8,128)(2,1)}, bf16[64,1024]{1,0:T(8,128)(2,1)S(1)}) custom-call(s32[1]{0:T(128)} %bitcast.24.part_ref, s32[8,32]{1,0:T(8,128)} %bitcast.68, f32[8,32]{1,0:T(8,128)} %bitcast.69, bf16[32,2048]{1,0:T(8,128)(2,1)} %all_rows_ref.1, ...), custom_call_target="tpu_custom_call" | custom-call | flops 1 | bytes 1 | tf_op jit(solution)/shard_map/pallas_call | solution.py:494
  2.9 3.0 %collective-permute-start.29 = (bf16[64,1024]{1,0:T(8,128)(2,1)S(1)}, bf16[64,1024]{1,0:T(8,128)(2,1)}, u32[]{:S(2)}, u32[]{:S(2)}) collective-permute-start(bf16[64,1024]{1,0:T(8,128)(2,1)S(1)} %get-tuple-element.263), channel_id=1, source_target_pairs={{0,16},{16,0},{1,17},{17,1},{2,18},{18,2},{3,19},{19,3},{4,20},{20... | collective-permute-start | bytes 393224 | tf_op jit(solution)/shard_map/ppermute | solution.py:29
  5.9 0.0 copy-start.14
  5.9 0.0 copy-start.15
  5.9 0.1 shard_map.140
  6.0 3.5 %collective-permute-done.29 = bf16[64,1024]{1,0:T(8,128)(2,1)} collective-permute-done((bf16[64,1024]{1,0:T(8,128)(2,1)S(1)}, bf16[64,1024]{1,0:T(8,128)(2,1)}, u32[]{:S(2)}, u32[]{:S(2)}) %collective-permute-start.29) | collective-permute-done | bytes 131104 | tf_op jit(solution)/shard_map/ppermute | solution.py:29
  9.5 1.3 collective-permute-start.32
  10.8 1.3 collective-permute-start.33
  12.2 34.0 %conditional.4 = (f32[128,256]{1,0:T(8,128)}, bf16[384,256]{1,0:T(8,128)(2,1)}, bf16[576,1024]{1,0:T(8,128)(2,1)}, bf16[288,1024]{1,0:T(8,128)(2,1)}, bf16[288,1024]{1,0:T(8,128)(2,1)}) conditional(s32[]{:T(128)} %convert_element_type.43, (s32[128,2]{0,1:T(2,128)S(1)}, f32[128,2]{0,1:T(2,128)S(1)}, s32[1,2,4]{2,1,0:T(2,128)S(1)}, ...), branch_computations={%region_0.0_spmd, %region_1.0_spmd} | conditional | flops 7077889 | bytes 12976449 | solution.py:701
  12.2 13.9 %all_to_all.64 = bf16[8,48,256]{2,1,0:T(8,128)(2,1)S(1)} all-to-all(bf16[8,48,256]{2,1,0:T(8,128)(2,1)} %bitcast.3), channel_id=1, replica_groups=mesh['sect'=2,'exp'=8,'dp'=2] {'exp'}, dimensions={0} | all-to-all | bytes 393216 | tf_op jit(solution)/shard_map/cond/branch_1_fun/all_to_all | solution.py:552
  26.1 0.0 collective-permute-start.13
  26.1 1.4 collective-permute-done.13.refs_1_
  27.5 3.3 %branch_1_fun.10 = (bf16[384,256]{1,0:T(8,128)(2,1)S(1)}, bf16[384,256]{1,0:T(8,128)(2,1)S(1)}) custom-call(s32[1]{0:T(128)} %get-tuple-element.135.part_ref, f32[1,2048]{1,0:T(1,128)S(1)} %get-tuple-element.136.gain_ref, bf16[384,256]{1,0:T(8,128)(2,1)S(1)} %bitcast.47, bf16[384,256]{1,0:T(8,128)(2,1)S(1)} %collective-permute-done.13.refs_1_, ...), custom_call_target="tpu_custom_call" | custom-call | flops 1 | bytes 1 | tf_op jit(solution)/shard_map/cond/branch_1_fun/pallas_call | solution.py:534
  30.8 0.2 collective-permute-start.14
  31.0 1.3 collective-permute-done.14
  32.3 0.7 add_convert_fusion
  33.1 3.4 %all-to-all-start.1 = ((bf16[8,48,256]{2,1,0:T(8,128)(2,1)}), bf16[8,48,256]{2,1,0:T(8,128)(2,1)S(1)}, u32[]{:S(2)}, u32[]{:S(2)}) async-start(bf16[8,48,256]{2,1,0:T(8,128)(2,1)} %bitcast.5), calls=%async_computation.1 | async-start | bytes 393216 | tf_op jit(solution)/shard_map/cond/branch_1_fun/all_to_all | solution.py:557
  36.5 0.9 copy.61.states_ref
  37.4 7.6 %all-to-all-done.1 = bf16[8,48,256]{2,1,0:T(8,128)(2,1)S(1)} async-done(((bf16[8,48,256]{2,1,0:T(8,128)(2,1)}), bf16[8,48,256]{2,1,0:T(8,128)(2,1)S(1)}, u32[]{:S(2)}, u32[]{:S(2)}) %all-to-all-start.1) | async-done | bytes 196640 | tf_op jit(solution)/shard_map/cond/branch_1_fun/all_to_all | solution.py:557
  44.9 1.2 branch_1_fun.11
  46.2 30.9 %conditional.5 = (f32[128,256]{1,0:T(8,128)}, bf16[768,2048]{1,0:T(8,128)(2,1)}, bf16[768,2048]{1,0:T(8,128)(2,1)}) conditional(s32[]{:T(128)} %convert_element_type.43, (s32[]{:T(128)}, bf16[576,1024]{1,0:T(8,128)(2,1)}, bf16[288,1024]{1,0:T(8,128)(2,1)}, bf16[288,1024]{1,0:T(8,128)(2,1)}, s32[1]{0:T(128)}, ...), branch_computations={%region_2.0_spmd, %region_3.0_spmd} | conditional | flops 393219 | bytes 18882816 | solution.py:713
  46.2 11.1 %all_to_all.65 = bf16[8,48,256]{2,1,0:T(8,128)(2,1)S(1)} all-to-all(bf16[8,48,256]{2,1,0:T(8,128)(2,1)} %bitcast.8), channel_id=1, replica_groups=mesh['sect'=2,'exp'=8,'dp'=2] {'exp'}, dimensions={0} | all-to-all | bytes 393216 | tf_op jit(solution)/shard_map/cond/branch_1_fun/all_to_all | solution.py:552
  57.3 0.0 collective-permute-start.15
  57.3 1.4 collective-permute-done.15.refs_1_
  58.7 3.3 %branch_1_fun.13 = (bf16[384,256]{1,0:T(8,128)(2,1)S(1)}, bf16[384,256]{1,0:T(8,128)(2,1)S(1)}) custom-call(s32[1]{0:T(128)} %get-tuple-element.160.part_ref, f32[1,2048]{1,0:T(1,128)S(1)} %get-tuple-element.161.gain_ref, bf16[384,256]{1,0:T(8,128)(2,1)S(1)} %bitcast.49, bf16[384,256]{1,0:T(8,128)(2,1)S(1)} %collective-permute-done.15.refs_1_, ...), custom_call_target="tpu_custom_call" | custom-call | flops 1 | bytes 1 | tf_op jit(solution)/shard_map/cond/branch_1_fun/pallas_call | solution.py:534
  62.0 0.2 collective-permute-start.16
  62.3 1.3 collective-permute-done.16
  63.5 0.7 add_convert_fusion.1
  64.3 3.4 %all-to-all-start.3 = ((bf16[8,48,256]{2,1,0:T(8,128)(2,1)}), bf16[8,48,256]{2,1,0:T(8,128)(2,1)S(1)}, u32[]{:S(2)}, u32[]{:S(2)}) async-start(bf16[8,48,256]{2,1,0:T(8,128)(2,1)} %bitcast.10), calls=%async_computation.3 | async-start | bytes 393216 | tf_op jit(solution)/shard_map/cond/branch_1_fun/all_to_all | solution.py:557
  67.7 0.9 copy.62.states_ref
  68.6 7.6 %all-to-all-done.3 = bf16[8,48,256]{2,1,0:T(8,128)(2,1)S(1)} async-done(((bf16[8,48,256]{2,1,0:T(8,128)(2,1)}), bf16[8,48,256]{2,1,0:T(8,128)(2,1)S(1)}, u32[]{:S(2)}, u32[]{:S(2)}) %all-to-all-start.3) | async-done | bytes 196640 | tf_op jit(solution)/shard_map/cond/branch_1_fun/all_to_all | solution.py:557
  76.2 1.0 branch_1_fun.14
  77.1 1.3 collective-permute-start.30
  78.4 3.2 %collective-permute-done.30 = f32[128,256]{1,0:T(8,128)S(1)} collective-permute-done((f32[128,256]{1,0:T(8,128)}, f32[128,256]{1,0:T(8,128)S(1)}, u32[]{:S(2)}, u32[]{:S(2)}) %collective-permute-start.30) | collective-permute-done | bytes 131104 | tf_op jit(solution)/shard_map/ppermute | solution.py:714
  81.6 40.5 %conditional.6 = (f32[128,256]{1,0:T(8,128)S(1)}, bf16[384,256]{1,0:T(8,128)(2,1)}, bf16[576,1024]{1,0:T(8,128)(2,1)}, bf16[288,1024]{1,0:T(8,128)(2,1)}, bf16[288,1024]{1,0:T(8,128)(2,1)}) conditional(s32[]{:T(128)} %convert_element_type.43, (s32[4,2,128]{2,1,0:T(2,128)S(1)}, f32[128,256]{1,0:T(8,128)S(1)}, s32[1]{0:T(128)}, ...), branch_computations={%region_4.0_spmd, %region_5.0_spmd} | conditional | flops 7077889 | bytes 13238593 | solution.py:739
  81.6 1.1 branch_1_fun.16
  82.7 3.2 %collective-permute-start.21 = (bf16[144,1024]{1,0:T(8,128)(2,1)S(1)}, bf16[144,1024]{1,0:T(8,128)(2,1)S(1)}, u32[]{:S(2)}, u32[]{:S(2)}) collective-permute-start(bf16[144,1024]{1,0:T(8,128)(2,1)S(1)} %branch_1_fun.16), channel_id=1, source_target_pairs={{0,12},{2,14},{4,0},{6,2},{8,4},{10,6},{12,8},{14,10},{1,13},{3,15... | collective-permute-start | bytes 884744 | tf_op jit(solution)/shard_map/cond/branch_1_fun/ppermute | solution.py:590
  85.9 1.5 collective-permute-start.19
  87.4 5.9 %collective-permute-done.21 = bf16[144,1024]{1,0:T(8,128)(2,1)S(1)} collective-permute-done((bf16[144,1024]{1,0:T(8,128)(2,1)S(1)}, bf16[144,1024]{1,0:T(8,128)(2,1)S(1)}, u32[]{:S(2)}, u32[]{:S(2)}) %collective-permute-start.21) | collective-permute-done | bytes 294944 | tf_op jit(solution)/shard_map/cond/branch_1_fun/ppermute | solution.py:590
  93.3 5.3 %collective-permute-done.20 = bf16[144,1024]{1,0:T(8,128)(2,1)S(1)} collective-permute-done((bf16[144,1024]{1,0:T(8,128)(2,1)S(1)}, bf16[144,1024]{1,0:T(8,128)(2,1)S(1)}, u32[]{:S(2)}, u32[]{:S(2)}) %collective-permute-start.20) | collective-permute-done | bytes 294944 | tf_op jit(solution)/shard_map/cond/branch_1_fun/ppermute | solution.py:590
  98.6 0.1 collective-permute-start.24
  98.7 1.5 %collective-permute-start.22 = (bf16[144,1024]{1,0:T(8,128)(2,1)S(1)}, bf16[144,1024]{1,0:T(8,128)(2,1)S(1)}, u32[]{:S(2)}, u32[]{:S(2)}) collective-permute-start(bf16[144,1024]{1,0:T(8,128)(2,1)S(1)} %collective-permute-done.20), channel_id=1, source_target_pairs={{0,2},{2,0},{4,6},{6,4},{8,10},{10,8},{12,14},{14,12},{1,3},{3,1},... | collective-permute-start | bytes 884744 | tf_op jit(solution)/shard_map/cond/branch_1_fun/ppermute | solution.py:29
  100.3 0.5 collective-permute-start.23
  100.8 12.7 %collective-permute-done.24 = bf16[144,1024]{1,0:T(8,128)(2,1)S(1)} collective-permute-done((bf16[144,1024]{1,0:T(8,128)(2,1)S(1)}, bf16[144,1024]{1,0:T(8,128)(2,1)S(1)}, u32[]{:S(2)}, u32[]{:S(2)}) %collective-permute-start.24) | collective-permute-done | bytes 294944 | tf_op jit(solution)/shard_map/cond/branch_1_fun/ppermute | solution.py:590
  113.5 1.5 collective-permute-start.25
  115.0 0.9 copy.40
  115.9 1.1 pad_maximum_fusion.3
  117.0 0.9 pad_maximum_fusion.4
  117.9 3.4 %collective-permute-done.25 = bf16[144,1024]{1,0:T(8,128)(2,1)S(1)} collective-permute-done((bf16[144,1024]{1,0:T(8,128)(2,1)S(1)}, bf16[144,1024]{1,0:T(8,128)(2,1)S(1)}, u32[]{:S(2)}, u32[]{:S(2)}) %collective-permute-start.25) | collective-permute-done | bytes 294944 | tf_op jit(solution)/shard_map/cond/branch_1_fun/ppermute | solution.py:29
  121.2 0.9 pad_maximum_fusion.5
  122.1 9.1 %conditional.7 = (bf16[32,1024]{1,0:T(8,128)(2,1)S(1)}, bf16[32,1024]{1,0:T(8,128)(2,1)S(1)}, bf16[512,2048]{1,0:T(8,128)(2,1)}, bf16[512,2048]{1,0:T(8,128)(2,1)}, f32[1,512]{1,0:T(1,128)}) conditional(s32[]{:T(128)} %convert_element_type.43, (bf16[384,256]{1,0:T(8,128)(2,1)}, s32[1]{0:T(128)}, f32[1,2048]{1,0:T(1,128)S(1)}, ...), branch_computations={%region_6.0_spmd, %region_7.0_spmd} | conditional | flops 393220 | bytes 16515291 | solution.py:767
  122.1 0.5 collective-permute-start.4
  122.6 0.1 collective-permute-start.5
  122.7 2.0 %branch_1_fun.17.refs_0_ = f32[1,512]{1,0:T(1,128)} custom-call(s32[1]{0:T(128)} %bitcast.23.me_ref, bf16[576,1024]{1,0:T(8,128)(2,1)} %get-tuple-element.213.refs_0_, bf16[288,1024]{1,0:T(8,128)(2,1)} %get-tuple-element.214.refs_1_, bf16[288,1024]{1,0:T(8,128)(2,1)} %get-tuple-element.215.refs_2_), custom_call_target="tpu_custom_call" | custom-call | flops 1 | bytes 1 | tf_op jit(solution)/shard_map/cond/branch_1_fun/pallas_call | solution.py:610
  124.8 1.4 collective-permute-done.4.refs_4_
  126.2 0.8 collective-permute-done.5.refs_5_
  127.0 0.0 collective-permute-done.3.refs_3_
  127.0 4.2 %branch_1_fun.19 = (bf16[512,2048]{1,0:T(8,128)(2,1)}, bf16[512,2048]{1,0:T(8,128)(2,1)}) custom-call(s32[1]{0:T(128)} %get-tuple-element.218.part_ref, bf16[576,1024]{1,0:T(8,128)(2,1)S(1)} %copy-done.3, bf16[288,1024]{1,0:T(8,128)(2,1)S(1)} %copy-done.4, bf16[288,1024]{1,0:T(8,128)(2,1)} %get-tuple-element.215.refs_2_, ...), custom_call_target="tpu_custom_call" | custom-call | flops 1 | bytes 1 | tf_op jit(solution)/shard_map/cond/branch_1_fun/pallas_call | solution.py:743
  131.3 1.3 collective-permute-start.31
  132.6 0.0 collective-permute-done.32.refs_2_
  132.6 12.9 %shard_map.142 = (bf16[768,2048]{1,0:T(8,128)(2,1)}, bf16[768,2048]{1,0:T(8,128)(2,1)}, f32[256,512]{1,0:T(8,128)}, f32[256,2048]{1,0:T(8,128)}) custom-call(s32[1]{0:T(128)} %bitcast.31.go_ref, f32[1,512]{1,0:T(1,128)} %get-tuple-element.291.weight_ref, bf16[512,2048]{1,0:T(8,128)(2,1)} %get-tuple-element.287.refs_0_, ...), custom_call_target="tpu_custom_call", output_to_operand_aliasing={{0}: (5, {}), {1}: (6, {})} | custom-call | flops 1 | bytes 1 | tf_op jit(solution)/shard_map/pallas_call | solution.py:657
  145.5 2.9 %collective-permute-done.33.refs_3_ = bf16[256,2048]{1,0:T(8,128)(2,1)} collective-permute-done((bf16[256,2048]{1,0:T(8,128)(2,1)}, bf16[256,2048]{1,0:T(8,128)(2,1)}, u32[]{:S(2)}, u32[]{:S(2)}) %collective-permute-start.33) | collective-permute-done | bytes 1048608 | tf_op jit(solution)/shard_map/ppermute | solution.py:530
  148.4 5.0 %shard_map.143 = (bf16[768,2048]{1,0:T(8,128)(2,1)}, bf16[768,2048]{1,0:T(8,128)(2,1)}) custom-call(s32[1]{0:T(128)} %bitcast.31.go_ref, bf16[512,2048]{1,0:T(8,128)(2,1)} %get-tuple-element.287.refs_0_, bf16[512,2048]{1,0:T(8,128)(2,1)} %get-tuple-element.288.refs_1_, ...), custom_call_target="tpu_custom_call", output_to_operand_aliasing={{0}: (7, {}), {1}: (8, {})} | custom-call | flops 1 | bytes 1 | tf_op jit(solution)/shard_map/pallas_call | solution.py:673
  153.4 0.6 broadcast_select_fusion
  (28 shorter events, 0.1 us)
Async XLA Ops:
  2.9 9.3 %copy-start.8 = (bf16[64,1024]{1,0:T(8,128)(2,1)}, bf16[64,1024]{1,0:T(8,128)(2,1)S(1)}, u32[]{:S(2)}) copy-start(bf16[64,1024]{1,0:T(8,128)(2,1)S(1)} %get-tuple-element.263) | copy-start | bytes 393220
  2.9 6.6 %collective-permute-start.29 = (bf16[64,1024]{1,0:T(8,128)(2,1)S(1)}, bf16[64,1024]{1,0:T(8,128)(2,1)}, u32[]{:S(2)}, u32[]{:S(2)}) collective-permute-start(bf16[64,1024]{1,0:T(8,128)(2,1)S(1)} %get-tuple-element.263), channel_id=1, source_target_pairs={{0,16},{16,0},{1,17},{17,1},{2,18},{18,2},{3,19},{19,3},{4,20},{20... | collective-permute-start | bytes 393224 | tf_op jit(solution)/shard_map/ppermute | solution.py:29
  5.9 6.2 %copy-start.2 = (bf16[1,1,768,2048]{3,2,1,0:T(8,128)(2,1)S(1)}, bf16[1,1,768,2048]{3,2,1,0:T(8,128)(2,1)}, u32[]{:S(2)}) copy-start(bf16[1,1,768,2048]{3,2,1,0:T(8,128)(2,1)} %param.24) | copy-start | bytes 9437188
  5.9 6.2 %copy-start.10 = (f32[2048]{0:T(1024)S(1)}, f32[2048]{0:T(1024)}, u32[]{:S(2)}) copy-start(f32[2048]{0:T(1024)} %param.21) | copy-start | bytes 24580
  5.9 6.2 %copy-start.12 = (s32[128,2]{0,1:T(2,128)S(1)}, s32[128,2]{0,1:T(2,128)}, u32[]{:S(2)}) copy-start(s32[128,2]{0,1:T(2,128)} %param.30) | copy-start | bytes 3076
  5.9 6.2 %copy-start.13 = (f32[128,2]{0,1:T(2,128)S(1)}, f32[128,2]{0,1:T(2,128)}, u32[]{:S(2)}) copy-start(f32[128,2]{0,1:T(2,128)} %param.31) | copy-start | bytes 3076
  5.9 6.2 %copy-start.14 = (s32[1,2,4]{2,1,0:T(2,128)S(1)}, s32[1,2,4]{2,1,0:T(2,128)}, u32[]{:S(2)}) copy-start(s32[1,2,4]{2,1,0:T(2,128)} %param.28) | copy-start | bytes 100
  5.9 6.2 %copy-start.15 = (s32[1,8]{1,0:T(1,128)S(1)}, s32[1,8]{1,0:T(1,128)}, u32[]{:S(2)}) copy-start(s32[1,8]{1,0:T(1,128)} %param.29) | copy-start | bytes 100
  9.5 123.1 %collective-permute-start.32 = (bf16[1280,2048]{1,0:T(8,128)(2,1)}, bf16[1280,2048]{1,0:T(8,128)(2,1)}, u32[]{:S(2)}, u32[]{:S(2)}) collective-permute-start(bf16[1280,2048]{1,0:T(8,128)(2,1)} %get-tuple-element.289), channel_id=1, source_target_pairs={{16,0},{17,1},{18,2},{19,3},{20,4},{21,5},{22,6},{23,7},{24,8},{25... | collective-permute-start | bytes 15728648 | tf_op jit(solution)/shard_map/ppermute | solution.py:529
  10.8 137.6 %collective-permute-start.33 = (bf16[256,2048]{1,0:T(8,128)(2,1)}, bf16[256,2048]{1,0:T(8,128)(2,1)}, u32[]{:S(2)}, u32[]{:S(2)}) collective-permute-start(bf16[256,2048]{1,0:T(8,128)(2,1)} %get-tuple-element.290), channel_id=1, source_target_pairs={{16,0},{17,1},{18,2},{19,3},{20,4},{21,5},{22,6},{23,7},{24,8},{25... | collective-permute-start | bytes 3145736 | tf_op jit(solution)/shard_map/ppermute | solution.py:530
  26.1 1.4 collective-permute-start.13
  30.8 1.5 collective-permute-start.14
  33.1 11.9 %all-to-all-start.1 = ((bf16[8,48,256]{2,1,0:T(8,128)(2,1)}), bf16[8,48,256]{2,1,0:T(8,128)(2,1)S(1)}, u32[]{:S(2)}, u32[]{:S(2)}) async-start(bf16[8,48,256]{2,1,0:T(8,128)(2,1)} %bitcast.5), calls=%async_computation.1 | async-start | bytes 393216 | tf_op jit(solution)/shard_map/cond/branch_1_fun/all_to_all | solution.py:557
  57.3 1.4 collective-permute-start.15
  62.0 1.5 collective-permute-start.16
  64.3 11.9 %all-to-all-start.3 = ((bf16[8,48,256]{2,1,0:T(8,128)(2,1)}), bf16[8,48,256]{2,1,0:T(8,128)(2,1)S(1)}, u32[]{:S(2)}, u32[]{:S(2)}) async-start(bf16[8,48,256]{2,1,0:T(8,128)(2,1)} %bitcast.10), calls=%async_computation.3 | async-start | bytes 393216 | tf_op jit(solution)/shard_map/cond/branch_1_fun/all_to_all | solution.py:557
  77.1 4.5 %collective-permute-start.30 = (f32[128,256]{1,0:T(8,128)}, f32[128,256]{1,0:T(8,128)S(1)}, u32[]{:S(2)}, u32[]{:S(2)}) collective-permute-start(f32[128,256]{1,0:T(8,128)} %get-tuple-element.277), channel_id=1, source_target_pairs={{0,16},{1,17},{2,18},{3,19},{4,20},{5,21},{6,22},{7,23},{8,24},{9,... | collective-permute-start | bytes 393224 | tf_op jit(solution)/shard_map/ppermute | solution.py:714
  78.4 3.2 %copy-start.9 = (bf16[64,1024]{1,0:T(8,128)(2,1)S(1)}, bf16[64,1024]{1,0:T(8,128)(2,1)}, u32[]{:S(2)}) copy-start(bf16[64,1024]{1,0:T(8,128)(2,1)} %copy-done.8) | copy-start | bytes 393220
  82.7 10.6 %collective-permute-start.21 = (bf16[144,1024]{1,0:T(8,128)(2,1)S(1)}, bf16[144,1024]{1,0:T(8,128)(2,1)S(1)}, u32[]{:S(2)}, u32[]{:S(2)}) collective-permute-start(bf16[144,1024]{1,0:T(8,128)(2,1)S(1)} %branch_1_fun.16), channel_id=1, source_target_pairs={{0,12},{2,14},{4,0},{6,2},{8,4},{10,6},{12,8},{14,10},{1,13},{3,15... | collective-permute-start | bytes 884744 | tf_op jit(solution)/shard_map/cond/branch_1_fun/ppermute | solution.py:590
  85.8 12.8 %collective-permute-start.20 = (bf16[144,1024]{1,0:T(8,128)(2,1)S(1)}, bf16[144,1024]{1,0:T(8,128)(2,1)S(1)}, u32[]{:S(2)}, u32[]{:S(2)}) collective-permute-start(bf16[144,1024]{1,0:T(8,128)(2,1)S(1)} %branch_1_fun.16), channel_id=1, source_target_pairs={{0,4},{2,6},{4,8},{6,10},{8,12},{10,14},{12,0},{14,2},{1,5},{3,7},... | collective-permute-start | bytes 884744 | tf_op jit(solution)/shard_map/cond/branch_1_fun/ppermute | solution.py:590
  85.9 12.8 %collective-permute-start.19 = (bf16[144,1024]{1,0:T(8,128)(2,1)S(1)}, bf16[144,1024]{1,0:T(8,128)(2,1)S(1)}, u32[]{:S(2)}, u32[]{:S(2)}) collective-permute-start(bf16[144,1024]{1,0:T(8,128)(2,1)S(1)} %branch_1_fun.16), channel_id=1, source_target_pairs={{0,2},{2,0},{4,6},{6,4},{8,10},{10,8},{12,14},{14,12},{1,3},{3,1},... | collective-permute-start | bytes 884744 | tf_op jit(solution)/shard_map/cond/branch_1_fun/ppermute | solution.py:29
  98.6 14.8 %collective-permute-start.24 = (bf16[144,1024]{1,0:T(8,128)(2,1)S(1)}, bf16[144,1024]{1,0:T(8,128)(2,1)S(1)}, u32[]{:S(2)}, u32[]{:S(2)}) collective-permute-start(bf16[144,1024]{1,0:T(8,128)(2,1)S(1)} %branch_1_fun.16), channel_id=1, source_target_pairs={{0,8},{2,10},{4,12},{6,14},{8,0},{10,2},{12,4},{14,6},{1,9},{3,11}... | collective-permute-start | bytes 884744 | tf_op jit(solution)/shard_map/cond/branch_1_fun/ppermute | solution.py:590
  98.7 18.3 %collective-permute-start.22 = (bf16[144,1024]{1,0:T(8,128)(2,1)S(1)}, bf16[144,1024]{1,0:T(8,128)(2,1)S(1)}, u32[]{:S(2)}, u32[]{:S(2)}) collective-permute-start(bf16[144,1024]{1,0:T(8,128)(2,1)S(1)} %collective-permute-done.20), channel_id=1, source_target_pairs={{0,2},{2,0},{4,6},{6,4},{8,10},{10,8},{12,14},{14,12},{1,3},{3,1},... | collective-permute-start | bytes 884744 | tf_op jit(solution)/shard_map/cond/branch_1_fun/ppermute | solution.py:29
  100.3 16.7 %collective-permute-start.23 = (bf16[144,1024]{1,0:T(8,128)(2,1)S(1)}, bf16[144,1024]{1,0:T(8,128)(2,1)S(1)}, u32[]{:S(2)}, u32[]{:S(2)}) collective-permute-start(bf16[144,1024]{1,0:T(8,128)(2,1)S(1)} %collective-permute-done.21), channel_id=1, source_target_pairs={{0,2},{2,0},{4,6},{6,4},{8,10},{10,8},{12,14},{14,12},{1,3},{3,1},... | collective-permute-start | bytes 884744 | tf_op jit(solution)/shard_map/cond/branch_1_fun/ppermute | solution.py:29
  113.5 7.8 %collective-permute-start.25 = (bf16[144,1024]{1,0:T(8,128)(2,1)S(1)}, bf16[144,1024]{1,0:T(8,128)(2,1)S(1)}, u32[]{:S(2)}, u32[]{:S(2)}) collective-permute-start(bf16[144,1024]{1,0:T(8,128)(2,1)S(1)} %collective-permute-done.24), channel_id=1, source_target_pairs={{0,2},{2,0},{4,6},{6,4},{8,10},{10,8},{12,14},{14,12},{1,3},{3,1},... | collective-permute-start | bytes 884744 | tf_op jit(solution)/shard_map/cond/branch_1_fun/ppermute | solution.py:29
  122.1 4.9 %copy-start.3 = (bf16[576,1024]{1,0:T(8,128)(2,1)S(1)}, bf16[576,1024]{1,0:T(8,128)(2,1)}, u32[]{:S(2)}) copy-start(bf16[576,1024]{1,0:T(8,128)(2,1)} %get-tuple-element.213.refs_0_) | copy-start | bytes 3538948 | tf_op jit(solution)/shard_map/cond
  122.1 4.9 %copy-start.4 = (bf16[288,1024]{1,0:T(8,128)(2,1)S(1)}, bf16[288,1024]{1,0:T(8,128)(2,1)}, u32[]{:S(2)}) copy-start(bf16[288,1024]{1,0:T(8,128)(2,1)} %get-tuple-element.214.refs_1_) | copy-start | bytes 1769476 | tf_op jit(solution)/shard_map/cond
  122.1 4.9 %collective-permute-start.3 = (bf16[576,1024]{1,0:T(8,128)(2,1)}, bf16[576,1024]{1,0:T(8,128)(2,1)}, u32[]{:S(2)}, u32[]{:S(2)}) collective-permute-start(bf16[576,1024]{1,0:T(8,128)(2,1)} %get-tuple-element.213.refs_0_), channel_id=1, source_target_pairs={{0,1},{1,0},{2,3},{3,2},{4,5},{5,4},{6,7},{7,6},{8,9},{9,8},{10,11... | collective-permute-start | bytes 3538952 | tf_op jit(solution)/shard_map/cond/branch_1_fun/ppermute | solution.py:25
  122.1 4.0 %collective-permute-start.4 = (bf16[288,1024]{1,0:T(8,128)(2,1)}, bf16[288,1024]{1,0:T(8,128)(2,1)}, u32[]{:S(2)}, u32[]{:S(2)}) collective-permute-start(bf16[288,1024]{1,0:T(8,128)(2,1)} %get-tuple-element.214.refs_1_), channel_id=1, source_target_pairs={{0,1},{1,0},{2,3},{3,2},{4,5},{5,4},{6,7},{7,6},{8,9},{9,8},{10,11... | collective-permute-start | bytes 1769480 | tf_op jit(solution)/shard_map/cond/branch_1_fun/ppermute | solution.py:25
  122.6 4.4 %collective-permute-start.5 = (bf16[288,1024]{1,0:T(8,128)(2,1)}, bf16[288,1024]{1,0:T(8,128)(2,1)}, u32[]{:S(2)}, u32[]{:S(2)}) collective-permute-start(bf16[288,1024]{1,0:T(8,128)(2,1)} %get-tuple-element.215.refs_2_), channel_id=1, source_target_pairs={{0,1},{1,0},{2,3},{3,2},{4,5},{5,4},{6,7},{7,6},{8,9},{9,8},{10,11... | collective-permute-start | bytes 1769480 | tf_op jit(solution)/shard_map/cond/branch_1_fun/ppermute | solution.py:25
  131.3 22.1 %collective-permute-start.31 = (bf16[32,1024]{1,0:T(8,128)(2,1)S(1)}, bf16[32,1024]{1,0:T(8,128)(2,1)S(1)}, u32[]{:S(2)}, u32[]{:S(2)}) collective-permute-start(bf16[32,1024]{1,0:T(8,128)(2,1)S(1)} %get-tuple-element.285), channel_id=1, source_target_pairs={{16,0},{17,1},{18,2},{19,3},{20,4},{21,5},{22,6},{23,7},{24,8},{25... | collective-permute-start | bytes 196616 | tf_op jit(solution)/shard_map/ppermute | solution.py:770
